TPU v7x, 256 devices: a whole 4x4x8 slice. The times are simulated.
256 devices in a mesh: band: 64 (over x, z_lo, y, core), img: 4 (over z_hi).
Axes of the slice: x: 4, y: 4, z: 8 (z_hi: 4, z_lo: 2; z = z_hi * 2 + z_lo), core: 2. Of those that a mesh axis runs over, the one named last changes fastest.
Arguments:
- latent: bfloat16 [512, 128, 640], P(('img', 'band')), parts along dimension 0, may hold values from -27 to 27
- gn_gain: float32 [640], replicated, may hold values from 0.25 to 1.75
- gn_bias: float32 [640], replicated, may hold values from -3 to 3
- conv_weight: bfloat16 [3, 3, 640, 640], replicated, may hold values from -0.15625 to 0.15625
- conv_bias: float32 [640], replicated, may hold values from -3 to 3
- ln_gain: float32 [640], replicated, may hold values from 0.5 to 3.5
- ln_bias: float32 [640], replicated, may hold values from -2 to 2
- w_query: bfloat16 [640, 640], replicated, may hold values from -4 to 4
- w_key: bfloat16 [640, 640], replicated, may hold values from -4 to 4
- w_value: bfloat16 [640, 640], replicated, may hold values from -4 to 4
Outputs:
- result: bfloat16 [512, 128, 640], P(('img', 'band')), parts along dimension 0
There are 4 independent parts, one for each index of `img`. A program takes and returns all parts, laid end to end along the dimension named above; an argument that names none is the same for every part. Nothing has to cross between parts.
All inputs are finite; a program needn't handle non-finite values.
Results may differ from a plain program's by a relative error of at most 0.015.
Values may be sent and summed in bfloat16 or wider, within the bound.
No kernel may reach another device: no remote copies, remote signals or barrier semaphores. Data moves between devices by JAX's collectives and lax.ppermute only.
A program may use at most 128 MiB of HBM per device.

v0:
```python
import math

import jax
import jax.numpy as jnp
from jax import lax
from jax.sharding import PartitionSpec as P

HEADS = 10
GROUPS = 16


def with_halo(array, sides, width):
    for axis, dim in sides:
        count, length = (lax.axis_size(axis), array.shape[dim])
        up = [(i, (i + 1) % count) for i in range(count - 1)]
        down = [(j, i) for i, j in up]
        last = lax.slice_in_dim(array, length - width, length, axis=dim)
        first = lax.slice_in_dim(array, 0, width, axis=dim)
        before = lax.ppermute(last, axis, up)
        after = lax.ppermute(first, axis, down)
        array = jnp.concatenate([before, array, after], axis=dim)
    return array


def fold_block(carry, q_heads, k_block, v_block, scale):
    run_max, run_sum, run_acc = carry
    count = k_block.shape[0]
    heads = q_heads.shape[1]
    k_heads = k_block.reshape(count, heads, -1)
    v_heads = v_block.reshape(count, heads, -1)
    score = jnp.einsum("qhd,khd->hqk", q_heads, k_heads, preferred_element_type=jnp.float32) * scale
    new_max = jnp.maximum(run_max, jnp.max(score, axis=-1))
    factor = jnp.exp(run_max - new_max)
    weights = jnp.exp(score - new_max[..., None])
    new_sum = run_sum * factor + jnp.sum(weights, axis=-1)
    update = jnp.einsum(
        "hqk,khd->hqd", weights.astype(jnp.bfloat16), v_heads, preferred_element_type=jnp.float32
    )
    return (new_max, new_sum, run_acc * factor[..., None] + update)


def blockwise(carry, rows, step_fn, size):
    count = rows[0].shape[0]
    stacked = tuple((r.reshape(count // size, size, r.shape[1]) for r in rows))

    def inner(state, block):
        return (step_fn(state, block), None)

    carry, unused = lax.scan(inner, carry, stacked)
    return carry


def fresh_state(heads, count, head_dim):
    return (
        jnp.full((heads, count), -1e30, jnp.float32),
        jnp.zeros((heads, count), jnp.float32),
        jnp.zeros((heads, count, head_dim), jnp.float32),
    )


def on_device(
    latent, gn_gain, gn_bias, conv_weight, conv_bias, ln_gain, ln_bias, w_query, w_key, w_value
):
    rows_here, cols, chans = latent.shape
    groups = GROUPS
    width = chans // groups
    flat = latent.astype(jnp.float32).reshape(-1, groups, width)
    sums, squares = lax.psum(
        (jnp.sum(flat, axis=(0, 2)), jnp.sum(flat * flat, axis=(0, 2))), "band"
    )
    count_all = flat.shape[0] * width * lax.axis_size("band")
    mean = sums / count_all
    var = squares / count_all - mean * mean
    normed_g = (flat - mean[None, :, None]) * lax.rsqrt(var + 1e-05)[None, :, None]
    act = jax.nn.silu(normed_g.reshape(-1, chans) * gn_gain + gn_bias).astype(jnp.bfloat16)
    act = act.reshape(rows_here, cols, chans)
    extended = with_halo(act, (("band", 0),), 1)
    padded = jnp.pad(extended, ((0, 0), (1, 1), (0, 0)))
    total = latent.astype(jnp.float32).reshape(-1, chans) + conv_bias
    for row_off in range(3):
        for col_off in range(3):
            window = padded[row_off : row_off + rows_here, col_off : col_off + cols].reshape(
                -1, chans
            )
            total = total + jnp.dot(
                window, conv_weight[row_off, col_off], preferred_element_type=jnp.float32
            )
    hidden = total.astype(jnp.bfloat16)
    values = hidden.astype(jnp.float32)
    centre = jnp.mean(values, axis=-1, keepdims=True)
    spread = jnp.mean((values - centre) ** 2, axis=-1, keepdims=True)
    normed = ((values - centre) * lax.rsqrt(spread + 1e-05) * ln_gain + ln_bias).astype(
        jnp.bfloat16
    )
    tok_here = normed.shape[0]
    heads = HEADS
    head_dim = chans // heads
    scale = 1.0 / math.sqrt(head_dim)
    query = jnp.dot(normed, w_query, preferred_element_type=jnp.float32).astype(jnp.bfloat16)
    q_heads = query.reshape(tok_here, heads, head_dim)
    key = jnp.dot(normed, w_key, preferred_element_type=jnp.float32).astype(jnp.bfloat16)
    value = jnp.dot(normed, w_value, preferred_element_type=jnp.float32).astype(jnp.bfloat16)

    def pair_step(state, block):
        return fold_block(state, q_heads, block[0], block[1], scale)

    final = blockwise(
        fresh_state(heads, tok_here, head_dim),
        (
            lax.all_gather(key, "band", axis=0, tiled=True),
            lax.all_gather(value, "band", axis=0, tiled=True),
        ),
        pair_step,
        1024,
    )
    run_max, run_sum, run_acc = final
    attended = run_acc / run_sum[..., None]
    attended = jnp.transpose(attended, (1, 0, 2)).reshape(tok_here, chans)
    result = (values + attended).astype(jnp.bfloat16)
    return result.reshape(rows_here, cols, chans)


def solution(mesh):
    in_specs = (P(("img", "band"), None, None), P(), P(), P(), P(), P(), P(), P(), P(), P())
    out_specs = P(("img", "band"), None, None)
    return jax.shard_map(
        on_device, mesh=mesh, in_specs=in_specs, out_specs=out_specs, check_vma=False
    )
```

profile of v0, /device:TPU:1, one launch (start us, length us, event | category | flops | bytes accessed | tf_op | source)
XLA Modules:
  0.0 638.9 jit_solution(15564352180611018925)
XLA Ops:
  8.1 141.0 %all-reduce.1 = (f32[16]{0:T(128)S(1)}, f32[16]{0:T(128)S(1)}) all-reduce(f32[16]{0:T(128)S(1)} %reduce_sum.64, f32[16]{0:T(128)S(1)} %reduce_sum.61), channel_id=1, replica_groups=mesh['band'=64,'img'=4] {'band'}, use_global_device_ids=true, to_apply=%region_5.6 | all-reduce | flops 32 | bytes 256 | tf_op jit(solution)/shard_map/psum | solution.py:68
  150.9 2.2 collective-permute-start
  153.2 6.2 collective-permute-start.1
  169.9 128.6 %all-gather.5.cloned.1.call-done = bf16[16384,640]{1,0:T(8,128)(2,1)} async-done(((bf16[256,640]{1,0:T(8,128)(2,1)}), bf16[16384,640]{1,0:T(8,128)(2,1)}) %all-gather.5.cloned.1.call-update) | async-done | bytes 20971536 | tf_op jit(solution)/shard_map/all_gather | solution.py:111
  298.5 133.1 %all-gather.3.cloned.1.call-done = bf16[16384,640]{1,0:T(8,128)(2,1)} async-done(((bf16[256,640]{1,0:T(8,128)(2,1)}), bf16[16384,640]{1,0:T(8,128)(2,1)}) %all-gather.3.cloned.1.call-update) | async-done | bytes 20971536 | tf_op jit(solution)/shard_map/all_gather | solution.py:110
  431.6 197.1 %while.15 = (s32[]{:T(128)}, f32[10,256]{1,0:T(8,128)S(1)}, f32[10,256]{1,0:T(8,128)S(1)}, f32[10,256,64]{1,2,0:T(8,128)}, bf16[16,1024,640]{2,1,0:T(8,128)(2,1)...) while((s32[]{:T(128)}, f32[10,256]{1,0:T(8,128)S(1)}, ...), condition=%wide.region_11.12_spmd.clone, body=%wide.region_8.0_spmd.clone.sunk | while | flops 692564480 | bytes 46366832 | solution.py:49
  431.6 3.0 constant_dynamic-slice_fusion.3
  435.3 1.6 copy.32
  438.5 1.7 fusion.92
  440.2 2.7 fusion.94
  442.9 3.0 constant_dynamic-slice_fusion.3
  446.6 1.6 copy.32
  449.8 1.7 fusion.92
  451.5 3.8 fusion.94
  455.3 3.0 constant_dynamic-slice_fusion.3
  458.9 1.6 copy.32
  462.2 1.7 fusion.92
  463.9 3.8 fusion.94
  467.7 3.0 constant_dynamic-slice_fusion.3
  471.3 1.6 copy.32
  474.6 1.7 fusion.92
  476.3 3.8 fusion.94
  480.1 3.0 constant_dynamic-slice_fusion.3
  483.7 1.6 copy.32
  487.0 1.7 fusion.92
  488.7 3.8 fusion.94
  492.5 3.0 constant_dynamic-slice_fusion.3
  496.1 1.6 copy.32
  499.3 1.7 fusion.92
  501.1 3.8 fusion.94
  504.9 3.0 constant_dynamic-slice_fusion.3
  508.5 1.6 copy.32
  511.7 1.7 fusion.92
  513.5 3.8 fusion.94
  517.2 3.0 constant_dynamic-slice_fusion.3
  520.9 1.6 copy.32
  524.1 1.7 fusion.92
  525.9 3.8 fusion.94
  529.6 3.0 constant_dynamic-slice_fusion.3
  536.5 1.7 fusion.92
  538.2 3.8 fusion.94
  542.0 3.0 constant_dynamic-slice_fusion.3
  548.9 1.7 fusion.92
  550.6 3.8 fusion.94
  554.4 3.0 constant_dynamic-slice_fusion.3
  561.3 1.7 fusion.92
  563.0 3.8 fusion.94
  566.8 3.0 constant_dynamic-slice_fusion.3
  573.7 1.7 fusion.92
  575.4 3.8 fusion.94
  579.2 3.0 constant_dynamic-slice_fusion.3
  586.0 1.7 fusion.92
  587.8 3.8 fusion.94
  591.6 3.0 constant_dynamic-slice_fusion.3
  598.4 1.7 fusion.92
  600.2 3.8 fusion.94
  604.0 3.0 constant_dynamic-slice_fusion.3
  610.8 1.7 fusion.92
  612.6 3.8 fusion.94
  616.3 3.0 constant_dynamic-slice_fusion.3
  620.0 1.6 copy.32
  623.2 1.7 fusion.92
  625.0 3.8 fusion.94
  630.2 1.9 add_convert_fusion
  (147 shorter events, 62.5 us)
Async XLA Ops:
  6.5 160.0 %copy-start = (bf16[640,640]{1,0:T(8,128)(2,1)S(1)}, bf16[640,640]{1,0:T(8,128)(2,1)}, u32[]{:S(2)}) copy-start(bf16[640,640]{1,0:T(8,128)(2,1)} %param.21) | copy-start | bytes 2457604
  6.5 292.0 %all-gather.5.cloned.1.call-start = ((), (), s32[]{:S(2)}) async-start(), calls=%async_computation.1 | async-start | bytes 21299200 | tf_op jit(solution)/shard_map/all_gather | solution.py:111
  149.5 11.6 %copy-start.3 = (bf16[3,3,640,640]{3,2,1,0:T(8,128)(2,1)S(1)}, bf16[3,3,640,640]{3,2,1,0:T(8,128)(2,1)}, u32[]{:S(2)}) copy-start(bf16[3,3,640,640]{3,2,1,0:T(8,128)(2,1)} %param.15) | copy-start | bytes 22118404
  150.9 9.6 %collective-permute-start = (bf16[1,128,640]{2,1,0:T(8,128)(2,1)S(1)}, bf16[1,128,640]{2,1,0:T(8,128)(2,1)S(1)}, u32[]{:S(2)}, u32[]{:S(2)}) collective-permute-start(bf16[1,128,640]{2,1,0:T(8,128)(2,1)S(1)} %get-tuple-element.124), channel_id=1, source_target_pairs={{0,4},{4,8},{8,12},{12,16},{16,20},{20,24},{24,28},{28,32},{32,36}... | collective-permute-start | bytes 491528 | tf_op jit(solution)/shard_map/ppermute | solution.py:19
  153.2 7.4 %collective-permute-start.1 = (bf16[1,128,640]{2,1,0:T(8,128)(2,1)S(1)}, bf16[1,128,640]{2,1,0:T(8,128)(2,1)S(1)}, u32[]{:S(2)}, u32[]{:S(2)}) collective-permute-start(bf16[1,128,640]{2,1,0:T(8,128)(2,1)S(1)} %get-tuple-element.125), channel_id=1, source_target_pairs={{4,0},{8,4},{12,8},{16,12},{20,16},{24,20},{28,24},{32,28},{36,32}... | collective-permute-start | bytes 491528 | tf_op jit(solution)/shard_map/ppermute | solution.py:20
  163.0 3.4 copy-start.6
  163.0 3.3 copy-start.7
  163.5 4.5 copy-start.4
  163.5 5.8 copy-start.5
  165.5 0.9 copy-start.2
  167.8 263.8 %all-gather.3.cloned.1.call-start = ((), (), s32[]{:S(2)}) async-start(), calls=%async_computation | async-start | bytes 21299200 | tf_op jit(solution)/shard_map/all_gather | solution.py:110
  628.7 3.4 copy-start.1
Sparse Core Ops, SparseCore 0:
  167.9 130.6 all-gather.4
  300.4 131.1 all-gather.2
where the time goes:
time: 641 us; the launch traced here: 639 us
  waiting for transfers between devices  262 us (41%)
  blocking collectives  141 us (22%)
  matrix products  91.8 us (14%)
  local copies, waits for them, and re-layouts  85.8 us (13%)
  other arithmetic  35.5 us (6%)
  between operations  13.7 us (2%)
  starting transfers between devices  8.6 us (1%)
    psum x1, blocking collectives, on_device(): lax.psum((jnp.sum(flat, axis=(0, 2)), jnp.sum(flat * flat, axis=(0, 2))),...  141 us
    all_gather x1, waiting for transfers between devices, on_device(): lax.all_gather(key, 'band', axis=0, tiled=True)  133 us
    all_gather x1, waiting for transfers between devices, on_device(): lax.all_gather(value, 'band', axis=0, tiled=True)  129 us
    dynamic_slice x48, local copies, waits for them, and re-layouts, blockwise(): carry, unused = lax.scan(inner, carry, stacked)  83.9 us
    dot_general x16, matrix products, fold_block(): jnp.einsum('hqk,khd->hqd', weights.astype(jnp.bfloat16), v_heads, preferr...  59.3 us
    reduce_sum x16, other arithmetic, fold_block(): new_sum = run_sum * factor + jnp.sum(weights, axis=-1)  27.4 us
    dot_general x16, matrix products, fold_block(): jnp.einsum('qhd,khd->hqk', q_heads, k_heads, preferred_element_type=jnp.f...  25.4 us
  transfers between devices with their start and end apart: 4, of which 2 were waited for; matrix products, arithmetic and copies ran while one was open for 0% of the time, Pallas kernels for 0%

commit v1 on v0

v1 whole, which is shorter than its diff:
```python
import functools
import math

import jax
import jax.numpy as jnp
from jax import lax
from jax.experimental import pallas as pl
from jax.experimental.pallas import tpu as pltpu
from jax.sharding import Mesh
from jax.sharding import PartitionSpec as P

HEADS = 10
HEAD_DIM = 64
GROUPS = 16
NX, NZ, NY, NC = (4, 2, 4, 2)
BAND = ("x", "z", "y", "core")
RING = ("y", "core")
SETS = NX * NZ
BANDS = NX * NZ * NY * NC
TILE = 512
TILES = 4
LANES = 128
Q_ROWS = 256
KV_ROWS = 320
SEND_ROWS = Q_ROWS + KV_ROWS
BACK_ROWS = 272
HIGH = 2.0**100
LOW = 2.0**-60
BF16 = jnp.bfloat16
F32 = jnp.float32
VMEM = pltpu.CompilerParams(vmem_limit_bytes=24 * 1024 * 1024)


def total_of(value):
    for axis, size in (("y", NY), (("z", "core"), NZ * NC), ("x", NX)):
        parts = [value]
        for step in range(1, size):
            perm = [(i, (i + step) % size) for i in range(size)]
            parts.append(lax.ppermute(value, axis, perm))
        value = sum(parts[1:], parts[0])
    return value


def halo(latent):
    up = [(i, i + 1) for i in range(BANDS - 1)]
    down = [(j, i) for i, j in up]
    before = lax.ppermute(latent[-1:], BAND, up)
    after = lax.ppermute(latent[:1], BAND, down)
    return before, after


def dot(a, b):
    return jnp.dot(a, b, preferred_element_type=F32)


def swap(a):
    return jnp.concatenate([a[:, 64:128], a[:, 0:64]], axis=1)


def lanes(rows):
    return lax.broadcasted_iota(jnp.int32, (rows, LANES), 1)


def front_kernel(
    sums_ref, vec_ref, before_ref, after_ref, latent_hbm, conv_hbm, wq_hbm, wk_hbm, wv_hbm,
    hidden_ref, send_ref, shift_ref, latent_ref, conv_ref, w_ref, sems,
):
    copies = [pltpu.make_async_copy(latent_hbm, latent_ref, sems.at[0])]
    for i in range(3):
        copies.append(pltpu.make_async_copy(conv_hbm.at[i], conv_ref.at[i], sems.at[1 + i]))
    for i, w_hbm in enumerate((wq_hbm, wk_hbm, wv_hbm)):
        copies.append(pltpu.make_async_copy(w_hbm, w_ref.at[i], sems.at[4 + i]))
    for copy in copies:
        copy.start()
    chans = latent_ref.shape[2]
    count = float(BANDS * 256 * (chans // GROUPS))
    mean = sums_ref[0:1] / count
    var = sums_ref[1:2] / count - mean * mean
    rate = lax.rsqrt(var + 1e-05)
    gain, bias = vec_ref[0:1], vec_ref[1:2]
    row = lax.broadcasted_iota(jnp.int32, (128, chans), 0)
    copies[0].wait()
    sources = [before_ref[0], latent_ref[0], latent_ref[1], after_ref[0]]
    for r, source in enumerate(sources):
        value = (source.astype(F32) - mean) * rate * gain + bias
        act = value / (1.0 + jnp.exp(-value))
        if r == 0:
            act = act * vec_ref[5:6]
        if r == 3:
            act = act * vec_ref[6:7]
        here = slice(128 * r, 128 * r + 128)
        left = jnp.where(row == 0, 0.0, pltpu.roll(act, 1, 0))
        right = jnp.where(row == 127, 0.0, pltpu.roll(act, 127, 0))
        shift_ref[0, here] = left.astype(BF16)
        shift_ref[1, here] = act.astype(BF16)
        shift_ref[2, here] = right.astype(BF16)
    total = latent_ref[...].reshape(256, chans).astype(F32) + vec_ref[2:3]
    for i in range(3):
        copies[1 + i].wait()
        for col in range(3):
            total = total + dot(shift_ref[col, 128 * i : 128 * i + 256, :], conv_ref[i, col])
    hidden = total.astype(BF16)
    hidden_ref[...] = hidden
    values = hidden.astype(F32)
    values = values - jnp.mean(values, axis=1, keepdims=True)
    spread = jnp.mean(values * values, axis=1, keepdims=True)
    normed = (values * lax.rsqrt(spread + 1e-05) * vec_ref[3:4] + vec_ref[4:5]).astype(BF16)
    scale = math.log2(math.e) / math.sqrt(HEAD_DIM)
    copies[4].wait()
    query = (dot(normed, w_ref[0]) * scale).astype(BF16)
    copies[5].wait()
    key = dot(normed, w_ref[1]).T.astype(BF16)
    copies[6].wait()
    value = dot(normed, w_ref[2]).astype(BF16)
    for s in range(SETS):
        main, extra, part = 64 * s, 64 * (SETS + s // 4), 64 * (s % 4)
        send_ref[s, 0:256] = jnp.concatenate(
            [query[:, main : main + 64], query[:, extra : extra + 64]], axis=1
        )
        send_ref[s, 256:320] = key[main : main + 64, 0:128]
        send_ref[s, 320:384] = key[main : main + 64, 128:256]
        send_ref[s, 384:512] = jnp.concatenate(
            [value[0:128, main : main + 64], value[128:256, main : main + 64]], axis=1
        )
        send_ref[s, 512:576] = jnp.concatenate(
            [key[extra : extra + 64, part : part + 64], value[part : part + 64, extra : extra + 64]],
            axis=1,
        )


def front(sums, vec, before, after, latent, conv_weight, w_query, w_key, w_value):
    chans = latent.shape[2]
    far = [latent, conv_weight, w_query, w_key, w_value]
    far = [pltpu.with_memory_space_constraint(a, pltpu.HBM) for a in far]
    return pl.pallas_call(
        front_kernel,
        in_specs=[pl.BlockSpec(memory_space=pltpu.VMEM)] * 4
        + [pl.BlockSpec(memory_space=pltpu.HBM)] * 5,
        out_specs=[pl.BlockSpec(memory_space=pltpu.VMEM)] * 2,
        out_shape=[
            jax.ShapeDtypeStruct((256, chans), BF16),
            jax.ShapeDtypeStruct((SETS, SEND_ROWS, LANES), BF16),
        ],
        scratch_shapes=[
            pltpu.VMEM((3, 512, chans), BF16),
            pltpu.VMEM(latent.shape, BF16),
            pltpu.VMEM(conv_weight.shape, BF16),
            pltpu.VMEM((3, chans, chans), BF16),
            pltpu.SemaphoreType.DMA((7,)),
        ],
        compiler_params=VMEM,
        name="front",
    )(sums, vec, before, after, *far)


def main_step(kv_ref, pair):
    lane = lanes(128)
    keys, values = [], []
    for src in (2 * pair, 2 * pair + 1):
        keys += [kv_ref[src, 0:64, :], kv_ref[src, 64:128, :]]
        value = kv_ref[src, 128:256, :]
        for side in (value, swap(value)):
            values.append(jnp.where(lane < 64, side, jnp.ones_like(side)))
    keys = jnp.concatenate([jnp.concatenate(keys, axis=1), jnp.zeros((64, TILE), BF16)], axis=0)
    return 0, keys, jnp.concatenate(values, axis=0)


def extra_step(kv_ref, block):
    lane = lanes(64)
    sources = [SETS * block + src for src in range(SETS)]
    keys = [kv_ref[src, 256:320, 0:64] for src in sources]
    values = [kv_ref[src, 256:320, :] for src in sources]
    values = [jnp.where(lane >= 64, v, jnp.ones_like(v)) for v in values]
    keys = jnp.concatenate([jnp.zeros((64, TILE), BF16), jnp.concatenate(keys, axis=1)], axis=0)
    return 1, keys, jnp.concatenate(values, axis=0)


def fold_kernel(count, first, last, q_ref, *refs):
    kv_refs, refs = refs[:count], refs[count:]
    if not first:
        acc_in, refs = refs[0], refs[1:]
    if last:
        far_refs, refs = refs[:SETS], refs[SETS:]
    acc_ref = refs[0]
    acc_ref[0] = jnp.zeros((2, TILE, LANES), F32) if first else acc_in[0]
    query = q_ref[...].reshape(TILE, LANES)

    steps = []
    for kv_ref in kv_refs:
        steps += [functools.partial(main_step, kv_ref, pair) for pair in range(SETS // 2)]
        steps.append(functools.partial(extra_step, kv_ref, 0))
    held = None
    for step in steps + [None]:
        if step is not None:
            kind, keys, values = step()
            score = dot(query, keys)
        if held is not None:
            held_kind, held_score, held_values = held
            weight = jnp.exp2(held_score).astype(BF16)
            acc_ref[0, held_kind] += dot(weight, held_values)
        held = None if step is None else (kind, score, values)

    if last:
        out_ref, store_ref, top_ref, sems = refs[1:]
        wide = lanes(TILE)
        total = jnp.where(wide < 64, acc_ref[0, 1], acc_ref[0, 0])
        good = (jnp.min(total) > LOW) & (jnp.max(total) < HIGH)
        top_ref[...] = jnp.zeros((2, TILE, LANES), F32)

        @pl.when(jnp.logical_not(good))
        def _():
            copies = []
            for i, far_ref in enumerate(far_refs):
                here = store_ref.at[pl.ds(SETS * i, SETS)]
                copies.append(pltpu.make_async_copy(far_ref, here, sems.at[i]))
                copies[-1].start()
            acc_ref[0] = jnp.zeros((2, TILE, LANES), F32)
            top_ref[...] = jnp.full((2, TILE, LANES), -1e30, F32)
            for copy in copies:
                copy.wait()

            def online(step):
                kind, keys, values = step
                score = dot(query, keys)
                top = jnp.maximum(top_ref[kind], jnp.max(score, axis=1, keepdims=True))
                weight = jnp.exp2(score - top[:, 0:1]).astype(BF16)
                factor = jnp.exp2(top_ref[kind] - top)
                acc_ref[0, kind] = acc_ref[0, kind] * factor + dot(weight, values)
                top_ref[kind] = top

            def pair_body(pair, carry):
                online(main_step(store_ref, pair))
                return carry

            def block_body(block, carry):
                online(extra_step(store_ref, block))
                return carry

            lax.fori_loop(0, SETS * SETS // 2, pair_body, 0)
            lax.fori_loop(0, SETS, block_body, 0)

        main, extra = acc_ref[0, 0], acc_ref[0, 1]
        out = jnp.where(wide < 64, main / swap(main), extra / swap(extra)).astype(BF16)
        level = (jnp.log2(extra) + top_ref[1])[:, 0:1]
        row = lax.broadcasted_iota(jnp.int32, (16, LANES), 0)
        for src in range(2):
            out_ref[src, 0:256] = out[256 * src : 256 * src + 256]
            tail = jnp.zeros((16, LANES), F32)
            for half in range(2):
                base = 256 * src + 128 * half
                line = jnp.broadcast_to(level[base : base + 128], (128, LANES)).T[0:16]
                for part in range(3):
                    piece = line.astype(BF16).astype(F32)
                    tail = jnp.where(row == 2 * part + half, piece, tail)
                    line = line - piece
            out_ref[src, 256:272] = tail.astype(BF16)


def fold(got, blocks, acc, every=None):
    first, last = acc is None, every is not None
    acc_spec = pl.BlockSpec((1, 2, TILE, LANES), lambda t: (t, 0, 0, 0))
    kv_spec = pl.BlockSpec((SETS, KV_ROWS, LANES), lambda t: (0, 0, 0))
    out_specs = [acc_spec]
    out_shape = [jax.ShapeDtypeStruct((TILES, 2, TILE, LANES), F32)]
    scratch = []
    if last:
        out_specs.append(pl.BlockSpec((2, BACK_ROWS, LANES), lambda t: (t, 0, 0)))
        out_shape.append(jax.ShapeDtypeStruct((SETS, BACK_ROWS, LANES), BF16))
        scratch = [
            pltpu.VMEM((SETS * SETS, KV_ROWS, LANES), BF16),
            pltpu.VMEM((2, TILE, LANES), F32),
            pltpu.SemaphoreType.DMA((SETS,)),
        ]
    return pl.pallas_call(
        functools.partial(fold_kernel, len(blocks), first, last),
        grid=(TILES,),
        in_specs=[pl.BlockSpec((2, Q_ROWS, LANES), lambda t: (t, 0, 0))]
        + [kv_spec] * len(blocks)
        + ([] if first else [acc_spec])
        + ([pl.BlockSpec(memory_space=pl.ANY)] * SETS if last else []),
        out_specs=out_specs,
        out_shape=out_shape,
        scratch_shapes=scratch,
        input_output_aliases={} if first else {1 + len(blocks): 0},
        compiler_params=VMEM,
        name="fold",
    )(got, *blocks, *(() if first else (acc,)), *(every or ()))


def on_device(
    latent, gn_gain, gn_bias, conv_weight, conv_bias, ln_gain, ln_bias, w_query, w_key, w_value
):
    rows_here, cols, chans = latent.shape
    tokens = rows_here * cols
    width = chans // GROUPS
    before, after = halo(latent)
    flat = latent.astype(F32).reshape(-1, chans)
    sums = jnp.stack([jnp.sum(flat, axis=0), jnp.sum(flat * flat, axis=0)])
    sums = jnp.sum(sums.reshape(2, GROUPS, width), axis=2, keepdims=True)
    sums = total_of(jnp.broadcast_to(sums, (2, GROUPS, width)).reshape(2, chans))
    place = lax.axis_index(BAND)
    row = lax.broadcasted_iota(jnp.int32, (8, chans), 0)
    vec = jnp.where(row == 5, jnp.where(place > 0, 1.0, 0.0), 0.0)
    vec = jnp.where(row == 6, jnp.where(place < BANDS - 1, 1.0, 0.0), vec)
    for i, part in enumerate((gn_gain, gn_bias, conv_bias, ln_gain, ln_bias)):
        vec = jnp.where(row == i, part, vec)
    hidden, send = front(
        sums, vec, before, after, latent, conv_weight, w_query, w_key, w_value
    )

    got = lax.all_to_all(send, ("x", "z"), 0, 0)
    own = got[:, Q_ROWS:]
    spots = [(y, c) for y in range(NY) for c in range(NC)]
    along = [(2 * y + c, 2 * ((y + 1 - 2 * c) % NY) + c) for y, c in spots]
    against = [(j, i) for i, j in along]
    cross = [(2 * y + c, 2 * y + 1 - c) for y, c in spots]

    tied = lax.optimization_barrier
    twin = lax.ppermute(own, RING, cross)
    ahead = lax.ppermute(own, RING, along)
    (acc,) = fold(got, [own], None)
    own, acc = tied((own, acc))
    behind = lax.ppermute(own, RING, against)
    (acc,) = fold(got, [twin], acc)
    ahead, acc = tied((ahead, acc))
    ahead_twin = lax.ppermute(ahead, RING, cross)
    (acc,) = fold(got, [ahead], acc)
    ahead, acc = tied((ahead, acc))
    far = lax.ppermute(ahead, RING, along)
    (acc,) = fold(got, [behind], acc)
    behind, acc = tied((behind, acc))
    behind_twin = lax.ppermute(behind, RING, cross)
    (acc,) = fold(got, [ahead_twin], acc)
    far, acc = tied((far, acc))
    far_twin = lax.ppermute(far, RING, cross)
    (acc,) = fold(got, [behind_twin, far], acc)
    every = [own, twin, ahead, behind, ahead_twin, behind_twin, far, far_twin]
    unused, out = fold(got, [far_twin], acc, every)

    back = lax.all_to_all(out, ("x", "z"), 0, 0)
    main = back[:, :256, :64].transpose(1, 0, 2).reshape(tokens, SETS * HEAD_DIM)
    level = jnp.sum(back[:, 256:262].astype(F32).reshape(SETS, 3, 256), axis=1).reshape(2, 4, 256)
    share = jnp.exp2(level - jnp.max(level, axis=1, keepdims=True))
    share = share / jnp.sum(share, axis=1, keepdims=True)
    extra = back[:, :256, 64:].astype(F32).reshape(2, 4, 256, HEAD_DIM)
    extra = jnp.sum(extra * share[..., None], axis=1).transpose(1, 0, 2)
    extra = extra.reshape(tokens, 2 * HEAD_DIM)
    attended = jnp.concatenate([main.astype(F32), extra], axis=1)
    return (hidden.astype(F32) + attended).astype(BF16).reshape(rows_here, cols, chans)


def solution(mesh):
    inner = Mesh(mesh.devices.reshape(NX, NZ, NY, NC, -1), BAND + ("img",))
    place = P(("img",) + BAND, None, None)
    in_specs = (place,) + (P(),) * 9
    return jax.shard_map(
        on_device, mesh=inner, in_specs=in_specs, out_specs=place, check_vma=False
    )
```

time: 641 us -> 257 us (0.40)
  waiting for transfers between devices: 262 us -> 3.02 us
  Pallas kernels: 0 us -> 187 us
  blocking collectives: 141 us -> 28.7 us
  matrix products: 91.8 us -> 0 us
  local copies, waits for them, and re-layouts: 85.8 us -> 2.05 us
  other arithmetic: 35.5 us -> 3.59 us
  starting transfers between devices: 8.6 us -> 31.8 us
  between operations: 13.7 us -> 0.35 us
    all_gather x2 -> x0, waiting for transfers between devices: 262 us -> none  [the longest x1 133 us: on_device(): lax.all_gather(key, 'band', axis=0, tiled=True)]
    pallas_call x0 -> x8, Pallas kernels: none -> 187 us  [the longest x7 180 us: fold(): pl.pallas_call(functools.partial(fold_kernel, len(blocks), first, last),...]
    psum x1 -> x0, blocking collectives: 141 us -> none  [on_device(): lax.psum((jnp.sum(flat, axis=(0, 2)), jnp.sum(flat * flat, axis=(0, 2))),...]
    dot_general x44 -> x0, matrix products: 91.8 us -> none  [the longest x16 59.3 us: fold_block(): jnp.einsum('hqk,khd->hqd', weights.astype(jnp.bfloat16), v_heads, preferr...]
    dynamic_slice x48 -> x0, local copies, waits for them, and re-layouts: 83.9 us -> none  [blockwise(): carry, unused = lax.scan(inner, carry, stacked)]
    all_to_all x0 -> x2, blocking collectives: none -> 28.7 us  [the longest x1 15.7 us: on_device(): got = lax.all_to_all(send, ('x', 'z'), 0, 0)]
    reduce_sum x20 -> x3, other arithmetic: 29 us -> 1.44 us  [the longest x1 1.08 us: on_device(): sums = jnp.stack([jnp.sum(flat, axis=0), jnp.sum(flat * flat, axis=0)])]
    ppermute x2 -> x18, starting transfers between devices: 8.37 us -> 31.8 us  [the longest x9 12 us: total_of(): parts.append(lax.ppermute(value, axis, perm))]
  transfers between devices with their start and end apart: 4 -> 18, of which waited for: 2 -> 3; matrix products, arithmetic and copies ran while one was open for 0% -> 1% of each run, Pallas kernels for 0% -> 17%
where the time goes in v1:
time: 257 us; the launch traced here: 256 us
  Pallas kernels  187 us (73%)
  starting transfers between devices  31.8 us (12%)
  blocking collectives  28.7 us (11%)
  other arithmetic  3.59 us (1%)
  waiting for transfers between devices  3.02 us (1%)
    pallas_call x7, Pallas kernels, fold(): pl.pallas_call(functools.partial(fold_kernel, len(blocks), first, last),...  180 us
    all_to_all x1, blocking collectives, on_device(): got = lax.all_to_all(send, ('x', 'z'), 0, 0)  15.7 us
    all_to_all x1, blocking collectives, on_device(): back = lax.all_to_all(out, ('x', 'z'), 0, 0)  12.9 us
    ppermute x9, starting transfers between devices, total_of(): parts.append(lax.ppermute(value, axis, perm))  12 us
    pallas_call x1, Pallas kernels, front(): pl.pallas_call(front_kernel, in_specs=[pl.BlockSpec(memory_space=pltpu.VM...  6.88 us
    ppermute x1, starting transfers between devices, on_device(): twin = lax.ppermute(own, RING, cross)  5.25 us
  transfers between devices with their start and end apart: 18, of which 3 were waited for; matrix products, arithmetic and copies ran while one was open for 1% of the time, Pallas kernels for 17%

profile of v1, /device:TPU:1, one launch (start us, length us, event | category | flops | bytes accessed | tf_op | source)
XLA Modules:
  0.0 256.3 jit_solution(6350125954135524234)
XLA Ops:
  0.0 1.1 convert_reduce_fusion
  1.1 0.1 stack.9
  1.2 0.1 stack.10
  1.3 0.2 fusion.1
  1.4 0.1 reshape.44
  1.5 3.6 %collective-permute-start.2 = (f32[2,640]{1,0:T(2,128)S(1)}, f32[2,640]{1,0:T(2,128)S(1)}, u32[]{:S(2)}, u32[]{:S(2)}) collective-permute-start(f32[2,640]{1,0:T(2,128)S(1)} %reshape.44), channel_id=1, source_target_pairs={{0,24},{8,0},{16,8},{24,16},{1,25},{9,1},{17,9},{25,17},{2,26},{10... | collective-permute-start | bytes 15368 | tf_op jit(solution)/shard_map/ppermute | solution.py:39
  5.2 0.3 collective-permute-start.1
  5.5 0.7 collective-permute-start
  6.2 1.0 fusion.15
  7.2 3.4 %collective-permute-start.10 = (bf16[1,128,640]{2,1,0:T(8,128)(2,1)S(1)}, bf16[1,128,640]{2,1,0:T(8,128)(2,1)S(1)}, u32[]{:S(2)}, u32[]{:S(2)}) collective-permute-start(bf16[1,128,640]{2,1,0:T(8,128)(2,1)S(1)} %get-tuple-element.35), channel_id=1, source_target_pairs={{4,0},{8,4},{12,8},{16,12},{20,16},{24,20},{28,24},{32,28},{36,32}... | collective-permute-start | bytes 491528 | tf_op jit(solution)/shard_map/ppermute | solution.py:48
  10.7 3.4 %collective-permute-start.9 = (bf16[1,128,640]{2,1,0:T(8,128)(2,1)S(1)}, bf16[1,128,640]{2,1,0:T(8,128)(2,1)S(1)}, u32[]{:S(2)}, u32[]{:S(2)}) collective-permute-start(bf16[1,128,640]{2,1,0:T(8,128)(2,1)S(1)} %get-tuple-element.36), channel_id=1, source_target_pairs={{0,4},{4,8},{8,12},{12,16},{16,20},{20,24},{24,28},{28,32},{32,36}... | collective-permute-start | bytes 491528 | tf_op jit(solution)/shard_map/ppermute | solution.py:47
  14.1 0.0 collective-permute-done.2
  14.2 0.0 collective-permute-done.1
  14.2 0.0 collective-permute-done
  14.2 0.1 collective-permute-start.5
  14.3 1.7 collective-permute-start.4
  16.0 1.9 collective-permute-start.3
  17.9 0.0 collective-permute-done.5
  17.9 0.0 collective-permute-done.4
  17.9 0.8 collective-permute-done.3
  18.7 2.5 collective-permute-start.8
  21.2 0.5 collective-permute-start.7
  21.7 0.6 collective-permute-start.6
  22.3 0.8 select_select_fusion.vec_ref
  23.1 0.0 collective-permute-done.8
  23.2 2.0 collective-permute-done.7
  25.2 0.2 collective-permute-done.6
  25.4 0.0 collective-permute-done.10.after_ref
  25.4 0.0 collective-permute-done.9.before_ref
  25.4 6.9 %front.1 = (bf16[256,640]{1,0:T(8,128)(2,1)S(1)}, bf16[8,576,128]{2,1,0:T(8,128)(2,1)S(1)}) custom-call(f32[2,640]{1,0:T(2,128)S(1)} %add_add_fusion.sums_ref, f32[8,640]{1,0:T(8,128)S(1)} %select_select_fusion.vec_ref, bf16[1,128,640]{2,1,0:T(8,128)(2,1)S(1)} %collective-permute-done.9.before_ref, ...), custom_call_target="tpu_custom_call" | custom-call | tf_op jit(solution)/shard_map/front/pallas_call | solution.py:135
  32.3 15.7 %all_to_all.10.q_ref = bf16[8,576,128]{2,1,0:T(8,128)(2,1)S(1)} all-to-all(bf16[8,576,128]{2,1,0:T(8,128)(2,1)S(1)} %get-tuple-element.19), channel_id=1, replica_groups=mesh['x'=4,'z'=2,'y'=4,'core'=2,'img'=4] {'x','z'}, dimensions={0} | all-to-all | bytes 2359296 | tf_op jit(solution)/shard_map/all_to_all | solution.py:311
  48.1 5.3 %collective-permute-start.12 = (bf16[8,320,128]{2,1,0:T(8,128)(2,1)S(1)}, bf16[8,320,128]{2,1,0:T(8,128)(2,1)S(1)}, u32[]{:S(2)}, u32[]{:S(2)}) collective-permute-start(bf16[8,320,128]{2,1,0:T(8,128)(2,1)S(1)} %slice.24.refs_0_.refs_2_), channel_id=1, source_target_pairs={{0,4},{4,0},{8,12},{12,8},{16,20},{20,16},{24,28},{28,24},{1,5},{5... | collective-permute-start | bytes 1966088 | tf_op jit(solution)/shard_map/ppermute | solution.py:319
  53.4 3.9 %collective-permute-start.11 = (bf16[8,320,128]{2,1,0:T(8,128)(2,1)S(1)}, bf16[8,320,128]{2,1,0:T(8,128)(2,1)S(1)}, u32[]{:S(2)}, u32[]{:S(2)}) collective-permute-start(bf16[8,320,128]{2,1,0:T(8,128)(2,1)S(1)} %slice.24.refs_0_.refs_2_), channel_id=1, source_target_pairs={{0,8},{4,28},{8,16},{12,4},{16,24},{20,12},{24,0},{28,20},{1,9},{5... | collective-permute-start | bytes 1966088 | tf_op jit(solution)/shard_map/ppermute | solution.py:320
  57.2 6.1 %fold.7.refs_1_ = f32[4,2,512,128]{3,2,1,0:T(8,128)S(1)} custom-call(bf16[8,576,128]{2,1,0:T(8,128)(2,1)S(1)} %all_to_all.10.q_ref, bf16[8,320,128]{2,1,0:T(8,128)(2,1)S(1)} %slice.24.refs_0_.refs_2_), custom_call_target="tpu_custom_call" | custom-call | tf_op jit(solution)/shard_map/fold/pallas_call | solution.py:274
  63.3 0.1 collective-permute-start.15
  63.4 0.0 collective-permute-done.12.refs_0_.refs_3_
  63.4 6.2 %fold.8.refs_1_ = f32[4,2,512,128]{3,2,1,0:T(8,128)S(1)} custom-call(bf16[8,576,128]{2,1,0:T(8,128)(2,1)S(1)} %all_to_all.10.q_ref, bf16[8,320,128]{2,1,0:T(8,128)(2,1)S(1)} %collective-permute-done.12.refs_0_.refs_3_, f32[4,2,512,128]{3,2,1,0:T(8,128)S(1)} %fold.7.refs_1_), custom_call_target="tpu_custom_call", output_to_operand_aliasing={{}: (2, {})} | custom-call | tf_op jit(solution)/shard_map/fold/pallas_call | solution.py:274
  69.7 0.0 collective-permute-done.11.refs_0_.refs_4_
  69.7 0.4 collective-permute-start.14
  70.1 6.2 %fold.9.refs_1_ = f32[4,2,512,128]{3,2,1,0:T(8,128)S(1)} custom-call(bf16[8,576,128]{2,1,0:T(8,128)(2,1)S(1)} %all_to_all.10.q_ref, bf16[8,320,128]{2,1,0:T(8,128)(2,1)S(1)} %collective-permute-done.11.refs_0_.refs_4_, f32[4,2,512,128]{3,2,1,0:T(8,128)S(1)} %fold.8.refs_1_), custom_call_target="tpu_custom_call", output_to_operand_aliasing={{}: (2, {})} | custom-call | tf_op jit(solution)/shard_map/fold/pallas_call | solution.py:274
  76.4 2.4 collective-permute-start.13
  78.7 0.0 collective-permute-done.15.refs_0_.refs_5_
  78.8 6.2 %fold.10.refs_1_ = f32[4,2,512,128]{3,2,1,0:T(8,128)S(1)} custom-call(bf16[8,576,128]{2,1,0:T(8,128)(2,1)S(1)} %all_to_all.10.q_ref, bf16[8,320,128]{2,1,0:T(8,128)(2,1)S(1)} %collective-permute-done.15.refs_0_.refs_5_, f32[4,2,512,128]{3,2,1,0:T(8,128)S(1)} %fold.9.refs_1_), custom_call_target="tpu_custom_call", output_to_operand_aliasing={{}: (2, {})} | custom-call | tf_op jit(solution)/shard_map/fold/pallas_call | solution.py:274
  85.0 0.1 collective-permute-start.17
  85.1 0.0 collective-permute-done.14.refs_0_.refs_6_
  85.1 6.2 %fold.11.refs_2_ = f32[4,2,512,128]{3,2,1,0:T(8,128)S(1)} custom-call(bf16[8,576,128]{2,1,0:T(8,128)(2,1)S(1)} %all_to_all.10.q_ref, bf16[8,320,128]{2,1,0:T(8,128)(2,1)S(1)} %collective-permute-done.14.refs_0_.refs_6_, f32[4,2,512,128]{3,2,1,0:T(8,128)S(1)} %fold.10.refs_1_), custom_call_target="tpu_custom_call", output_to_operand_aliasing={{}: (2, {})} | custom-call | tf_op jit(solution)/shard_map/fold/pallas_call | solution.py:274
  91.3 0.0 collective-permute-done.13.refs_1_.refs_8_
  91.3 0.8 collective-permute-start.16
  92.1 0.0 collective-permute-done.17.refs_0_.refs_7_
  92.1 12.2 %fold.12.refs_1_ = f32[4,2,512,128]{3,2,1,0:T(8,128)S(1)} custom-call(bf16[8,576,128]{2,1,0:T(8,128)(2,1)S(1)} %all_to_all.10.q_ref, bf16[8,320,128]{2,1,0:T(8,128)(2,1)S(1)} %collective-permute-done.17.refs_0_.refs_7_, bf16[8,320,128]{2,1,0:T(8,128)(2,1)S(1)} %collective-permute-done.13.refs_1_.refs_8_, ...), custom_call_target="tpu_custom_call", output_to_operand_aliasing={{}: (3, {})} | custom-call | tf_op jit(solution)/shard_map/fold/pallas_call | solution.py:274
  104.3 0.0 collective-permute-done.16.refs_0_.refs_9_
  104.4 136.8 %fold.13 = (f32[4,2,512,128]{3,2,1,0:T(8,128)S(1)}, bf16[8,272,128]{2,1,0:T(8,128)(2,1)S(1)}) custom-call(bf16[8,576,128]{2,1,0:T(8,128)(2,1)S(1)} %all_to_all.10.q_ref, bf16[8,320,128]{2,1,0:T(8,128)(2,1)S(1)} %collective-permute-done.16.refs_0_.refs_9_, f32[4,2,512,128]{3,2,1,0:T(8,128)S(1)} %fold.12.refs_1_, ...), custom_call_target="tpu_custom_call", output_to_operand_aliasing={{0}: (2, {})} | custom-call | tf_op jit(solution)/shard_map/fold/pallas_call | solution.py:274
  241.1 12.9 %all_to_all.11 = bf16[8,272,128]{2,1,0:T(8,128)(2,1)S(1)} all-to-all(bf16[8,272,128]{2,1,0:T(8,128)(2,1)S(1)} %get-tuple-element.30), channel_id=1, replica_groups=mesh['x'=4,'z'=2,'y'=4,'core'=2,'img'=4] {'x','z'}, dimensions={0} | all-to-all | bytes 1114112 | tf_op jit(solution)/shard_map/all_to_all | solution.py:340
  254.2 0.3 convert_bitcast_fusion
  254.4 0.3 copy.24
  254.7 0.2 copy.26
  254.9 0.3 fusion.5
  255.3 0.1 copy.25
  255.4 0.1 copy.27
  255.5 0.8 fusion.7
  (13 shorter events, 0.2 us)
Async XLA Ops:
  1.5 12.6 %collective-permute-start.2 = (f32[2,640]{1,0:T(2,128)S(1)}, f32[2,640]{1,0:T(2,128)S(1)}, u32[]{:S(2)}, u32[]{:S(2)}) collective-permute-start(f32[2,640]{1,0:T(2,128)S(1)} %reshape.44), channel_id=1, source_target_pairs={{0,24},{8,0},{16,8},{24,16},{1,25},{9,1},{17,9},{25,17},{2,26},{10... | collective-permute-start | bytes 15368 | tf_op jit(solution)/shard_map/ppermute | solution.py:39
  5.2 9.0 %collective-permute-start.1 = (f32[2,640]{1,0:T(2,128)S(1)}, f32[2,640]{1,0:T(2,128)S(1)}, u32[]{:S(2)}, u32[]{:S(2)}) collective-permute-start(f32[2,640]{1,0:T(2,128)S(1)} %reshape.44), channel_id=1, source_target_pairs={{0,16},{8,24},{16,0},{24,8},{1,17},{9,25},{17,1},{25,9},{2,18},{10... | collective-permute-start | bytes 15368 | tf_op jit(solution)/shard_map/ppermute | solution.py:39
  5.5 8.6 %collective-permute-start = (f32[2,640]{1,0:T(2,128)S(1)}, f32[2,640]{1,0:T(2,128)S(1)}, u32[]{:S(2)}, u32[]{:S(2)}) collective-permute-start(f32[2,640]{1,0:T(2,128)S(1)} %reshape.44), channel_id=1, source_target_pairs={{0,8},{8,16},{16,24},{24,0},{1,9},{9,17},{17,25},{25,1},{2,10},{10... | collective-permute-start | bytes 15368 | tf_op jit(solution)/shard_map/ppermute | solution.py:39
  7.2 18.2 %collective-permute-start.10 = (bf16[1,128,640]{2,1,0:T(8,128)(2,1)S(1)}, bf16[1,128,640]{2,1,0:T(8,128)(2,1)S(1)}, u32[]{:S(2)}, u32[]{:S(2)}) collective-permute-start(bf16[1,128,640]{2,1,0:T(8,128)(2,1)S(1)} %get-tuple-element.35), channel_id=1, source_target_pairs={{4,0},{8,4},{12,8},{16,12},{20,16},{24,20},{28,24},{32,28},{36,32}... | collective-permute-start | bytes 491528 | tf_op jit(solution)/shard_map/ppermute | solution.py:48
  10.7 14.7 %collective-permute-start.9 = (bf16[1,128,640]{2,1,0:T(8,128)(2,1)S(1)}, bf16[1,128,640]{2,1,0:T(8,128)(2,1)S(1)}, u32[]{:S(2)}, u32[]{:S(2)}) collective-permute-start(bf16[1,128,640]{2,1,0:T(8,128)(2,1)S(1)} %get-tuple-element.36), channel_id=1, source_target_pairs={{0,4},{4,8},{8,12},{12,16},{16,20},{20,24},{24,28},{28,32},{32,36}... | collective-permute-start | bytes 491528 | tf_op jit(solution)/shard_map/ppermute | solution.py:47
  14.2 3.7 %collective-permute-start.5 = (f32[2,640]{1,0:T(2,128)S(1)}, f32[2,640]{1,0:T(2,128)S(1)}, u32[]{:S(2)}, u32[]{:S(2)}) collective-permute-start(f32[2,640]{1,0:T(2,128)S(1)} %add_add_fusion.2), channel_id=1, source_target_pairs={{0,36},{4,0},{32,4},{36,32},{1,37},{5,1},{33,5},{37,33},{2,38},{6,... | collective-permute-start | bytes 15368 | tf_op jit(solution)/shard_map/ppermute | solution.py:39
  14.3 3.7 %collective-permute-start.4 = (f32[2,640]{1,0:T(2,128)S(1)}, f32[2,640]{1,0:T(2,128)S(1)}, u32[]{:S(2)}, u32[]{:S(2)}) collective-permute-start(f32[2,640]{1,0:T(2,128)S(1)} %add_add_fusion.2), channel_id=1, source_target_pairs={{0,32},{4,36},{32,0},{36,4},{1,33},{5,37},{33,1},{37,5},{2,34},{6,... | collective-permute-start | bytes 15368 | tf_op jit(solution)/shard_map/ppermute | solution.py:39
  16.0 2.7 %collective-permute-start.3 = (f32[2,640]{1,0:T(2,128)S(1)}, f32[2,640]{1,0:T(2,128)S(1)}, u32[]{:S(2)}, u32[]{:S(2)}) collective-permute-start(f32[2,640]{1,0:T(2,128)S(1)} %add_add_fusion.2), channel_id=1, source_target_pairs={{0,4},{4,32},{32,36},{36,0},{1,5},{5,33},{33,37},{37,1},{2,6},{6,3... | collective-permute-start | bytes 15368 | tf_op jit(solution)/shard_map/ppermute | solution.py:39
  18.7 4.4 %collective-permute-start.8 = (f32[2,640]{1,0:T(2,128)S(1)}, f32[2,640]{1,0:T(2,128)S(1)}, u32[]{:S(2)}, u32[]{:S(2)}) collective-permute-start(f32[2,640]{1,0:T(2,128)S(1)} %add_add_fusion.1), channel_id=1, source_target_pairs={{0,192},{64,0},{128,64},{192,128},{1,193},{65,1},{129,65},{193,129... | collective-permute-start | bytes 15368 | tf_op jit(solution)/shard_map/ppermute | solution.py:39
  21.2 4.0 %collective-permute-start.7 = (f32[2,640]{1,0:T(2,128)S(1)}, f32[2,640]{1,0:T(2,128)S(1)}, u32[]{:S(2)}, u32[]{:S(2)}) collective-permute-start(f32[2,640]{1,0:T(2,128)S(1)} %add_add_fusion.1), channel_id=1, source_target_pairs={{0,128},{64,192},{128,0},{192,64},{1,129},{65,193},{129,1},{193,65... | collective-permute-start | bytes 15368 | tf_op jit(solution)/shard_map/ppermute | solution.py:39
  21.7 3.7 %collective-permute-start.6 = (f32[2,640]{1,0:T(2,128)S(1)}, f32[2,640]{1,0:T(2,128)S(1)}, u32[]{:S(2)}, u32[]{:S(2)}) collective-permute-start(f32[2,640]{1,0:T(2,128)S(1)} %add_add_fusion.1), channel_id=1, source_target_pairs={{0,64},{64,128},{128,192},{192,0},{1,65},{65,129},{129,193},{193,1... | collective-permute-start | bytes 15368 | tf_op jit(solution)/shard_map/ppermute | solution.py:39
  48.1 15.3 %collective-permute-start.12 = (bf16[8,320,128]{2,1,0:T(8,128)(2,1)S(1)}, bf16[8,320,128]{2,1,0:T(8,128)(2,1)S(1)}, u32[]{:S(2)}, u32[]{:S(2)}) collective-permute-start(bf16[8,320,128]{2,1,0:T(8,128)(2,1)S(1)} %slice.24.refs_0_.refs_2_), channel_id=1, source_target_pairs={{0,4},{4,0},{8,12},{12,8},{16,20},{20,16},{24,28},{28,24},{1,5},{5... | collective-permute-start | bytes 1966088 | tf_op jit(solution)/shard_map/ppermute | solution.py:319
  53.4 16.3 %collective-permute-start.11 = (bf16[8,320,128]{2,1,0:T(8,128)(2,1)S(1)}, bf16[8,320,128]{2,1,0:T(8,128)(2,1)S(1)}, u32[]{:S(2)}, u32[]{:S(2)}) collective-permute-start(bf16[8,320,128]{2,1,0:T(8,128)(2,1)S(1)} %slice.24.refs_0_.refs_2_), channel_id=1, source_target_pairs={{0,8},{4,28},{8,16},{12,4},{16,24},{20,12},{24,0},{28,20},{1,9},{5... | collective-permute-start | bytes 1966088 | tf_op jit(solution)/shard_map/ppermute | solution.py:320
  63.3 15.4 %collective-permute-start.15 = (bf16[8,320,128]{2,1,0:T(8,128)(2,1)S(1)}, bf16[8,320,128]{2,1,0:T(8,128)(2,1)S(1)}, u32[]{:S(2)}, u32[]{:S(2)}) collective-permute-start(bf16[8,320,128]{2,1,0:T(8,128)(2,1)S(1)} %slice.24.refs_0_.refs_2_), channel_id=1, source_target_pairs={{8,0},{28,4},{16,8},{4,12},{24,16},{12,20},{0,24},{20,28},{9,1},{2... | collective-permute-start | bytes 1966088 | tf_op jit(solution)/shard_map/ppermute | solution.py:323
  69.7 15.4 %collective-permute-start.14 = (bf16[8,320,128]{2,1,0:T(8,128)(2,1)S(1)}, bf16[8,320,128]{2,1,0:T(8,128)(2,1)S(1)}, u32[]{:S(2)}, u32[]{:S(2)}) collective-permute-start(bf16[8,320,128]{2,1,0:T(8,128)(2,1)S(1)} %collective-permute-done.11.refs_0_.refs_4_), channel_id=1, source_target_pairs={{0,4},{4,0},{8,12},{12,8},{16,20},{20,16},{24,28},{28,24},{1,5},{5... | collective-permute-start | bytes 1966088 | tf_op jit(solution)/shard_map/ppermute | solution.py:326
  76.4 15.0 %collective-permute-start.13 = (bf16[8,320,128]{2,1,0:T(8,128)(2,1)S(1)}, bf16[8,320,128]{2,1,0:T(8,128)(2,1)S(1)}, u32[]{:S(2)}, u32[]{:S(2)}) collective-permute-start(bf16[8,320,128]{2,1,0:T(8,128)(2,1)S(1)} %collective-permute-done.11.refs_0_.refs_4_), channel_id=1, source_target_pairs={{0,8},{4,28},{8,16},{12,4},{16,24},{20,12},{24,0},{28,20},{1,9},{5... | collective-permute-start | bytes 1966088 | tf_op jit(solution)/shard_map/ppermute | solution.py:329
  85.0 7.2 %collective-permute-start.17 = (bf16[8,320,128]{2,1,0:T(8,128)(2,1)S(1)}, bf16[8,320,128]{2,1,0:T(8,128)(2,1)S(1)}, u32[]{:S(2)}, u32[]{:S(2)}) collective-permute-start(bf16[8,320,128]{2,1,0:T(8,128)(2,1)S(1)} %collective-permute-done.15.refs_0_.refs_5_), channel_id=1, source_target_pairs={{0,4},{4,0},{8,12},{12,8},{16,20},{20,16},{24,28},{28,24},{1,5},{5... | collective-permute-start | bytes 1966088 | tf_op jit(solution)/shard_map/ppermute | solution.py:332
  91.3 13.0 %collective-permute-start.16 = (bf16[8,320,128]{2,1,0:T(8,128)(2,1)S(1)}, bf16[8,320,128]{2,1,0:T(8,128)(2,1)S(1)}, u32[]{:S(2)}, u32[]{:S(2)}) collective-permute-start(bf16[8,320,128]{2,1,0:T(8,128)(2,1)S(1)} %collective-permute-done.13.refs_1_.refs_8_), channel_id=1, source_target_pairs={{0,4},{4,0},{8,12},{12,8},{16,20},{20,16},{24,28},{28,24},{1,5},{5... | collective-permute-start | bytes 1966088 | tf_op jit(solution)/shard_map/ppermute | solution.py:335

commit v2 on v1

--- a/solution.py
+++ b/solution.py
@@ -19,10 +19,10 @@
 BANDS = NX * NZ * NY * NC
 TILE = 512
 TILES = 4
+PER_TILE = SETS // TILES
+STEPS = 5
 LANES = 128
-Q_ROWS = 256
-KV_ROWS = 320
-SEND_ROWS = Q_ROWS + KV_ROWS
+SEND_ROWS = 576
 BACK_ROWS = 272
 HIGH = 2.0**100
 LOW = 2.0**-60
@@ -153,57 +153,79 @@
     )(sums, vec, before, after, *far)
 
 
-def main_step(kv_ref, pair):
-    lane = lanes(128)
-    keys, values = [], []
-    for src in (2 * pair, 2 * pair + 1):
-        keys += [kv_ref[src, 0:64, :], kv_ref[src, 64:128, :]]
-        value = kv_ref[src, 128:256, :]
-        for side in (value, swap(value)):
-            values.append(jnp.where(lane < 64, side, jnp.ones_like(side)))
-    keys = jnp.concatenate([jnp.concatenate(keys, axis=1), jnp.zeros((64, TILE), BF16)], axis=0)
-    return 0, keys, jnp.concatenate(values, axis=0)
-
-
-def extra_step(kv_ref, block):
-    lane = lanes(64)
-    sources = [SETS * block + src for src in range(SETS)]
-    keys = [kv_ref[src, 256:320, 0:64] for src in sources]
-    values = [kv_ref[src, 256:320, :] for src in sources]
-    values = [jnp.where(lane >= 64, v, jnp.ones_like(v)) for v in values]
-    keys = jnp.concatenate([jnp.zeros((64, TILE), BF16), jnp.concatenate(keys, axis=1)], axis=0)
-    return 1, keys, jnp.concatenate(values, axis=0)
-
-
-def fold_kernel(count, first, last, q_ref, *refs):
-    kv_refs, refs = refs[:count], refs[count:]
+def convert_kernel(got_ref, q_ref, kv_ref):
+    for src in range(SETS):
+        here = slice(256 * src, 256 * src + 256)
+        query = got_ref[src, 0:256, :]
+        q_ref[0, here] = query
+        q_ref[1, here] = swap(query)
+        step, odd = src // 2, src % 2
+        kv_ref[step, 64 * odd : 64 * odd + 64] = got_ref[src, 256:320, :]
+        kv_ref[step, 128 + 64 * odd : 192 + 64 * odd] = got_ref[src, 320:384, :]
+        kv_ref[5 + step, 128 * odd : 128 * odd + 128] = got_ref[src, 384:512, :]
+    for pair in range(SETS // 2):
+        halves = [got_ref[2 * pair + odd, 512:576, 0:64] for odd in range(2)]
+        kv_ref[4, 64 * pair : 64 * pair + 64] = jnp.concatenate(halves, axis=1)
+        halves = [got_ref[pair + 4 * side, 512:576, 64:128] for side in range(2)]
+        kv_ref[9, 64 * pair : 64 * pair + 64] = jnp.concatenate(halves, axis=1)
+
+
+def near(*arrays):
+    return [pltpu.with_memory_space_constraint(a, pltpu.VMEM) for a in arrays]
+
+
+def convert(got):
+    return pl.pallas_call(
+        convert_kernel,
+        in_specs=[pl.BlockSpec(memory_space=pltpu.VMEM)],
+        out_specs=[pl.BlockSpec(memory_space=pltpu.VMEM)] * 2,
+        out_shape=[
+            pltpu.VMEM((2, TILES * TILE, LANES), BF16),
+            pltpu.VMEM((2 * STEPS, 256, LANES), BF16),
+        ],
+        name="convert",
+    )(got)
+
+
+def step_of(kv_ref, step):
+    lane = lanes(256)
+    keys = [kv_ref[step, 64 * i : 64 * i + 64, :] for i in range(4)]
+    value = kv_ref[STEPS + step]
+    values = [jnp.where(lane < 64, side, jnp.ones_like(side)) for side in (value, swap(value))]
+    return jnp.concatenate(keys, axis=1), jnp.concatenate(values, axis=0)
+
+
+def fold_kernel(first, last, q_ref, kv_ref, *refs):
     if not first:
-        acc_in, refs = refs[0], refs[1:]
+        refs = refs[1:]
     if last:
         far_refs, refs = refs[:SETS], refs[SETS:]
     acc_ref = refs[0]
-    acc_ref[0] = jnp.zeros((2, TILE, LANES), F32) if first else acc_in[0]
-    query = q_ref[...].reshape(TILE, LANES)
-
-    steps = []
-    for kv_ref in kv_refs:
-        steps += [functools.partial(main_step, kv_ref, pair) for pair in range(SETS // 2)]
-        steps.append(functools.partial(extra_step, kv_ref, 0))
+    tile = pl.program_id(0)
+    rows = pl.ds(pl.multiple_of(tile * TILE, TILE), TILE)
+
+    def scores(kind, keys):
+        return dot(q_ref[kind, rows, 0:64], keys)
+
     held = None
-    for step in steps + [None]:
+    for step in list(range(STEPS)) + [None]:
         if step is not None:
-            kind, keys, values = step()
-            score = dot(query, keys)
+            kind = step // (STEPS - 1)
+            keys, values = step_of(kv_ref, step)
+            score = scores(kind, keys)
         if held is not None:
-            held_kind, held_score, held_values = held
-            weight = jnp.exp2(held_score).astype(BF16)
-            acc_ref[0, held_kind] += dot(weight, held_values)
-        held = None if step is None else (kind, score, values)
+            held_step, held_kind, held_score, held_values = held
+            update = dot(jnp.exp2(held_score).astype(BF16), held_values)
+            if first and held_step in (0, STEPS - 1):
+                acc_ref[held_kind, rows] = update
+            else:
+                acc_ref[held_kind, rows] += update
+        held = None if step is None else (step, kind, score, values)
 
     if last:
         out_ref, store_ref, top_ref, sems = refs[1:]
-        wide = lanes(TILE)
-        total = jnp.where(wide < 64, acc_ref[0, 1], acc_ref[0, 0])
+        lane = lanes(TILE)
+        total = jnp.where(lane < 64, swap(acc_ref[1, rows]), acc_ref[0, rows])
         good = (jnp.min(total) > LOW) & (jnp.max(total) < HIGH)
         top_ref[...] = jnp.zeros((2, TILE, LANES), F32)
 
@@ -211,39 +233,34 @@
         def _():
             copies = []
             for i, far_ref in enumerate(far_refs):
-                here = store_ref.at[pl.ds(SETS * i, SETS)]
-                copies.append(pltpu.make_async_copy(far_ref, here, sems.at[i]))
+                copies.append(pltpu.make_async_copy(far_ref, store_ref.at[i], sems.at[i]))
                 copies[-1].start()
-            acc_ref[0] = jnp.zeros((2, TILE, LANES), F32)
+            for kind in range(2):
+                acc_ref[kind, rows] = jnp.zeros((TILE, LANES), F32)
             top_ref[...] = jnp.full((2, TILE, LANES), -1e30, F32)
             for copy in copies:
                 copy.wait()
 
-            def online(step):
-                kind, keys, values = step
-                score = dot(query, keys)
+            def body(i, carry):
+                block, step = i // STEPS, i % STEPS
+                kind = step // (STEPS - 1)
+                keys, values = step_of(store_ref.at[block], step)
+                score = scores(kind, keys)
                 top = jnp.maximum(top_ref[kind], jnp.max(score, axis=1, keepdims=True))
                 weight = jnp.exp2(score - top[:, 0:1]).astype(BF16)
                 factor = jnp.exp2(top_ref[kind] - top)
-                acc_ref[0, kind] = acc_ref[0, kind] * factor + dot(weight, values)
+                acc_ref[kind, rows] = acc_ref[kind, rows] * factor + dot(weight, values)
                 top_ref[kind] = top
-
-            def pair_body(pair, carry):
-                online(main_step(store_ref, pair))
                 return carry
 
-            def block_body(block, carry):
-                online(extra_step(store_ref, block))
-                return carry
-
-            lax.fori_loop(0, SETS * SETS // 2, pair_body, 0)
-            lax.fori_loop(0, SETS, block_body, 0)
-
-        main, extra = acc_ref[0, 0], acc_ref[0, 1]
-        out = jnp.where(wide < 64, main / swap(main), extra / swap(extra)).astype(BF16)
-        level = (jnp.log2(extra) + top_ref[1])[:, 0:1]
+            lax.fori_loop(0, SETS * STEPS, body, 0)
+
+        main, extra = acc_ref[0, rows], acc_ref[1, rows]
+        over = swap(extra)
+        out = jnp.where(lane < 64, main / swap(main), over / extra).astype(BF16)
+        level = (jnp.log2(over) + top_ref[1])[:, 0:1]
         row = lax.broadcasted_iota(jnp.int32, (16, LANES), 0)
-        for src in range(2):
+        for src in range(PER_TILE):
             out_ref[src, 0:256] = out[256 * src : 256 * src + 256]
             tail = jnp.zeros((16, LANES), F32)
             for half in range(2):
@@ -256,35 +273,32 @@
             out_ref[src, 256:272] = tail.astype(BF16)
 
 
-def fold(got, blocks, acc, every=None):
+def fold(query, block, acc, every=None):
     first, last = acc is None, every is not None
-    acc_spec = pl.BlockSpec((1, 2, TILE, LANES), lambda t: (t, 0, 0, 0))
-    kv_spec = pl.BlockSpec((SETS, KV_ROWS, LANES), lambda t: (0, 0, 0))
-    out_specs = [acc_spec]
-    out_shape = [jax.ShapeDtypeStruct((TILES, 2, TILE, LANES), F32)]
+    whole = pl.BlockSpec(memory_space=pltpu.VMEM)
+    out_specs = [whole]
+    out_shape = [pltpu.VMEM(query.shape, F32)]
     scratch = []
     if last:
-        out_specs.append(pl.BlockSpec((2, BACK_ROWS, LANES), lambda t: (t, 0, 0)))
+        out_specs.append(pl.BlockSpec((PER_TILE, BACK_ROWS, LANES), lambda t: (t, 0, 0)))
         out_shape.append(jax.ShapeDtypeStruct((SETS, BACK_ROWS, LANES), BF16))
         scratch = [
-            pltpu.VMEM((SETS * SETS, KV_ROWS, LANES), BF16),
+            pltpu.VMEM((SETS,) + block.shape, BF16),
             pltpu.VMEM((2, TILE, LANES), F32),
             pltpu.SemaphoreType.DMA((SETS,)),
         ]
     return pl.pallas_call(
-        functools.partial(fold_kernel, len(blocks), first, last),
+        functools.partial(fold_kernel, first, last),
         grid=(TILES,),
-        in_specs=[pl.BlockSpec((2, Q_ROWS, LANES), lambda t: (t, 0, 0))]
-        + [kv_spec] * len(blocks)
-        + ([] if first else [acc_spec])
+        in_specs=[whole] * (2 if first else 3)
         + ([pl.BlockSpec(memory_space=pl.ANY)] * SETS if last else []),
         out_specs=out_specs,
         out_shape=out_shape,
         scratch_shapes=scratch,
-        input_output_aliases={} if first else {1 + len(blocks): 0},
+        input_output_aliases={} if first else {2: 0},
         compiler_params=VMEM,
         name="fold",
-    )(got, *blocks, *(() if first else (acc,)), *(every or ()))
+    )(*near(query, block, *(() if first else (acc,))), *(every or ()))
 
 
 def on_device(
@@ -309,7 +323,7 @@
     )
 
     got = lax.all_to_all(send, ("x", "z"), 0, 0)
-    own = got[:, Q_ROWS:]
+    query, own = convert(got)
     spots = [(y, c) for y in range(NY) for c in range(NC)]
     along = [(2 * y + c, 2 * ((y + 1 - 2 * c) % NY) + c) for y, c in spots]
     against = [(j, i) for i, j in along]
@@ -318,24 +332,25 @@
     tied = lax.optimization_barrier
     twin = lax.ppermute(own, RING, cross)
     ahead = lax.ppermute(own, RING, along)
-    (acc,) = fold(got, [own], None)
+    (acc,) = fold(query, own, None)
     own, acc = tied((own, acc))
     behind = lax.ppermute(own, RING, against)
-    (acc,) = fold(got, [twin], acc)
+    (acc,) = fold(query, twin, acc)
     ahead, acc = tied((ahead, acc))
     ahead_twin = lax.ppermute(ahead, RING, cross)
-    (acc,) = fold(got, [ahead], acc)
+    (acc,) = fold(query, ahead, acc)
     ahead, acc = tied((ahead, acc))
     far = lax.ppermute(ahead, RING, along)
-    (acc,) = fold(got, [behind], acc)
+    (acc,) = fold(query, behind, acc)
     behind, acc = tied((behind, acc))
     behind_twin = lax.ppermute(behind, RING, cross)
-    (acc,) = fold(got, [ahead_twin], acc)
+    (acc,) = fold(query, ahead_twin, acc)
     far, acc = tied((far, acc))
     far_twin = lax.ppermute(far, RING, cross)
-    (acc,) = fold(got, [behind_twin, far], acc)
+    (acc,) = fold(query, behind_twin, acc)
+    (acc,) = fold(query, far, acc)
     every = [own, twin, ahead, behind, ahead_twin, behind_twin, far, far_twin]
-    unused, out = fold(got, [far_twin], acc, every)
+    unused, out = fold(query, far_twin, acc, every)
 
     back = lax.all_to_all(out, ("x", "z"), 0, 0)
     main = back[:, :256, :64].transpose(1, 0, 2).reshape(tokens, SETS * HEAD_DIM)

time: 257 us -> 254 us (0.988)
  Pallas kernels: 187 us -> 184 us
    pallas_call x7 -> x9, Pallas kernels: 180 us -> 177 us  [the longest x8 176 us: fold(): pl.pallas_call(functools.partial(fold_kernel, first, last), grid=(TILES,)...]
where the time goes in v2:
time: 254 us
  Pallas kernels  184 us (72%)
  starting transfers between devices  31.4 us (12%)
  blocking collectives  29.8 us (12%)
  other arithmetic  3.59 us (1%)
  waiting for transfers between devices  3.02 us (1%)
    pallas_call x8, Pallas kernels, fold(): pl.pallas_call(functools.partial(fold_kernel, first, last), grid=(TILES,)...  176 us
    all_to_all x1, blocking collectives, on_device(): got = lax.all_to_all(send, ('x', 'z'), 0, 0)  16.8 us
    all_to_all x1, blocking collectives, on_device(): back = lax.all_to_all(out, ('x', 'z'), 0, 0)  12.9 us
    ppermute x9, starting transfers between devices, total_of(): parts.append(lax.ppermute(value, axis, perm))  12 us
    pallas_call x1, Pallas kernels, front(): pl.pallas_call(front_kernel, in_specs=[pl.BlockSpec(memory_space=pltpu.VM...  6.88 us
  transfers between devices with their start and end apart: 18, of which 3 were waited for; matrix products, arithmetic and copies ran while one was open for 1% of the time, Pallas kernels for 17%

profile of v2, /device:TPU:1, one launch (start us, length us, event | category | flops | bytes accessed | tf_op | source)
XLA Modules:
  0.0 254.2 jit_solution(9788104305800861869)
XLA Ops:
  0.0 1.1 convert_reduce_fusion
  1.1 0.1 stack.9
  1.2 0.1 stack.10
  1.3 0.2 fusion.1
  1.4 0.1 reshape.44
  1.5 3.6 %collective-permute-start.2 = (f32[2,640]{1,0:T(2,128)S(1)}, f32[2,640]{1,0:T(2,128)S(1)}, u32[]{:S(2)}, u32[]{:S(2)}) collective-permute-start(f32[2,640]{1,0:T(2,128)S(1)} %reshape.44), channel_id=1, source_target_pairs={{0,24},{8,0},{16,8},{24,16},{1,25},{9,1},{17,9},{25,17},{2,26},{10... | collective-permute-start | bytes 15368 | tf_op jit(solution)/shard_map/ppermute | solution.py:39
  5.2 0.3 collective-permute-start.1
  5.5 0.7 collective-permute-start
  6.2 1.0 fusion.15
  7.2 3.4 %collective-permute-start.10 = (bf16[1,128,640]{2,1,0:T(8,128)(2,1)S(1)}, bf16[1,128,640]{2,1,0:T(8,128)(2,1)S(1)}, u32[]{:S(2)}, u32[]{:S(2)}) collective-permute-start(bf16[1,128,640]{2,1,0:T(8,128)(2,1)S(1)} %get-tuple-element.39), channel_id=1, source_target_pairs={{4,0},{8,4},{12,8},{16,12},{20,16},{24,20},{28,24},{32,28},{36,32}... | collective-permute-start | bytes 491528 | tf_op jit(solution)/shard_map/ppermute | solution.py:48
  10.7 3.4 %collective-permute-start.9 = (bf16[1,128,640]{2,1,0:T(8,128)(2,1)S(1)}, bf16[1,128,640]{2,1,0:T(8,128)(2,1)S(1)}, u32[]{:S(2)}, u32[]{:S(2)}) collective-permute-start(bf16[1,128,640]{2,1,0:T(8,128)(2,1)S(1)} %get-tuple-element.40), channel_id=1, source_target_pairs={{0,4},{4,8},{8,12},{12,16},{16,20},{20,24},{24,28},{28,32},{32,36}... | collective-permute-start | bytes 491528 | tf_op jit(solution)/shard_map/ppermute | solution.py:47
  14.1 0.0 collective-permute-done.2
  14.2 0.0 collective-permute-done.1
  14.2 0.0 collective-permute-done
  14.2 0.1 collective-permute-start.5
  14.3 1.7 collective-permute-start.4
  16.0 1.9 collective-permute-start.3
  17.9 0.0 collective-permute-done.5
  17.9 0.0 collective-permute-done.4
  17.9 0.8 collective-permute-done.3
  18.7 2.5 collective-permute-start.8
  21.2 0.5 collective-permute-start.7
  21.7 0.6 collective-permute-start.6
  22.3 0.8 select_select_fusion.vec_ref
  23.1 0.0 collective-permute-done.8
  23.2 2.0 collective-permute-done.7
  25.2 0.2 collective-permute-done.6
  25.4 0.0 collective-permute-done.10.after_ref
  25.4 0.0 collective-permute-done.9.before_ref
  25.4 6.9 %front.1 = (bf16[256,640]{1,0:T(8,128)(2,1)S(1)}, bf16[8,576,128]{2,1,0:T(8,128)(2,1)S(1)}) custom-call(f32[2,640]{1,0:T(2,128)S(1)} %add_add_fusion.sums_ref, f32[8,640]{1,0:T(8,128)S(1)} %select_select_fusion.vec_ref, bf16[1,128,640]{2,1,0:T(8,128)(2,1)S(1)} %collective-permute-done.9.before_ref, ...), custom_call_target="tpu_custom_call" | custom-call | tf_op jit(solution)/shard_map/front/pallas_call | solution.py:135
  32.3 16.8 %all_to_all.10.got_ref = bf16[8,576,128]{2,1,0:T(8,128)(2,1)} all-to-all(bf16[8,576,128]{2,1,0:T(8,128)(2,1)S(1)} %get-tuple-element.21), channel_id=1, replica_groups=mesh['x'=4,'z'=2,'y'=4,'core'=2,'img'=4] {'x','z'}, dimensions={0} | all-to-all | bytes 2359296 | tf_op jit(solution)/shard_map/all_to_all | solution.py:325
  49.1 1.6 convert.9
  50.7 4.7 %collective-permute-start.12 = (bf16[10,256,128]{2,1,0:T(8,128)(2,1)S(1)}, bf16[10,256,128]{2,1,0:T(8,128)(2,1)S(1)}, u32[]{:S(2)}, u32[]{:S(2)}) collective-permute-start(bf16[10,256,128]{2,1,0:T(8,128)(2,1)S(1)} %get-tuple-element.28.kv_ref.refs_1_), channel_id=1, source_target_pairs={{0,4},{4,0},{8,12},{12,8},{16,20},{20,16},{24,28},{28,24},{1,5},{5... | collective-permute-start | bytes 1966088 | tf_op jit(solution)/shard_map/ppermute | solution.py:333
  55.5 4.0 %collective-permute-start.11 = (bf16[10,256,128]{2,1,0:T(8,128)(2,1)S(1)}, bf16[10,256,128]{2,1,0:T(8,128)(2,1)S(1)}, u32[]{:S(2)}, u32[]{:S(2)}) collective-permute-start(bf16[10,256,128]{2,1,0:T(8,128)(2,1)S(1)} %get-tuple-element.28.kv_ref.refs_1_), channel_id=1, source_target_pairs={{0,8},{4,28},{8,16},{12,4},{16,24},{20,12},{24,0},{28,20},{1,9},{5... | collective-permute-start | bytes 1966088 | tf_op jit(solution)/shard_map/ppermute | solution.py:334
  59.5 6.0 %fold.8.refs_0_ = f32[2,2048,128]{2,1,0:T(8,128)S(1)} custom-call(bf16[2,2048,128]{2,1,0:T(8,128)(2,1)S(1)} %get-tuple-element.22.q_ref, bf16[10,256,128]{2,1,0:T(8,128)(2,1)S(1)} %get-tuple-element.28.kv_ref.refs_1_), custom_call_target="tpu_custom_call" | custom-call | tf_op jit(solution)/shard_map/fold/pallas_call | solution.py:290
  65.5 0.1 collective-permute-start.15
  65.6 0.0 collective-permute-done.12.kv_ref.refs_2_
  65.6 6.1 %fold.9.refs_0_ = f32[2,2048,128]{2,1,0:T(8,128)S(1)} custom-call(bf16[2,2048,128]{2,1,0:T(8,128)(2,1)S(1)} %get-tuple-element.22.q_ref, bf16[10,256,128]{2,1,0:T(8,128)(2,1)S(1)} %collective-permute-done.12.kv_ref.refs_2_, f32[2,2048,128]{2,1,0:T(8,128)S(1)} %fold.8.refs_0_), custom_call_target="tpu_custom_call", output_to_operand_aliasing={{}: (2, {})} | custom-call | tf_op jit(solution)/shard_map/fold/pallas_call | solution.py:290
  71.7 0.0 collective-permute-done.11.kv_ref.refs_3_
  71.7 0.4 collective-permute-start.14
  72.2 6.0 %fold.10.refs_0_ = f32[2,2048,128]{2,1,0:T(8,128)S(1)} custom-call(bf16[2,2048,128]{2,1,0:T(8,128)(2,1)S(1)} %get-tuple-element.22.q_ref, bf16[10,256,128]{2,1,0:T(8,128)(2,1)S(1)} %collective-permute-done.11.kv_ref.refs_3_, f32[2,2048,128]{2,1,0:T(8,128)S(1)} %fold.9.refs_0_), custom_call_target="tpu_custom_call", output_to_operand_aliasing={{}: (2, {})} | custom-call | tf_op jit(solution)/shard_map/fold/pallas_call | solution.py:290
  78.2 2.4 collective-permute-start.13
  80.6 0.0 collective-permute-done.15.kv_ref.refs_4_
  80.6 6.0 %fold.11.refs_0_ = f32[2,2048,128]{2,1,0:T(8,128)S(1)} custom-call(bf16[2,2048,128]{2,1,0:T(8,128)(2,1)S(1)} %get-tuple-element.22.q_ref, bf16[10,256,128]{2,1,0:T(8,128)(2,1)S(1)} %collective-permute-done.15.kv_ref.refs_4_, f32[2,2048,128]{2,1,0:T(8,128)S(1)} %fold.10.refs_0_), custom_call_target="tpu_custom_call", output_to_operand_aliasing={{}: (2, {})} | custom-call | tf_op jit(solution)/shard_map/fold/pallas_call | solution.py:290
  86.6 0.1 collective-permute-start.17
  86.7 0.0 collective-permute-done.14.kv_ref.refs_5_
  86.8 6.1 %fold.12.refs_0_ = f32[2,2048,128]{2,1,0:T(8,128)S(1)} custom-call(bf16[2,2048,128]{2,1,0:T(8,128)(2,1)S(1)} %get-tuple-element.22.q_ref, bf16[10,256,128]{2,1,0:T(8,128)(2,1)S(1)} %collective-permute-done.14.kv_ref.refs_5_, f32[2,2048,128]{2,1,0:T(8,128)S(1)} %fold.11.refs_0_), custom_call_target="tpu_custom_call", output_to_operand_aliasing={{}: (2, {})} | custom-call | tf_op jit(solution)/shard_map/fold/pallas_call | solution.py:290
  92.8 0.0 collective-permute-done.13.kv_ref.refs_7_
  92.8 0.8 collective-permute-start.16
  93.6 0.0 collective-permute-done.17.kv_ref.refs_6_
  93.6 6.0 %fold.13.refs_0_ = f32[2,2048,128]{2,1,0:T(8,128)S(1)} custom-call(bf16[2,2048,128]{2,1,0:T(8,128)(2,1)S(1)} %get-tuple-element.22.q_ref, bf16[10,256,128]{2,1,0:T(8,128)(2,1)S(1)} %collective-permute-done.17.kv_ref.refs_6_, f32[2,2048,128]{2,1,0:T(8,128)S(1)} %fold.12.refs_0_), custom_call_target="tpu_custom_call", output_to_operand_aliasing={{}: (2, {})} | custom-call | tf_op jit(solution)/shard_map/fold/pallas_call | solution.py:290
  99.7 6.1 %fold.14.refs_0_ = f32[2,2048,128]{2,1,0:T(8,128)S(1)} custom-call(bf16[2,2048,128]{2,1,0:T(8,128)(2,1)S(1)} %get-tuple-element.22.q_ref, bf16[10,256,128]{2,1,0:T(8,128)(2,1)S(1)} %collective-permute-done.13.kv_ref.refs_7_, f32[2,2048,128]{2,1,0:T(8,128)S(1)} %fold.13.refs_0_), custom_call_target="tpu_custom_call", output_to_operand_aliasing={{}: (2, {})} | custom-call | tf_op jit(solution)/shard_map/fold/pallas_call | solution.py:290
  105.7 0.0 collective-permute-done.16.kv_ref.refs_8_
  105.7 133.2 %fold.15 = (f32[2,2048,128]{2,1,0:T(8,128)S(1)}, bf16[8,272,128]{2,1,0:T(8,128)(2,1)S(1)}) custom-call(bf16[2,2048,128]{2,1,0:T(8,128)(2,1)S(1)} %get-tuple-element.22.q_ref, bf16[10,256,128]{2,1,0:T(8,128)(2,1)S(1)} %collective-permute-done.16.kv_ref.refs_8_, f32[2,2048,128]{2,1,0:T(8,128)S(1)} %fold.14.refs_0_, ...), custom_call_target="tpu_custom_call", output_to_operand_aliasing={{0}: (2, {})} | custom-call | tf_op jit(solution)/shard_map/fold/pallas_call | solution.py:290
  239.0 12.9 %all_to_all.11 = bf16[8,272,128]{2,1,0:T(8,128)(2,1)S(1)} all-to-all(bf16[8,272,128]{2,1,0:T(8,128)(2,1)S(1)} %get-tuple-element.34), channel_id=1, replica_groups=mesh['x'=4,'z'=2,'y'=4,'core'=2,'img'=4] {'x','z'}, dimensions={0} | all-to-all | bytes 1114112 | tf_op jit(solution)/shard_map/all_to_all | solution.py:355
  252.0 0.3 convert_bitcast_fusion
  252.3 0.3 copy.25
  252.6 0.2 copy.27
  252.8 0.3 fusion.5
  253.1 0.1 copy.26
  253.3 0.1 copy.28
  253.4 0.8 fusion.7
  (12 shorter events, 0.1 us)
Async XLA Ops:
  1.5 12.6 %collective-permute-start.2 = (f32[2,640]{1,0:T(2,128)S(1)}, f32[2,640]{1,0:T(2,128)S(1)}, u32[]{:S(2)}, u32[]{:S(2)}) collective-permute-start(f32[2,640]{1,0:T(2,128)S(1)} %reshape.44), channel_id=1, source_target_pairs={{0,24},{8,0},{16,8},{24,16},{1,25},{9,1},{17,9},{25,17},{2,26},{10... | collective-permute-start | bytes 15368 | tf_op jit(solution)/shard_map/ppermute | solution.py:39
  5.2 9.0 %collective-permute-start.1 = (f32[2,640]{1,0:T(2,128)S(1)}, f32[2,640]{1,0:T(2,128)S(1)}, u32[]{:S(2)}, u32[]{:S(2)}) collective-permute-start(f32[2,640]{1,0:T(2,128)S(1)} %reshape.44), channel_id=1, source_target_pairs={{0,16},{8,24},{16,0},{24,8},{1,17},{9,25},{17,1},{25,9},{2,18},{10... | collective-permute-start | bytes 15368 | tf_op jit(solution)/shard_map/ppermute | solution.py:39
  5.5 8.6 %collective-permute-start = (f32[2,640]{1,0:T(2,128)S(1)}, f32[2,640]{1,0:T(2,128)S(1)}, u32[]{:S(2)}, u32[]{:S(2)}) collective-permute-start(f32[2,640]{1,0:T(2,128)S(1)} %reshape.44), channel_id=1, source_target_pairs={{0,8},{8,16},{16,24},{24,0},{1,9},{9,17},{17,25},{25,1},{2,10},{10... | collective-permute-start | bytes 15368 | tf_op jit(solution)/shard_map/ppermute | solution.py:39
  7.2 18.2 %collective-permute-start.10 = (bf16[1,128,640]{2,1,0:T(8,128)(2,1)S(1)}, bf16[1,128,640]{2,1,0:T(8,128)(2,1)S(1)}, u32[]{:S(2)}, u32[]{:S(2)}) collective-permute-start(bf16[1,128,640]{2,1,0:T(8,128)(2,1)S(1)} %get-tuple-element.39), channel_id=1, source_target_pairs={{4,0},{8,4},{12,8},{16,12},{20,16},{24,20},{28,24},{32,28},{36,32}... | collective-permute-start | bytes 491528 | tf_op jit(solution)/shard_map/ppermute | solution.py:48
  10.7 14.7 %collective-permute-start.9 = (bf16[1,128,640]{2,1,0:T(8,128)(2,1)S(1)}, bf16[1,128,640]{2,1,0:T(8,128)(2,1)S(1)}, u32[]{:S(2)}, u32[]{:S(2)}) collective-permute-start(bf16[1,128,640]{2,1,0:T(8,128)(2,1)S(1)} %get-tuple-element.40), channel_id=1, source_target_pairs={{0,4},{4,8},{8,12},{12,16},{16,20},{20,24},{24,28},{28,32},{32,36}... | collective-permute-start | bytes 491528 | tf_op jit(solution)/shard_map/ppermute | solution.py:47
  14.2 3.7 %collective-permute-start.5 = (f32[2,640]{1,0:T(2,128)S(1)}, f32[2,640]{1,0:T(2,128)S(1)}, u32[]{:S(2)}, u32[]{:S(2)}) collective-permute-start(f32[2,640]{1,0:T(2,128)S(1)} %add_add_fusion.2), channel_id=1, source_target_pairs={{0,36},{4,0},{32,4},{36,32},{1,37},{5,1},{33,5},{37,33},{2,38},{6,... | collective-permute-start | bytes 15368 | tf_op jit(solution)/shard_map/ppermute | solution.py:39
  14.3 3.7 %collective-permute-start.4 = (f32[2,640]{1,0:T(2,128)S(1)}, f32[2,640]{1,0:T(2,128)S(1)}, u32[]{:S(2)}, u32[]{:S(2)}) collective-permute-start(f32[2,640]{1,0:T(2,128)S(1)} %add_add_fusion.2), channel_id=1, source_target_pairs={{0,32},{4,36},{32,0},{36,4},{1,33},{5,37},{33,1},{37,5},{2,34},{6,... | collective-permute-start | bytes 15368 | tf_op jit(solution)/shard_map/ppermute | solution.py:39
  16.0 2.7 %collective-permute-start.3 = (f32[2,640]{1,0:T(2,128)S(1)}, f32[2,640]{1,0:T(2,128)S(1)}, u32[]{:S(2)}, u32[]{:S(2)}) collective-permute-start(f32[2,640]{1,0:T(2,128)S(1)} %add_add_fusion.2), channel_id=1, source_target_pairs={{0,4},{4,32},{32,36},{36,0},{1,5},{5,33},{33,37},{37,1},{2,6},{6,3... | collective-permute-start | bytes 15368 | tf_op jit(solution)/shard_map/ppermute | solution.py:39
  18.7 4.4 %collective-permute-start.8 = (f32[2,640]{1,0:T(2,128)S(1)}, f32[2,640]{1,0:T(2,128)S(1)}, u32[]{:S(2)}, u32[]{:S(2)}) collective-permute-start(f32[2,640]{1,0:T(2,128)S(1)} %add_add_fusion.1), channel_id=1, source_target_pairs={{0,192},{64,0},{128,64},{192,128},{1,193},{65,1},{129,65},{193,129... | collective-permute-start | bytes 15368 | tf_op jit(solution)/shard_map/ppermute | solution.py:39
  21.2 4.0 %collective-permute-start.7 = (f32[2,640]{1,0:T(2,128)S(1)}, f32[2,640]{1,0:T(2,128)S(1)}, u32[]{:S(2)}, u32[]{:S(2)}) collective-permute-start(f32[2,640]{1,0:T(2,128)S(1)} %add_add_fusion.1), channel_id=1, source_target_pairs={{0,128},{64,192},{128,0},{192,64},{1,129},{65,193},{129,1},{193,65... | collective-permute-start | bytes 15368 | tf_op jit(solution)/shard_map/ppermute | solution.py:39
  21.7 3.7 %collective-permute-start.6 = (f32[2,640]{1,0:T(2,128)S(1)}, f32[2,640]{1,0:T(2,128)S(1)}, u32[]{:S(2)}, u32[]{:S(2)}) collective-permute-start(f32[2,640]{1,0:T(2,128)S(1)} %add_add_fusion.1), channel_id=1, source_target_pairs={{0,64},{64,128},{128,192},{192,0},{1,65},{65,129},{129,193},{193,1... | collective-permute-start | bytes 15368 | tf_op jit(solution)/shard_map/ppermute | solution.py:39
  50.7 14.9 %collective-permute-start.12 = (bf16[10,256,128]{2,1,0:T(8,128)(2,1)S(1)}, bf16[10,256,128]{2,1,0:T(8,128)(2,1)S(1)}, u32[]{:S(2)}, u32[]{:S(2)}) collective-permute-start(bf16[10,256,128]{2,1,0:T(8,128)(2,1)S(1)} %get-tuple-element.28.kv_ref.refs_1_), channel_id=1, source_target_pairs={{0,4},{4,0},{8,12},{12,8},{16,20},{20,16},{24,28},{28,24},{1,5},{5... | collective-permute-start | bytes 1966088 | tf_op jit(solution)/shard_map/ppermute | solution.py:333
  55.5 16.2 %collective-permute-start.11 = (bf16[10,256,128]{2,1,0:T(8,128)(2,1)S(1)}, bf16[10,256,128]{2,1,0:T(8,128)(2,1)S(1)}, u32[]{:S(2)}, u32[]{:S(2)}) collective-permute-start(bf16[10,256,128]{2,1,0:T(8,128)(2,1)S(1)} %get-tuple-element.28.kv_ref.refs_1_), channel_id=1, source_target_pairs={{0,8},{4,28},{8,16},{12,4},{16,24},{20,12},{24,0},{28,20},{1,9},{5... | collective-permute-start | bytes 1966088 | tf_op jit(solution)/shard_map/ppermute | solution.py:334
  65.5 15.1 %collective-permute-start.15 = (bf16[10,256,128]{2,1,0:T(8,128)(2,1)S(1)}, bf16[10,256,128]{2,1,0:T(8,128)(2,1)S(1)}, u32[]{:S(2)}, u32[]{:S(2)}) collective-permute-start(bf16[10,256,128]{2,1,0:T(8,128)(2,1)S(1)} %get-tuple-element.28.kv_ref.refs_1_), channel_id=1, source_target_pairs={{8,0},{28,4},{16,8},{4,12},{24,16},{12,20},{0,24},{20,28},{9,1},{2... | collective-permute-start | bytes 1966088 | tf_op jit(solution)/shard_map/ppermute | solution.py:337
  71.7 15.0 %collective-permute-start.14 = (bf16[10,256,128]{2,1,0:T(8,128)(2,1)S(1)}, bf16[10,256,128]{2,1,0:T(8,128)(2,1)S(1)}, u32[]{:S(2)}, u32[]{:S(2)}) collective-permute-start(bf16[10,256,128]{2,1,0:T(8,128)(2,1)S(1)} %collective-permute-done.11.kv_ref.refs_3_), channel_id=1, source_target_pairs={{0,4},{4,0},{8,12},{12,8},{16,20},{20,16},{24,28},{28,24},{1,5},{5... | collective-permute-start | bytes 1966088 | tf_op jit(solution)/shard_map/ppermute | solution.py:340
  78.2 14.6 %collective-permute-start.13 = (bf16[10,256,128]{2,1,0:T(8,128)(2,1)S(1)}, bf16[10,256,128]{2,1,0:T(8,128)(2,1)S(1)}, u32[]{:S(2)}, u32[]{:S(2)}) collective-permute-start(bf16[10,256,128]{2,1,0:T(8,128)(2,1)S(1)} %collective-permute-done.11.kv_ref.refs_3_), channel_id=1, source_target_pairs={{0,8},{4,28},{8,16},{12,4},{16,24},{20,12},{24,0},{28,20},{1,9},{5... | collective-permute-start | bytes 1966088 | tf_op jit(solution)/shard_map/ppermute | solution.py:343
  86.6 7.0 %collective-permute-start.17 = (bf16[10,256,128]{2,1,0:T(8,128)(2,1)S(1)}, bf16[10,256,128]{2,1,0:T(8,128)(2,1)S(1)}, u32[]{:S(2)}, u32[]{:S(2)}) collective-permute-start(bf16[10,256,128]{2,1,0:T(8,128)(2,1)S(1)} %collective-permute-done.15.kv_ref.refs_4_), channel_id=1, source_target_pairs={{0,4},{4,0},{8,12},{12,8},{16,20},{20,16},{24,28},{28,24},{1,5},{5... | collective-permute-start | bytes 1966088 | tf_op jit(solution)/shard_map/ppermute | solution.py:346
  92.8 12.9 %collective-permute-start.16 = (bf16[10,256,128]{2,1,0:T(8,128)(2,1)S(1)}, bf16[10,256,128]{2,1,0:T(8,128)(2,1)S(1)}, u32[]{:S(2)}, u32[]{:S(2)}) collective-permute-start(bf16[10,256,128]{2,1,0:T(8,128)(2,1)S(1)} %collective-permute-done.13.kv_ref.refs_7_), channel_id=1, source_target_pairs={{0,4},{4,0},{8,12},{12,8},{16,20},{20,16},{24,28},{28,24},{1,5},{5... | collective-permute-start | bytes 1966088 | tf_op jit(solution)/shard_map/ppermute | solution.py:349

commit v3 on v1

--- a/solution.py
+++ b/solution.py
@@ -41,11 +41,11 @@
     return value
 
 
-def halo(latent):
+def halo(last, first):
     up = [(i, i + 1) for i in range(BANDS - 1)]
     down = [(j, i) for i, j in up]
-    before = lax.ppermute(latent[-1:], BAND, up)
-    after = lax.ppermute(latent[:1], BAND, down)
+    before = lax.ppermute(last, BAND, up)
+    after = lax.ppermute(first, BAND, down)
     return before, after
 
 
@@ -240,7 +240,8 @@
             lax.fori_loop(0, SETS, block_body, 0)
 
         main, extra = acc_ref[0, 0], acc_ref[0, 1]
-        out = jnp.where(wide < 64, main / swap(main), extra / swap(extra)).astype(BF16)
+        out = jnp.where(wide < 64, main, extra) / jnp.where(wide < 64, swap(main), swap(extra))
+        out = out.astype(BF16)
         level = (jnp.log2(extra) + top_ref[1])[:, 0:1]
         row = lax.broadcasted_iota(jnp.int32, (16, LANES), 0)
         for src in range(2):
@@ -293,8 +294,9 @@
     rows_here, cols, chans = latent.shape
     tokens = rows_here * cols
     width = chans // GROUPS
-    before, after = halo(latent)
-    flat = latent.astype(F32).reshape(-1, chans)
+    edges = lax.optimization_barrier((latent[-1:], latent[:1], latent))
+    before, after = halo(*edges[:2])
+    flat = edges[2].astype(F32).reshape(-1, chans)
     sums = jnp.stack([jnp.sum(flat, axis=0), jnp.sum(flat * flat, axis=0)])
     sums = jnp.sum(sums.reshape(2, GROUPS, width), axis=2, keepdims=True)
     sums = total_of(jnp.broadcast_to(sums, (2, GROUPS, width)).reshape(2, chans))

time: 257 us -> 257 us (level)
  starting transfers between devices: 31.8 us -> 27.2 us
    ppermute x1, starting transfers between devices: 3.88 us -> 0.01 us  [on_device(): ahead = lax.ppermute(own, RING, along)]
  transfers between devices with their start and end apart: 18 -> 18, of which waited for: 3 -> 3; matrix products, arithmetic and copies ran while one was open for 1% -> 0% of each run, Pallas kernels for 17% -> 17%
where the time goes in v3:
time: 257 us; the launch traced here: 256 us
  Pallas kernels  187 us (73%)
  blocking collectives  31.1 us (12%)
  starting transfers between devices  27.2 us (11%)
  waiting for transfers between devices  5.32 us (2%)
  other arithmetic  3.6 us (1%)
    pallas_call x7, Pallas kernels, fold(): pl.pallas_call(functools.partial(fold_kernel, len(blocks), first, last),...  180 us
    all_to_all x1, blocking collectives, on_device(): got = lax.all_to_all(send, ('x', 'z'), 0, 0)  18.1 us
    all_to_all x1, blocking collectives, on_device(): back = lax.all_to_all(out, ('x', 'z'), 0, 0)  12.9 us
    ppermute x9, starting transfers between devices, total_of(): parts.append(lax.ppermute(value, axis, perm))  12.5 us
    pallas_call x1, Pallas kernels, front(): pl.pallas_call(front_kernel, in_specs=[pl.BlockSpec(memory_space=pltpu.VM...  6.88 us
    ppermute x9, waiting for transfers between devices, total_of(): parts.append(lax.ppermute(value, axis, perm))  5.3 us
  transfers between devices with their start and end apart: 18, of which 3 were waited for; matrix products, arithmetic and copies ran while one was open for 0% of the time, Pallas kernels for 17%

profile of v3, /device:TPU:1, one launch (start us, length us, event | category | flops | bytes accessed | tf_op | source)
XLA Modules:
  0.0 256.4 jit_solution(2795959681655298625)
XLA Ops:
  0.0 1.0 fusion.15
  1.0 1.1 convert_reduce_fusion
  2.1 0.1 stack.9
  2.2 0.1 stack.10
  2.3 0.2 fusion.1
  2.5 0.1 reshape.44
  2.6 3.6 %collective-permute-start.2 = (f32[2,640]{1,0:T(2,128)S(1)}, f32[2,640]{1,0:T(2,128)S(1)}, u32[]{:S(2)}, u32[]{:S(2)}) collective-permute-start(f32[2,640]{1,0:T(2,128)S(1)} %reshape.44), channel_id=1, source_target_pairs={{0,24},{8,0},{16,8},{24,16},{1,25},{9,1},{17,9},{25,17},{2,26},{10... | collective-permute-start | bytes 15368 | tf_op jit(solution)/shard_map/ppermute | solution.py:39
  6.2 0.3 collective-permute-start.1
  6.6 0.7 collective-permute-start
  7.2 4.9 %collective-permute-start.9 = (bf16[1,128,640]{2,1,0:T(8,128)(2,1)S(1)}, bf16[1,128,640]{2,1,0:T(8,128)(2,1)S(1)}, u32[]{:S(2)}, u32[]{:S(2)}) collective-permute-start(bf16[1,128,640]{2,1,0:T(8,128)(2,1)S(1)} %get-tuple-element.22), channel_id=1, source_target_pairs={{0,4},{4,8},{8,12},{12,16},{16,20},{20,24},{24,28},{28,32},{32,36}... | collective-permute-start | bytes 491528 | tf_op jit(solution)/shard_map/ppermute | solution.py:47
  12.2 1.9 collective-permute-start.10
  14.1 0.0 collective-permute-done.2
  14.1 0.0 collective-permute-done.1
  14.2 0.0 collective-permute-done
  14.2 0.1 collective-permute-start.5
  14.3 4.0 %collective-permute-start.4 = (f32[2,640]{1,0:T(2,128)S(1)}, f32[2,640]{1,0:T(2,128)S(1)}, u32[]{:S(2)}, u32[]{:S(2)}) collective-permute-start(f32[2,640]{1,0:T(2,128)S(1)} %add_add_fusion.2), channel_id=1, source_target_pairs={{0,32},{4,36},{32,0},{36,4},{1,33},{5,37},{33,1},{37,5},{2,34},{6,... | collective-permute-start | bytes 15368 | tf_op jit(solution)/shard_map/ppermute | solution.py:39
  18.3 0.1 collective-permute-start.3
  18.3 3.1 %collective-permute-done.5 = f32[2,640]{1,0:T(2,128)S(1)} collective-permute-done((f32[2,640]{1,0:T(2,128)S(1)}, f32[2,640]{1,0:T(2,128)S(1)}, u32[]{:S(2)}, u32[]{:S(2)}) %collective-permute-start.5) | collective-permute-done | bytes 5152 | tf_op jit(solution)/shard_map/ppermute | solution.py:39
  21.4 0.0 collective-permute-done.4
  21.4 0.0 collective-permute-done.3
  21.4 2.6 collective-permute-start.8
  24.0 0.5 collective-permute-start.7
  24.5 0.6 collective-permute-start.6
  25.1 0.8 select_select_fusion.vec_ref
  25.9 0.0 collective-permute-done.8
  25.9 2.0 collective-permute-done.7
  27.9 0.2 collective-permute-done.6
  28.2 0.0 collective-permute-done.9.before_ref
  28.2 0.0 collective-permute-done.10.after_ref
  28.2 6.9 %front.1 = (bf16[256,640]{1,0:T(8,128)(2,1)S(1)}, bf16[8,576,128]{2,1,0:T(8,128)(2,1)S(1)}) custom-call(f32[2,640]{1,0:T(2,128)S(1)} %add_add_fusion.sums_ref, f32[8,640]{1,0:T(8,128)S(1)} %select_select_fusion.vec_ref, bf16[1,128,640]{2,1,0:T(8,128)(2,1)S(1)} %collective-permute-done.9.before_ref, ...), custom_call_target="tpu_custom_call" | custom-call | tf_op jit(solution)/shard_map/front/pallas_call | solution.py:135
  35.1 18.1 %all_to_all.10.q_ref = bf16[8,576,128]{2,1,0:T(8,128)(2,1)S(1)} all-to-all(bf16[8,576,128]{2,1,0:T(8,128)(2,1)S(1)} %get-tuple-element.25), channel_id=1, replica_groups=mesh['x'=4,'z'=2,'y'=4,'core'=2,'img'=4] {'x','z'}, dimensions={0} | all-to-all | bytes 2359296 | tf_op jit(solution)/shard_map/all_to_all | solution.py:313
  53.3 3.4 %collective-permute-start.12 = (bf16[8,320,128]{2,1,0:T(8,128)(2,1)S(1)}, bf16[8,320,128]{2,1,0:T(8,128)(2,1)S(1)}, u32[]{:S(2)}, u32[]{:S(2)}) collective-permute-start(bf16[8,320,128]{2,1,0:T(8,128)(2,1)S(1)} %slice.24.refs_0_.refs_2_), channel_id=1, source_target_pairs={{0,4},{4,0},{8,12},{12,8},{16,20},{20,16},{24,28},{28,24},{1,5},{5... | collective-permute-start | bytes 1966088 | tf_op jit(solution)/shard_map/ppermute | solution.py:321
  56.6 0.0 collective-permute-start.11
  56.6 6.1 %fold.7.refs_1_ = f32[4,2,512,128]{3,2,1,0:T(8,128)S(1)} custom-call(bf16[8,576,128]{2,1,0:T(8,128)(2,1)S(1)} %all_to_all.10.q_ref, bf16[8,320,128]{2,1,0:T(8,128)(2,1)S(1)} %slice.24.refs_0_.refs_2_), custom_call_target="tpu_custom_call" | custom-call | tf_op jit(solution)/shard_map/fold/pallas_call | solution.py:275
  62.7 1.5 collective-permute-start.15
  64.3 0.0 collective-permute-done.12.refs_0_.refs_3_
  64.3 6.2 %fold.8.refs_1_ = f32[4,2,512,128]{3,2,1,0:T(8,128)S(1)} custom-call(bf16[8,576,128]{2,1,0:T(8,128)(2,1)S(1)} %all_to_all.10.q_ref, bf16[8,320,128]{2,1,0:T(8,128)(2,1)S(1)} %collective-permute-done.12.refs_0_.refs_3_, f32[4,2,512,128]{3,2,1,0:T(8,128)S(1)} %fold.7.refs_1_), custom_call_target="tpu_custom_call", output_to_operand_aliasing={{}: (2, {})} | custom-call | tf_op jit(solution)/shard_map/fold/pallas_call | solution.py:275
  70.5 0.0 collective-permute-done.11.refs_0_.refs_4_
  70.5 1.9 collective-permute-start.14
  72.5 6.2 %fold.9.refs_1_ = f32[4,2,512,128]{3,2,1,0:T(8,128)S(1)} custom-call(bf16[8,576,128]{2,1,0:T(8,128)(2,1)S(1)} %all_to_all.10.q_ref, bf16[8,320,128]{2,1,0:T(8,128)(2,1)S(1)} %collective-permute-done.11.refs_0_.refs_4_, f32[4,2,512,128]{3,2,1,0:T(8,128)S(1)} %fold.8.refs_1_), custom_call_target="tpu_custom_call", output_to_operand_aliasing={{}: (2, {})} | custom-call | tf_op jit(solution)/shard_map/fold/pallas_call | solution.py:275
  78.7 0.1 collective-permute-start.13
  78.8 0.0 collective-permute-done.15.refs_0_.refs_5_
  78.8 6.2 %fold.10.refs_1_ = f32[4,2,512,128]{3,2,1,0:T(8,128)S(1)} custom-call(bf16[8,576,128]{2,1,0:T(8,128)(2,1)S(1)} %all_to_all.10.q_ref, bf16[8,320,128]{2,1,0:T(8,128)(2,1)S(1)} %collective-permute-done.15.refs_0_.refs_5_, f32[4,2,512,128]{3,2,1,0:T(8,128)S(1)} %fold.9.refs_1_), custom_call_target="tpu_custom_call", output_to_operand_aliasing={{}: (2, {})} | custom-call | tf_op jit(solution)/shard_map/fold/pallas_call | solution.py:275
  85.0 0.1 collective-permute-start.17
  85.1 0.0 collective-permute-done.14.refs_0_.refs_6_
  85.1 6.2 %fold.11.refs_2_ = f32[4,2,512,128]{3,2,1,0:T(8,128)S(1)} custom-call(bf16[8,576,128]{2,1,0:T(8,128)(2,1)S(1)} %all_to_all.10.q_ref, bf16[8,320,128]{2,1,0:T(8,128)(2,1)S(1)} %collective-permute-done.14.refs_0_.refs_6_, f32[4,2,512,128]{3,2,1,0:T(8,128)S(1)} %fold.10.refs_1_), custom_call_target="tpu_custom_call", output_to_operand_aliasing={{}: (2, {})} | custom-call | tf_op jit(solution)/shard_map/fold/pallas_call | solution.py:275
  91.4 0.0 collective-permute-done.13.refs_1_.refs_8_
  91.4 0.8 collective-permute-start.16
  92.2 0.0 collective-permute-done.17.refs_0_.refs_7_
  92.2 12.2 %fold.12.refs_1_ = f32[4,2,512,128]{3,2,1,0:T(8,128)S(1)} custom-call(bf16[8,576,128]{2,1,0:T(8,128)(2,1)S(1)} %all_to_all.10.q_ref, bf16[8,320,128]{2,1,0:T(8,128)(2,1)S(1)} %collective-permute-done.17.refs_0_.refs_7_, bf16[8,320,128]{2,1,0:T(8,128)(2,1)S(1)} %collective-permute-done.13.refs_1_.refs_8_, ...), custom_call_target="tpu_custom_call", output_to_operand_aliasing={{}: (3, {})} | custom-call | tf_op jit(solution)/shard_map/fold/pallas_call | solution.py:275
  104.4 0.0 collective-permute-done.16.refs_0_.refs_9_
  104.4 136.8 %fold.13 = (f32[4,2,512,128]{3,2,1,0:T(8,128)S(1)}, bf16[8,272,128]{2,1,0:T(8,128)(2,1)S(1)}) custom-call(bf16[8,576,128]{2,1,0:T(8,128)(2,1)S(1)} %all_to_all.10.q_ref, bf16[8,320,128]{2,1,0:T(8,128)(2,1)S(1)} %collective-permute-done.16.refs_0_.refs_9_, f32[4,2,512,128]{3,2,1,0:T(8,128)S(1)} %fold.12.refs_1_, ...), custom_call_target="tpu_custom_call", output_to_operand_aliasing={{0}: (2, {})} | custom-call | tf_op jit(solution)/shard_map/fold/pallas_call | solution.py:275
  241.2 12.9 %all_to_all.11 = bf16[8,272,128]{2,1,0:T(8,128)(2,1)S(1)} all-to-all(bf16[8,272,128]{2,1,0:T(8,128)(2,1)S(1)} %get-tuple-element.36), channel_id=1, replica_groups=mesh['x'=4,'z'=2,'y'=4,'core'=2,'img'=4] {'x','z'}, dimensions={0} | all-to-all | bytes 1114112 | tf_op jit(solution)/shard_map/all_to_all | solution.py:342
  254.2 0.3 convert_bitcast_fusion
  254.5 0.3 copy.24
  254.8 0.2 copy.26
  255.0 0.3 fusion.5
  255.3 0.1 copy.25
  255.5 0.1 copy.27
  255.6 0.8 fusion.7
  (13 shorter events, 0.2 us)
Async XLA Ops:
  2.6 11.6 %collective-permute-start.2 = (f32[2,640]{1,0:T(2,128)S(1)}, f32[2,640]{1,0:T(2,128)S(1)}, u32[]{:S(2)}, u32[]{:S(2)}) collective-permute-start(f32[2,640]{1,0:T(2,128)S(1)} %reshape.44), channel_id=1, source_target_pairs={{0,24},{8,0},{16,8},{24,16},{1,25},{9,1},{17,9},{25,17},{2,26},{10... | collective-permute-start | bytes 15368 | tf_op jit(solution)/shard_map/ppermute | solution.py:39
  6.2 7.9 %collective-permute-start.1 = (f32[2,640]{1,0:T(2,128)S(1)}, f32[2,640]{1,0:T(2,128)S(1)}, u32[]{:S(2)}, u32[]{:S(2)}) collective-permute-start(f32[2,640]{1,0:T(2,128)S(1)} %reshape.44), channel_id=1, source_target_pairs={{0,16},{8,24},{16,0},{24,8},{1,17},{9,25},{17,1},{25,9},{2,18},{10... | collective-permute-start | bytes 15368 | tf_op jit(solution)/shard_map/ppermute | solution.py:39
  6.6 7.6 %collective-permute-start = (f32[2,640]{1,0:T(2,128)S(1)}, f32[2,640]{1,0:T(2,128)S(1)}, u32[]{:S(2)}, u32[]{:S(2)}) collective-permute-start(f32[2,640]{1,0:T(2,128)S(1)} %reshape.44), channel_id=1, source_target_pairs={{0,8},{8,16},{16,24},{24,0},{1,9},{9,17},{17,25},{25,1},{2,10},{10... | collective-permute-start | bytes 15368 | tf_op jit(solution)/shard_map/ppermute | solution.py:39
  7.2 20.9 %collective-permute-start.9 = (bf16[1,128,640]{2,1,0:T(8,128)(2,1)S(1)}, bf16[1,128,640]{2,1,0:T(8,128)(2,1)S(1)}, u32[]{:S(2)}, u32[]{:S(2)}) collective-permute-start(bf16[1,128,640]{2,1,0:T(8,128)(2,1)S(1)} %get-tuple-element.22), channel_id=1, source_target_pairs={{0,4},{4,8},{8,12},{12,16},{16,20},{20,24},{24,28},{28,32},{32,36}... | collective-permute-start | bytes 491528 | tf_op jit(solution)/shard_map/ppermute | solution.py:47
  12.2 16.0 %collective-permute-start.10 = (bf16[1,128,640]{2,1,0:T(8,128)(2,1)S(1)}, bf16[1,128,640]{2,1,0:T(8,128)(2,1)S(1)}, u32[]{:S(2)}, u32[]{:S(2)}) collective-permute-start(bf16[1,128,640]{2,1,0:T(8,128)(2,1)S(1)} %get-tuple-element.23), channel_id=1, source_target_pairs={{4,0},{8,4},{12,8},{16,12},{20,16},{24,20},{28,24},{32,28},{36,32}... | collective-permute-start | bytes 491528 | tf_op jit(solution)/shard_map/ppermute | solution.py:48
  14.2 7.2 %collective-permute-start.5 = (f32[2,640]{1,0:T(2,128)S(1)}, f32[2,640]{1,0:T(2,128)S(1)}, u32[]{:S(2)}, u32[]{:S(2)}) collective-permute-start(f32[2,640]{1,0:T(2,128)S(1)} %add_add_fusion.2), channel_id=1, source_target_pairs={{0,36},{4,0},{32,4},{36,32},{1,37},{5,1},{33,5},{37,33},{2,38},{6,... | collective-permute-start | bytes 15368 | tf_op jit(solution)/shard_map/ppermute | solution.py:39
  14.3 7.1 %collective-permute-start.4 = (f32[2,640]{1,0:T(2,128)S(1)}, f32[2,640]{1,0:T(2,128)S(1)}, u32[]{:S(2)}, u32[]{:S(2)}) collective-permute-start(f32[2,640]{1,0:T(2,128)S(1)} %add_add_fusion.2), channel_id=1, source_target_pairs={{0,32},{4,36},{32,0},{36,4},{1,33},{5,37},{33,1},{37,5},{2,34},{6,... | collective-permute-start | bytes 15368 | tf_op jit(solution)/shard_map/ppermute | solution.py:39
  18.3 3.1 %collective-permute-start.3 = (f32[2,640]{1,0:T(2,128)S(1)}, f32[2,640]{1,0:T(2,128)S(1)}, u32[]{:S(2)}, u32[]{:S(2)}) collective-permute-start(f32[2,640]{1,0:T(2,128)S(1)} %add_add_fusion.2), channel_id=1, source_target_pairs={{0,4},{4,32},{32,36},{36,0},{1,5},{5,33},{33,37},{37,1},{2,6},{6,3... | collective-permute-start | bytes 15368 | tf_op jit(solution)/shard_map/ppermute | solution.py:39
  21.4 4.5 %collective-permute-start.8 = (f32[2,640]{1,0:T(2,128)S(1)}, f32[2,640]{1,0:T(2,128)S(1)}, u32[]{:S(2)}, u32[]{:S(2)}) collective-permute-start(f32[2,640]{1,0:T(2,128)S(1)} %add_add_fusion.1), channel_id=1, source_target_pairs={{0,192},{64,0},{128,64},{192,128},{1,193},{65,1},{129,65},{193,129... | collective-permute-start | bytes 15368 | tf_op jit(solution)/shard_map/ppermute | solution.py:39
  24.0 4.0 %collective-permute-start.7 = (f32[2,640]{1,0:T(2,128)S(1)}, f32[2,640]{1,0:T(2,128)S(1)}, u32[]{:S(2)}, u32[]{:S(2)}) collective-permute-start(f32[2,640]{1,0:T(2,128)S(1)} %add_add_fusion.1), channel_id=1, source_target_pairs={{0,128},{64,192},{128,0},{192,64},{1,129},{65,193},{129,1},{193,65... | collective-permute-start | bytes 15368 | tf_op jit(solution)/shard_map/ppermute | solution.py:39
  24.5 3.7 %collective-permute-start.6 = (f32[2,640]{1,0:T(2,128)S(1)}, f32[2,640]{1,0:T(2,128)S(1)}, u32[]{:S(2)}, u32[]{:S(2)}) collective-permute-start(f32[2,640]{1,0:T(2,128)S(1)} %add_add_fusion.1), channel_id=1, source_target_pairs={{0,64},{64,128},{128,192},{192,0},{1,65},{65,129},{129,193},{193,1... | collective-permute-start | bytes 15368 | tf_op jit(solution)/shard_map/ppermute | solution.py:39
  53.3 11.0 %collective-permute-start.12 = (bf16[8,320,128]{2,1,0:T(8,128)(2,1)S(1)}, bf16[8,320,128]{2,1,0:T(8,128)(2,1)S(1)}, u32[]{:S(2)}, u32[]{:S(2)}) collective-permute-start(bf16[8,320,128]{2,1,0:T(8,128)(2,1)S(1)} %slice.24.refs_0_.refs_2_), channel_id=1, source_target_pairs={{0,4},{4,0},{8,12},{12,8},{16,20},{20,16},{24,28},{28,24},{1,5},{5... | collective-permute-start | bytes 1966088 | tf_op jit(solution)/shard_map/ppermute | solution.py:321
  56.6 13.9 %collective-permute-start.11 = (bf16[8,320,128]{2,1,0:T(8,128)(2,1)S(1)}, bf16[8,320,128]{2,1,0:T(8,128)(2,1)S(1)}, u32[]{:S(2)}, u32[]{:S(2)}) collective-permute-start(bf16[8,320,128]{2,1,0:T(8,128)(2,1)S(1)} %slice.24.refs_0_.refs_2_), channel_id=1, source_target_pairs={{0,8},{4,28},{8,16},{12,4},{16,24},{20,12},{24,0},{28,20},{1,9},{5... | collective-permute-start | bytes 1966088 | tf_op jit(solution)/shard_map/ppermute | solution.py:322
  62.7 16.0 %collective-permute-start.15 = (bf16[8,320,128]{2,1,0:T(8,128)(2,1)S(1)}, bf16[8,320,128]{2,1,0:T(8,128)(2,1)S(1)}, u32[]{:S(2)}, u32[]{:S(2)}) collective-permute-start(bf16[8,320,128]{2,1,0:T(8,128)(2,1)S(1)} %slice.24.refs_0_.refs_2_), channel_id=1, source_target_pairs={{8,0},{28,4},{16,8},{4,12},{24,16},{12,20},{0,24},{20,28},{9,1},{2... | collective-permute-start | bytes 1966088 | tf_op jit(solution)/shard_map/ppermute | solution.py:325
  70.5 14.6 %collective-permute-start.14 = (bf16[8,320,128]{2,1,0:T(8,128)(2,1)S(1)}, bf16[8,320,128]{2,1,0:T(8,128)(2,1)S(1)}, u32[]{:S(2)}, u32[]{:S(2)}) collective-permute-start(bf16[8,320,128]{2,1,0:T(8,128)(2,1)S(1)} %collective-permute-done.11.refs_0_.refs_4_), channel_id=1, source_target_pairs={{0,4},{4,0},{8,12},{12,8},{16,20},{20,16},{24,28},{28,24},{1,5},{5... | collective-permute-start | bytes 1966088 | tf_op jit(solution)/shard_map/ppermute | solution.py:328
  78.7 12.7 %collective-permute-start.13 = (bf16[8,320,128]{2,1,0:T(8,128)(2,1)S(1)}, bf16[8,320,128]{2,1,0:T(8,128)(2,1)S(1)}, u32[]{:S(2)}, u32[]{:S(2)}) collective-permute-start(bf16[8,320,128]{2,1,0:T(8,128)(2,1)S(1)} %collective-permute-done.11.refs_0_.refs_4_), channel_id=1, source_target_pairs={{0,8},{4,28},{8,16},{12,4},{16,24},{20,12},{24,0},{28,20},{1,9},{5... | collective-permute-start | bytes 1966088 | tf_op jit(solution)/shard_map/ppermute | solution.py:331
  85.0 7.2 %collective-permute-start.17 = (bf16[8,320,128]{2,1,0:T(8,128)(2,1)S(1)}, bf16[8,320,128]{2,1,0:T(8,128)(2,1)S(1)}, u32[]{:S(2)}, u32[]{:S(2)}) collective-permute-start(bf16[8,320,128]{2,1,0:T(8,128)(2,1)S(1)} %collective-permute-done.15.refs_0_.refs_5_), channel_id=1, source_target_pairs={{0,4},{4,0},{8,12},{12,8},{16,20},{20,16},{24,28},{28,24},{1,5},{5... | collective-permute-start | bytes 1966088 | tf_op jit(solution)/shard_map/ppermute | solution.py:334
  91.4 13.0 %collective-permute-start.16 = (bf16[8,320,128]{2,1,0:T(8,128)(2,1)S(1)}, bf16[8,320,128]{2,1,0:T(8,128)(2,1)S(1)}, u32[]{:S(2)}, u32[]{:S(2)}) collective-permute-start(bf16[8,320,128]{2,1,0:T(8,128)(2,1)S(1)} %collective-permute-done.13.refs_1_.refs_8_), channel_id=1, source_target_pairs={{0,4},{4,0},{8,12},{12,8},{16,20},{20,16},{24,28},{28,24},{1,5},{5... | collective-permute-start | bytes 1966088 | tf_op jit(solution)/shard_map/ppermute | solution.py:337

commit v4 on v3

--- a/solution.py
+++ b/solution.py
@@ -17,8 +17,8 @@
 RING = ("y", "core")
 SETS = NX * NZ
 BANDS = NX * NZ * NY * NC
-TILE = 512
-TILES = 4
+SPAN = 512
+TOKENS = 2048
 LANES = 128
 Q_ROWS = 256
 KV_ROWS = 320
@@ -59,6 +59,29 @@
 
 def lanes(rows):
     return lax.broadcasted_iota(jnp.int32, (rows, LANES), 1)
+
+
+def begin_kernel(latent_hbm, sums_ref, last_ref, first_ref, latent_ref, sem):
+    copy = pltpu.make_async_copy(latent_hbm, latent_ref, sem.at[0])
+    copy.start()
+    copy.wait()
+    first, last = latent_ref[0].astype(F32), latent_ref[1].astype(F32)
+    sums_ref[0:1] = jnp.sum(first + last, axis=0, keepdims=True)
+    sums_ref[1:2] = jnp.sum(first * first + last * last, axis=0, keepdims=True)
+    last_ref[0] = latent_ref[1]
+    first_ref[0] = latent_ref[0]
+
+
+def begin(latent):
+    edge = jax.ShapeDtypeStruct((1,) + latent.shape[1:], BF16)
+    return pl.pallas_call(
+        begin_kernel,
+        in_specs=[pl.BlockSpec(memory_space=pltpu.HBM)],
+        out_specs=[pl.BlockSpec(memory_space=pltpu.VMEM)] * 3,
+        out_shape=[jax.ShapeDtypeStruct((2, latent.shape[2]), F32), edge, edge],
+        scratch_shapes=[pltpu.VMEM(latent.shape, BF16), pltpu.SemaphoreType.DMA((1,))],
+        name="begin",
+    )(pltpu.with_memory_space_constraint(latent, pltpu.HBM))
 
 
 def front_kernel(
@@ -77,7 +100,7 @@
     mean = sums_ref[0:1] / count
     var = sums_ref[1:2] / count - mean * mean
     rate = lax.rsqrt(var + 1e-05)
-    gain, bias = vec_ref[0:1], vec_ref[1:2]
+    gain, bias, conv_bias, ln_gain, ln_bias = [vec_ref[i : i + 1] for i in range(5)]
     row = lax.broadcasted_iota(jnp.int32, (128, chans), 0)
     copies[0].wait()
     sources = [before_ref[0], latent_ref[0], latent_ref[1], after_ref[0]]
@@ -94,7 +117,7 @@
         shift_ref[0, here] = left.astype(BF16)
         shift_ref[1, here] = act.astype(BF16)
         shift_ref[2, here] = right.astype(BF16)
-    total = latent_ref[...].reshape(256, chans).astype(F32) + vec_ref[2:3]
+    total = latent_ref[...].reshape(256, chans).astype(F32) + conv_bias
     for i in range(3):
         copies[1 + i].wait()
         for col in range(3):
@@ -104,7 +127,7 @@
     values = hidden.astype(F32)
     values = values - jnp.mean(values, axis=1, keepdims=True)
     spread = jnp.mean(values * values, axis=1, keepdims=True)
-    normed = (values * lax.rsqrt(spread + 1e-05) * vec_ref[3:4] + vec_ref[4:5]).astype(BF16)
+    normed = (values * lax.rsqrt(spread + 1e-05) * ln_gain + ln_bias).astype(BF16)
     scale = math.log2(math.e) / math.sqrt(HEAD_DIM)
     copies[4].wait()
     query = (dot(normed, w_ref[0]) * scale).astype(BF16)
@@ -161,7 +184,7 @@
         value = kv_ref[src, 128:256, :]
         for side in (value, swap(value)):
             values.append(jnp.where(lane < 64, side, jnp.ones_like(side)))
-    keys = jnp.concatenate([jnp.concatenate(keys, axis=1), jnp.zeros((64, TILE), BF16)], axis=0)
+    keys = jnp.concatenate([jnp.concatenate(keys, axis=1), jnp.zeros((64, SPAN), BF16)], axis=0)
     return 0, keys, jnp.concatenate(values, axis=0)
 
 
@@ -171,19 +194,19 @@
     keys = [kv_ref[src, 256:320, 0:64] for src in sources]
     values = [kv_ref[src, 256:320, :] for src in sources]
     values = [jnp.where(lane >= 64, v, jnp.ones_like(v)) for v in values]
-    keys = jnp.concatenate([jnp.zeros((64, TILE), BF16), jnp.concatenate(keys, axis=1)], axis=0)
+    keys = jnp.concatenate([jnp.zeros((64, SPAN), BF16), jnp.concatenate(keys, axis=1)], axis=0)
     return 1, keys, jnp.concatenate(values, axis=0)
 
 
-def fold_kernel(count, first, last, q_ref, *refs):
+def fold_kernel(count, tile, first, last, q_ref, *refs):
     kv_refs, refs = refs[:count], refs[count:]
     if not first:
         acc_in, refs = refs[0], refs[1:]
     if last:
         far_refs, refs = refs[:SETS], refs[SETS:]
     acc_ref = refs[0]
-    acc_ref[0] = jnp.zeros((2, TILE, LANES), F32) if first else acc_in[0]
-    query = q_ref[...].reshape(TILE, LANES)
+    acc_ref[...] = jnp.zeros((2, tile, LANES), F32) if first else acc_in[...]
+    query = q_ref[...].reshape(tile, LANES)
 
     steps = []
     for kv_ref in kv_refs:
@@ -197,15 +220,15 @@
         if held is not None:
             held_kind, held_score, held_values = held
             weight = jnp.exp2(held_score).astype(BF16)
-            acc_ref[0, held_kind] += dot(weight, held_values)
+            acc_ref[held_kind] += dot(weight, held_values)
         held = None if step is None else (kind, score, values)
 
     if last:
         out_ref, store_ref, top_ref, sems = refs[1:]
-        wide = lanes(TILE)
-        total = jnp.where(wide < 64, acc_ref[0, 1], acc_ref[0, 0])
+        wide = lanes(tile)
+        total = jnp.where(wide < 64, acc_ref[1], acc_ref[0])
         good = (jnp.min(total) > LOW) & (jnp.max(total) < HIGH)
-        top_ref[...] = jnp.zeros((2, TILE, LANES), F32)
+        top_ref[...] = jnp.zeros((2, tile, LANES), F32)
 
         @pl.when(jnp.logical_not(good))
         def _():
@@ -214,8 +237,8 @@
                 here = store_ref.at[pl.ds(SETS * i, SETS)]
                 copies.append(pltpu.make_async_copy(far_ref, here, sems.at[i]))
                 copies[-1].start()
-            acc_ref[0] = jnp.zeros((2, TILE, LANES), F32)
-            top_ref[...] = jnp.full((2, TILE, LANES), -1e30, F32)
+            acc_ref[...] = jnp.zeros((2, tile, LANES), F32)
+            top_ref[...] = jnp.full((2, tile, LANES), -1e30, F32)
             for copy in copies:
                 copy.wait()
 
@@ -225,7 +248,7 @@
                 top = jnp.maximum(top_ref[kind], jnp.max(score, axis=1, keepdims=True))
                 weight = jnp.exp2(score - top[:, 0:1]).astype(BF16)
                 factor = jnp.exp2(top_ref[kind] - top)
-                acc_ref[0, kind] = acc_ref[0, kind] * factor + dot(weight, values)
+                acc_ref[kind] = acc_ref[kind] * factor + dot(weight, values)
                 top_ref[kind] = top
 
             def pair_body(pair, carry):
@@ -239,12 +262,12 @@
             lax.fori_loop(0, SETS * SETS // 2, pair_body, 0)
             lax.fori_loop(0, SETS, block_body, 0)
 
-        main, extra = acc_ref[0, 0], acc_ref[0, 1]
+        main, extra = acc_ref[0], acc_ref[1]
         out = jnp.where(wide < 64, main, extra) / jnp.where(wide < 64, swap(main), swap(extra))
         out = out.astype(BF16)
         level = (jnp.log2(extra) + top_ref[1])[:, 0:1]
         row = lax.broadcasted_iota(jnp.int32, (16, LANES), 0)
-        for src in range(2):
+        for src in range(tile // 256):
             out_ref[src, 0:256] = out[256 * src : 256 * src + 256]
             tail = jnp.zeros((16, LANES), F32)
             for half in range(2):
@@ -257,25 +280,25 @@
             out_ref[src, 256:272] = tail.astype(BF16)
 
 
-def fold(got, blocks, acc, every=None):
+def fold(got, blocks, acc, every=None, tile=512):
     first, last = acc is None, every is not None
-    acc_spec = pl.BlockSpec((1, 2, TILE, LANES), lambda t: (t, 0, 0, 0))
+    acc_spec = pl.BlockSpec((2, tile, LANES), lambda t: (0, t, 0))
     kv_spec = pl.BlockSpec((SETS, KV_ROWS, LANES), lambda t: (0, 0, 0))
     out_specs = [acc_spec]
-    out_shape = [jax.ShapeDtypeStruct((TILES, 2, TILE, LANES), F32)]
+    out_shape = [jax.ShapeDtypeStruct((2, TOKENS, LANES), F32)]
     scratch = []
     if last:
-        out_specs.append(pl.BlockSpec((2, BACK_ROWS, LANES), lambda t: (t, 0, 0)))
+        out_specs.append(pl.BlockSpec((tile // 256, BACK_ROWS, LANES), lambda t: (t, 0, 0)))
         out_shape.append(jax.ShapeDtypeStruct((SETS, BACK_ROWS, LANES), BF16))
         scratch = [
             pltpu.VMEM((SETS * SETS, KV_ROWS, LANES), BF16),
-            pltpu.VMEM((2, TILE, LANES), F32),
+            pltpu.VMEM((2, tile, LANES), F32),
             pltpu.SemaphoreType.DMA((SETS,)),
         ]
     return pl.pallas_call(
-        functools.partial(fold_kernel, len(blocks), first, last),
-        grid=(TILES,),
-        in_specs=[pl.BlockSpec((2, Q_ROWS, LANES), lambda t: (t, 0, 0))]
+        functools.partial(fold_kernel, len(blocks), tile, first, last),
+        grid=(TOKENS // tile,),
+        in_specs=[pl.BlockSpec((tile // 256, Q_ROWS, LANES), lambda t: (t, 0, 0))]
         + [kv_spec] * len(blocks)
         + ([] if first else [acc_spec])
         + ([pl.BlockSpec(memory_space=pl.ANY)] * SETS if last else []),
@@ -288,18 +311,57 @@
     )(got, *blocks, *(() if first else (acc,)), *(every or ()))
 
 
+def finish_kernel(back_ref, hidden_ref, out_ref):
+    for pair in range(SETS // 2):
+        here = slice(128 * pair, 128 * pair + 128)
+        both = [back_ref[2 * pair, 0:256, 0:64], back_ref[2 * pair + 1, 0:256, 0:64]]
+        both = jnp.concatenate(both, axis=1).astype(F32)
+        out_ref[:, here] = (hidden_ref[:, here].astype(F32) + both).astype(BF16)
+    for half in range(2):
+        rows = slice(128 * half, 128 * half + 128)
+        shares = []
+        for head in range(2):
+            levels = []
+            for s in range(4 * head, 4 * head + 4):
+                tail = back_ref[s, 256:272].astype(F32)
+                levels.append(sum(tail[2 * p + half : 2 * p + half + 1] for p in range(3)))
+            top = functools.reduce(jnp.maximum, levels)
+            parts = [jnp.exp2(level - top) for level in levels]
+            total = sum(parts)
+            shares += [part / total for part in parts]
+        table = jnp.concatenate(shares + [jnp.zeros((LANES - SETS, LANES), F32)], axis=0).T
+        both = []
+        for head in range(2):
+            value = jnp.zeros((128, 64), F32)
+            for s in range(4 * head, 4 * head + 4):
+                part = back_ref[s, rows, 64:128].astype(F32)
+                value = value + part * jnp.broadcast_to(table[:, s : s + 1], (128, 64))
+            both.append(value)
+        here = slice(64 * SETS, 64 * SETS + 128)
+        value = hidden_ref[rows, here].astype(F32) + jnp.concatenate(both, axis=1)
+        out_ref[rows, here] = value.astype(BF16)
+
+
+def finish(back, hidden):
+    return pl.pallas_call(
+        finish_kernel,
+        in_specs=[pl.BlockSpec(memory_space=pltpu.VMEM)] * 2,
+        out_specs=pl.BlockSpec(memory_space=pltpu.VMEM),
+        out_shape=jax.ShapeDtypeStruct(hidden.shape, BF16),
+        name="finish",
+    )(*[pltpu.with_memory_space_constraint(a, pltpu.VMEM) for a in (back, hidden)])
+
+
 def on_device(
     latent, gn_gain, gn_bias, conv_weight, conv_bias, ln_gain, ln_bias, w_query, w_key, w_value
 ):
     rows_here, cols, chans = latent.shape
-    tokens = rows_here * cols
     width = chans // GROUPS
-    edges = lax.optimization_barrier((latent[-1:], latent[:1], latent))
-    before, after = halo(*edges[:2])
-    flat = edges[2].astype(F32).reshape(-1, chans)
-    sums = jnp.stack([jnp.sum(flat, axis=0), jnp.sum(flat * flat, axis=0)])
+    sums, last, first = begin(latent)
+    before, after = halo(last, first)
+    sums = total_of(sums)
     sums = jnp.sum(sums.reshape(2, GROUPS, width), axis=2, keepdims=True)
-    sums = total_of(jnp.broadcast_to(sums, (2, GROUPS, width)).reshape(2, chans))
+    sums = jnp.broadcast_to(sums, (2, GROUPS, width)).reshape(2, chans)
     place = lax.axis_index(BAND)
     row = lax.broadcasted_iota(jnp.int32, (8, chans), 0)
     vec = jnp.where(row == 5, jnp.where(place > 0, 1.0, 0.0), 0.0)
@@ -326,10 +388,10 @@
     (acc,) = fold(got, [twin], acc)
     ahead, acc = tied((ahead, acc))
     ahead_twin = lax.ppermute(ahead, RING, cross)
-    (acc,) = fold(got, [ahead], acc)
+    (acc,) = fold(got, [ahead], acc, tile=1024)
     ahead, acc = tied((ahead, acc))
     far = lax.ppermute(ahead, RING, along)
-    (acc,) = fold(got, [behind], acc)
+    (acc,) = fold(got, [behind], acc, tile=1024)
     behind, acc = tied((behind, acc))
     behind_twin = lax.ppermute(behind, RING, cross)
     (acc,) = fold(got, [ahead_twin], acc)
@@ -340,15 +402,7 @@
     unused, out = fold(got, [far_twin], acc, every)
 
     back = lax.all_to_all(out, ("x", "z"), 0, 0)
-    main = back[:, :256, :64].transpose(1, 0, 2).reshape(tokens, SETS * HEAD_DIM)
-    level = jnp.sum(back[:, 256:262].astype(F32).reshape(SETS, 3, 256), axis=1).reshape(2, 4, 256)
-    share = jnp.exp2(level - jnp.max(level, axis=1, keepdims=True))
-    share = share / jnp.sum(share, axis=1, keepdims=True)
-    extra = back[:, :256, 64:].astype(F32).reshape(2, 4, 256, HEAD_DIM)
-    extra = jnp.sum(extra * share[..., None], axis=1).transpose(1, 0, 2)
-    extra = extra.reshape(tokens, 2 * HEAD_DIM)
-    attended = jnp.concatenate([main.astype(F32), extra], axis=1)
-    return (hidden.astype(F32) + attended).astype(BF16).reshape(rows_here, cols, chans)
+    return finish(back, hidden).reshape(rows_here, cols, chans)
 
 
 def solution(mesh):

time: 257 us -> 255 us (level)
  Pallas kernels: 187 us -> 190 us
    pallas_call x7 -> x9, Pallas kernels: 180 us -> 183 us  [the longest x7 180 us: fold(): pl.pallas_call(functools.partial(fold_kernel, len(blocks), tile, first, l...]
  transfers between devices with their start and end apart: 18 -> 18, of which waited for: 3 -> 3; matrix products, arithmetic and copies ran while one was open for 0% -> 1% of each run, Pallas kernels for 17% -> 17%
where the time goes in v4:
time: 255 us
  Pallas kernels  190 us (75%)
  blocking collectives  29.8 us (12%)
  starting transfers between devices  28 us (11%)
  waiting for transfers between devices  4.59 us (2%)
    pallas_call x7, Pallas kernels, fold(): pl.pallas_call(functools.partial(fold_kernel, len(blocks), tile, first, l...  180 us
    all_to_all x1, blocking collectives, on_device(): got = lax.all_to_all(send, ('x', 'z'), 0, 0)  16.9 us
    all_to_all x1, blocking collectives, on_device(): back = lax.all_to_all(out, ('x', 'z'), 0, 0)  12.9 us
    ppermute x9, starting transfers between devices, total_of(): parts.append(lax.ppermute(value, axis, perm))  12.4 us
    pallas_call x1, Pallas kernels, front(): pl.pallas_call(front_kernel, in_specs=[pl.BlockSpec(memory_space=pltpu.VM...  6.88 us
  transfers between devices with their start and end apart: 18, of which 3 were waited for; matrix products, arithmetic and copies ran while one was open for 1% of the time, Pallas kernels for 17%

profile of v4, /device:TPU:1, one launch (start us, length us, event | category | flops | bytes accessed | tf_op | source)
XLA Modules:
  0.0 255.0 jit_solution(18431657886005030467)
XLA Ops:
  0.0 1.7 begin.1
  1.7 3.6 %collective-permute-start.2 = (f32[2,640]{1,0:T(2,128)}, f32[2,640]{1,0:T(2,128)S(1)}, u32[]{:S(2)}, u32[]{:S(2)}) collective-permute-start(f32[2,640]{1,0:T(2,128)} %get-tuple-element.21), channel_id=1, source_target_pairs={{0,24},{8,0},{16,8},{24,16},{1,25},{9,1},{17,9},{25,17},{2,26},{10... | collective-permute-start | bytes 15368 | tf_op jit(solution)/shard_map/ppermute | solution.py:39
  5.4 0.3 collective-permute-start.1
  5.7 0.7 collective-permute-start
  6.4 4.9 %collective-permute-start.9 = (bf16[1,128,640]{2,1,0:T(8,128)(2,1)}, bf16[1,128,640]{2,1,0:T(8,128)(2,1)S(1)}, u32[]{:S(2)}, u32[]{:S(2)}) collective-permute-start(bf16[1,128,640]{2,1,0:T(8,128)(2,1)} %get-tuple-element.22), channel_id=1, source_target_pairs={{0,4},{4,8},{8,12},{12,16},{16,20},{20,24},{24,28},{28,32},{32,36}... | collective-permute-start | bytes 491528 | tf_op jit(solution)/shard_map/ppermute | solution.py:47
  11.3 1.9 collective-permute-start.10
  13.3 0.0 collective-permute-done.2
  13.3 0.0 collective-permute-done.1
  13.3 0.0 collective-permute-done
  13.3 0.7 add_add_fusion.2
  14.0 0.0 collective-permute-start.5
  14.0 4.0 %collective-permute-start.4 = (f32[2,640]{1,0:T(2,128)S(1)}, f32[2,640]{1,0:T(2,128)S(1)}, u32[]{:S(2)}, u32[]{:S(2)}) collective-permute-start(f32[2,640]{1,0:T(2,128)S(1)} %add_add_fusion.2), channel_id=1, source_target_pairs={{0,32},{4,36},{32,0},{36,4},{1,33},{5,37},{33,1},{37,5},{2,34},{6,... | collective-permute-start | bytes 15368 | tf_op jit(solution)/shard_map/ppermute | solution.py:39
  18.0 0.1 collective-permute-start.3
  18.1 2.3 collective-permute-done.5
  20.4 0.0 collective-permute-done.4
  20.4 0.0 collective-permute-done.3
  20.4 2.6 %collective-permute-start.8 = (f32[2,640]{1,0:T(2,128)S(1)}, f32[2,640]{1,0:T(2,128)S(1)}, u32[]{:S(2)}, u32[]{:S(2)}) collective-permute-start(f32[2,640]{1,0:T(2,128)S(1)} %add_add_fusion.1), channel_id=1, source_target_pairs={{0,192},{64,0},{128,64},{192,128},{1,193},{65,1},{129,65},{193,129... | collective-permute-start | bytes 15368 | tf_op jit(solution)/shard_map/ppermute | solution.py:39
  23.0 0.5 collective-permute-start.7
  23.5 0.6 collective-permute-start.6
  24.1 0.8 select_select_fusion.vec_ref
  25.0 0.0 collective-permute-done.8
  25.0 2.0 collective-permute-done.7
  27.0 0.2 collective-permute-done.6
  27.2 0.1 reshape.10
  27.3 0.2 fusion
  27.5 0.1 reshape.11.sums_ref
  27.6 0.0 collective-permute-done.9.before_ref
  27.6 0.0 collective-permute-done.10.after_ref
  27.6 6.9 %front.1 = (bf16[256,640]{1,0:T(8,128)(2,1)S(1)}, bf16[8,576,128]{2,1,0:T(8,128)(2,1)S(1)}) custom-call(f32[2,640]{1,0:T(2,128)S(1)} %reshape.11.sums_ref, f32[8,640]{1,0:T(8,128)S(1)} %select_select_fusion.vec_ref, bf16[1,128,640]{2,1,0:T(8,128)(2,1)S(1)} %collective-permute-done.9.before_ref, bf16[1,128,640]{2,1,0:T(8,128)(2,1)S(1)} %collective-permute-done.10.after_ref, ...), custom_call_target="tpu_custom_call" | custom-call | tf_op jit(solution)/shard_map/front/pallas_call | solution.py:158
  34.5 16.9 %all_to_all.10.q_ref = bf16[8,576,128]{2,1,0:T(8,128)(2,1)S(1)} all-to-all(bf16[8,576,128]{2,1,0:T(8,128)(2,1)S(1)} %get-tuple-element.24), channel_id=1, replica_groups=mesh['x'=4,'z'=2,'y'=4,'core'=2,'img'=4] {'x','z'}, dimensions={0} | all-to-all | bytes 2359296 | tf_op jit(solution)/shard_map/all_to_all | solution.py:375
  51.4 4.3 %collective-permute-start.12 = (bf16[8,320,128]{2,1,0:T(8,128)(2,1)S(1)}, bf16[8,320,128]{2,1,0:T(8,128)(2,1)S(1)}, u32[]{:S(2)}, u32[]{:S(2)}) collective-permute-start(bf16[8,320,128]{2,1,0:T(8,128)(2,1)S(1)} %slice.4.refs_0_.refs_2_), channel_id=1, source_target_pairs={{0,4},{4,0},{8,12},{12,8},{16,20},{20,16},{24,28},{28,24},{1,5},{5... | collective-permute-start | bytes 1966088 | tf_op jit(solution)/shard_map/ppermute | solution.py:383
  55.7 0.0 collective-permute-start.11
  55.7 6.2 %fold.7.refs_1_ = f32[2,2048,128]{2,1,0:T(8,128)S(1)} custom-call(bf16[8,576,128]{2,1,0:T(8,128)(2,1)S(1)} %all_to_all.10.q_ref, bf16[8,320,128]{2,1,0:T(8,128)(2,1)S(1)} %slice.4.refs_0_.refs_2_), custom_call_target="tpu_custom_call" | custom-call | tf_op jit(solution)/shard_map/fold/pallas_call | solution.py:298
  61.9 1.5 collective-permute-start.15
  63.5 0.0 collective-permute-done.12.refs_0_.refs_3_
  63.5 6.4 %fold.8.refs_1_ = f32[2,2048,128]{2,1,0:T(8,128)S(1)} custom-call(bf16[8,576,128]{2,1,0:T(8,128)(2,1)S(1)} %all_to_all.10.q_ref, bf16[8,320,128]{2,1,0:T(8,128)(2,1)S(1)} %collective-permute-done.12.refs_0_.refs_3_, f32[2,2048,128]{2,1,0:T(8,128)S(1)} %fold.7.refs_1_), custom_call_target="tpu_custom_call", output_to_operand_aliasing={{}: (2, {})} | custom-call | tf_op jit(solution)/shard_map/fold/pallas_call | solution.py:298
  69.8 0.0 collective-permute-done.11.refs_0_.refs_4_
  69.9 1.9 collective-permute-start.14
  71.8 6.1 %fold.9.refs_1_ = f32[2,2048,128]{2,1,0:T(8,128)S(1)} custom-call(bf16[8,576,128]{2,1,0:T(8,128)(2,1)S(1)} %all_to_all.10.q_ref, bf16[8,320,128]{2,1,0:T(8,128)(2,1)S(1)} %collective-permute-done.11.refs_0_.refs_4_, f32[2,2048,128]{2,1,0:T(8,128)S(1)} %fold.8.refs_1_), custom_call_target="tpu_custom_call", output_to_operand_aliasing={{}: (2, {})} | custom-call | tf_op jit(solution)/shard_map/fold/pallas_call | solution.py:298
  77.9 0.1 collective-permute-start.13
  78.0 0.0 collective-permute-done.15.refs_0_.refs_5_
  78.0 6.1 %fold.10.refs_1_ = f32[2,2048,128]{2,1,0:T(8,128)S(1)} custom-call(bf16[8,576,128]{2,1,0:T(8,128)(2,1)S(1)} %all_to_all.10.q_ref, bf16[8,320,128]{2,1,0:T(8,128)(2,1)S(1)} %collective-permute-done.15.refs_0_.refs_5_, f32[2,2048,128]{2,1,0:T(8,128)S(1)} %fold.9.refs_1_), custom_call_target="tpu_custom_call", output_to_operand_aliasing={{}: (2, {})} | custom-call | tf_op jit(solution)/shard_map/fold/pallas_call | solution.py:298
  84.1 0.3 collective-permute-start.17
  84.4 0.0 collective-permute-done.14.refs_0_.refs_6_
  84.4 6.4 %fold.11.refs_2_ = f32[2,2048,128]{2,1,0:T(8,128)S(1)} custom-call(bf16[8,576,128]{2,1,0:T(8,128)(2,1)S(1)} %all_to_all.10.q_ref, bf16[8,320,128]{2,1,0:T(8,128)(2,1)S(1)} %collective-permute-done.14.refs_0_.refs_6_, f32[2,2048,128]{2,1,0:T(8,128)S(1)} %fold.10.refs_1_), custom_call_target="tpu_custom_call", output_to_operand_aliasing={{}: (2, {})} | custom-call | tf_op jit(solution)/shard_map/fold/pallas_call | solution.py:298
  90.8 0.0 collective-permute-done.13.refs_1_.refs_8_
  90.8 0.6 collective-permute-start.16
  91.3 0.0 collective-permute-done.17.refs_0_.refs_7_
  91.4 12.3 %fold.12.refs_1_ = f32[2,2048,128]{2,1,0:T(8,128)S(1)} custom-call(bf16[8,576,128]{2,1,0:T(8,128)(2,1)S(1)} %all_to_all.10.q_ref, bf16[8,320,128]{2,1,0:T(8,128)(2,1)S(1)} %collective-permute-done.17.refs_0_.refs_7_, bf16[8,320,128]{2,1,0:T(8,128)(2,1)S(1)} %collective-permute-done.13.refs_1_.refs_8_, ...), custom_call_target="tpu_custom_call", output_to_operand_aliasing={{}: (3, {})} | custom-call | tf_op jit(solution)/shard_map/fold/pallas_call | solution.py:298
  103.6 0.0 collective-permute-done.16.refs_0_.refs_9_
  103.7 137.1 %fold.13 = (f32[2,2048,128]{2,1,0:T(8,128)S(1)}, bf16[8,272,128]{2,1,0:T(8,128)(2,1)S(1)}) custom-call(bf16[8,576,128]{2,1,0:T(8,128)(2,1)S(1)} %all_to_all.10.q_ref, bf16[8,320,128]{2,1,0:T(8,128)(2,1)S(1)} %collective-permute-done.16.refs_0_.refs_9_, f32[2,2048,128]{2,1,0:T(8,128)S(1)} %fold.12.refs_1_, ...), custom_call_target="tpu_custom_call", output_to_operand_aliasing={{0}: (2, {})} | custom-call | tf_op jit(solution)/shard_map/fold/pallas_call | solution.py:298
  240.8 12.9 %all_to_all.11.back_ref = bf16[8,272,128]{2,1,0:T(8,128)(2,1)S(1)} all-to-all(bf16[8,272,128]{2,1,0:T(8,128)(2,1)S(1)} %get-tuple-element.35), channel_id=1, replica_groups=mesh['x'=4,'z'=2,'y'=4,'core'=2,'img'=4] {'x','z'}, dimensions={0} | all-to-all | bytes 1114112 | tf_op jit(solution)/shard_map/all_to_all | solution.py:404
  253.7 1.3 finish.1
  (7 shorter events, 0.1 us)
Async XLA Ops:
  1.7 11.6 %collective-permute-start.2 = (f32[2,640]{1,0:T(2,128)}, f32[2,640]{1,0:T(2,128)S(1)}, u32[]{:S(2)}, u32[]{:S(2)}) collective-permute-start(f32[2,640]{1,0:T(2,128)} %get-tuple-element.21), channel_id=1, source_target_pairs={{0,24},{8,0},{16,8},{24,16},{1,25},{9,1},{17,9},{25,17},{2,26},{10... | collective-permute-start | bytes 15368 | tf_op jit(solution)/shard_map/ppermute | solution.py:39
  5.4 7.9 %collective-permute-start.1 = (f32[2,640]{1,0:T(2,128)}, f32[2,640]{1,0:T(2,128)S(1)}, u32[]{:S(2)}, u32[]{:S(2)}) collective-permute-start(f32[2,640]{1,0:T(2,128)} %get-tuple-element.21), channel_id=1, source_target_pairs={{0,16},{8,24},{16,0},{24,8},{1,17},{9,25},{17,1},{25,9},{2,18},{10... | collective-permute-start | bytes 15368 | tf_op jit(solution)/shard_map/ppermute | solution.py:39
  5.7 7.6 %collective-permute-start = (f32[2,640]{1,0:T(2,128)}, f32[2,640]{1,0:T(2,128)S(1)}, u32[]{:S(2)}, u32[]{:S(2)}) collective-permute-start(f32[2,640]{1,0:T(2,128)} %get-tuple-element.21), channel_id=1, source_target_pairs={{0,8},{8,16},{16,24},{24,0},{1,9},{9,17},{17,25},{25,1},{2,10},{10... | collective-permute-start | bytes 15368 | tf_op jit(solution)/shard_map/ppermute | solution.py:39
  6.4 21.2 %collective-permute-start.9 = (bf16[1,128,640]{2,1,0:T(8,128)(2,1)}, bf16[1,128,640]{2,1,0:T(8,128)(2,1)S(1)}, u32[]{:S(2)}, u32[]{:S(2)}) collective-permute-start(bf16[1,128,640]{2,1,0:T(8,128)(2,1)} %get-tuple-element.22), channel_id=1, source_target_pairs={{0,4},{4,8},{8,12},{12,16},{16,20},{20,24},{24,28},{28,32},{32,36}... | collective-permute-start | bytes 491528 | tf_op jit(solution)/shard_map/ppermute | solution.py:47
  11.3 16.3 %collective-permute-start.10 = (bf16[1,128,640]{2,1,0:T(8,128)(2,1)}, bf16[1,128,640]{2,1,0:T(8,128)(2,1)S(1)}, u32[]{:S(2)}, u32[]{:S(2)}) collective-permute-start(bf16[1,128,640]{2,1,0:T(8,128)(2,1)} %get-tuple-element.23), channel_id=1, source_target_pairs={{4,0},{8,4},{12,8},{16,12},{20,16},{24,20},{28,24},{32,28},{36,32}... | collective-permute-start | bytes 491528 | tf_op jit(solution)/shard_map/ppermute | solution.py:48
  14.0 6.4 %collective-permute-start.5 = (f32[2,640]{1,0:T(2,128)S(1)}, f32[2,640]{1,0:T(2,128)S(1)}, u32[]{:S(2)}, u32[]{:S(2)}) collective-permute-start(f32[2,640]{1,0:T(2,128)S(1)} %add_add_fusion.2), channel_id=1, source_target_pairs={{0,36},{4,0},{32,4},{36,32},{1,37},{5,1},{33,5},{37,33},{2,38},{6,... | collective-permute-start | bytes 15368 | tf_op jit(solution)/shard_map/ppermute | solution.py:39
  14.0 6.4 %collective-permute-start.4 = (f32[2,640]{1,0:T(2,128)S(1)}, f32[2,640]{1,0:T(2,128)S(1)}, u32[]{:S(2)}, u32[]{:S(2)}) collective-permute-start(f32[2,640]{1,0:T(2,128)S(1)} %add_add_fusion.2), channel_id=1, source_target_pairs={{0,32},{4,36},{32,0},{36,4},{1,33},{5,37},{33,1},{37,5},{2,34},{6,... | collective-permute-start | bytes 15368 | tf_op jit(solution)/shard_map/ppermute | solution.py:39
  18.0 2.4 collective-permute-start.3
  20.4 4.5 %collective-permute-start.8 = (f32[2,640]{1,0:T(2,128)S(1)}, f32[2,640]{1,0:T(2,128)S(1)}, u32[]{:S(2)}, u32[]{:S(2)}) collective-permute-start(f32[2,640]{1,0:T(2,128)S(1)} %add_add_fusion.1), channel_id=1, source_target_pairs={{0,192},{64,0},{128,64},{192,128},{1,193},{65,1},{129,65},{193,129... | collective-permute-start | bytes 15368 | tf_op jit(solution)/shard_map/ppermute | solution.py:39
  23.0 4.0 %collective-permute-start.7 = (f32[2,640]{1,0:T(2,128)S(1)}, f32[2,640]{1,0:T(2,128)S(1)}, u32[]{:S(2)}, u32[]{:S(2)}) collective-permute-start(f32[2,640]{1,0:T(2,128)S(1)} %add_add_fusion.1), channel_id=1, source_target_pairs={{0,128},{64,192},{128,0},{192,64},{1,129},{65,193},{129,1},{193,65... | collective-permute-start | bytes 15368 | tf_op jit(solution)/shard_map/ppermute | solution.py:39
  23.5 3.7 %collective-permute-start.6 = (f32[2,640]{1,0:T(2,128)S(1)}, f32[2,640]{1,0:T(2,128)S(1)}, u32[]{:S(2)}, u32[]{:S(2)}) collective-permute-start(f32[2,640]{1,0:T(2,128)S(1)} %add_add_fusion.1), channel_id=1, source_target_pairs={{0,64},{64,128},{128,192},{192,0},{1,65},{65,129},{129,193},{193,1... | collective-permute-start | bytes 15368 | tf_op jit(solution)/shard_map/ppermute | solution.py:39
  51.4 12.1 %collective-permute-start.12 = (bf16[8,320,128]{2,1,0:T(8,128)(2,1)S(1)}, bf16[8,320,128]{2,1,0:T(8,128)(2,1)S(1)}, u32[]{:S(2)}, u32[]{:S(2)}) collective-permute-start(bf16[8,320,128]{2,1,0:T(8,128)(2,1)S(1)} %slice.4.refs_0_.refs_2_), channel_id=1, source_target_pairs={{0,4},{4,0},{8,12},{12,8},{16,20},{20,16},{24,28},{28,24},{1,5},{5... | collective-permute-start | bytes 1966088 | tf_op jit(solution)/shard_map/ppermute | solution.py:383
  55.7 14.1 %collective-permute-start.11 = (bf16[8,320,128]{2,1,0:T(8,128)(2,1)S(1)}, bf16[8,320,128]{2,1,0:T(8,128)(2,1)S(1)}, u32[]{:S(2)}, u32[]{:S(2)}) collective-permute-start(bf16[8,320,128]{2,1,0:T(8,128)(2,1)S(1)} %slice.4.refs_0_.refs_2_), channel_id=1, source_target_pairs={{0,8},{4,28},{8,16},{12,4},{16,24},{20,12},{24,0},{28,20},{1,9},{5... | collective-permute-start | bytes 1966088 | tf_op jit(solution)/shard_map/ppermute | solution.py:384
  61.9 16.0 %collective-permute-start.15 = (bf16[8,320,128]{2,1,0:T(8,128)(2,1)S(1)}, bf16[8,320,128]{2,1,0:T(8,128)(2,1)S(1)}, u32[]{:S(2)}, u32[]{:S(2)}) collective-permute-start(bf16[8,320,128]{2,1,0:T(8,128)(2,1)S(1)} %slice.4.refs_0_.refs_2_), channel_id=1, source_target_pairs={{8,0},{28,4},{16,8},{4,12},{24,16},{12,20},{0,24},{20,28},{9,1},{2... | collective-permute-start | bytes 1966088 | tf_op jit(solution)/shard_map/ppermute | solution.py:387
  69.9 14.6 %collective-permute-start.14 = (bf16[8,320,128]{2,1,0:T(8,128)(2,1)S(1)}, bf16[8,320,128]{2,1,0:T(8,128)(2,1)S(1)}, u32[]{:S(2)}, u32[]{:S(2)}) collective-permute-start(bf16[8,320,128]{2,1,0:T(8,128)(2,1)S(1)} %collective-permute-done.11.refs_0_.refs_4_), channel_id=1, source_target_pairs={{0,4},{4,0},{8,12},{12,8},{16,20},{20,16},{24,28},{28,24},{1,5},{5... | collective-permute-start | bytes 1966088 | tf_op jit(solution)/shard_map/ppermute | solution.py:390
  77.9 12.9 %collective-permute-start.13 = (bf16[8,320,128]{2,1,0:T(8,128)(2,1)S(1)}, bf16[8,320,128]{2,1,0:T(8,128)(2,1)S(1)}, u32[]{:S(2)}, u32[]{:S(2)}) collective-permute-start(bf16[8,320,128]{2,1,0:T(8,128)(2,1)S(1)} %collective-permute-done.11.refs_0_.refs_4_), channel_id=1, source_target_pairs={{0,8},{4,28},{8,16},{12,4},{16,24},{20,12},{24,0},{28,20},{1,9},{5... | collective-permute-start | bytes 1966088 | tf_op jit(solution)/shard_map/ppermute | solution.py:393
  84.1 7.3 %collective-permute-start.17 = (bf16[8,320,128]{2,1,0:T(8,128)(2,1)S(1)}, bf16[8,320,128]{2,1,0:T(8,128)(2,1)S(1)}, u32[]{:S(2)}, u32[]{:S(2)}) collective-permute-start(bf16[8,320,128]{2,1,0:T(8,128)(2,1)S(1)} %collective-permute-done.15.refs_0_.refs_5_), channel_id=1, source_target_pairs={{0,4},{4,0},{8,12},{12,8},{16,20},{20,16},{24,28},{28,24},{1,5},{5... | collective-permute-start | bytes 1966088 | tf_op jit(solution)/shard_map/ppermute | solution.py:396
  90.8 12.9 %collective-permute-start.16 = (bf16[8,320,128]{2,1,0:T(8,128)(2,1)S(1)}, bf16[8,320,128]{2,1,0:T(8,128)(2,1)S(1)}, u32[]{:S(2)}, u32[]{:S(2)}) collective-permute-start(bf16[8,320,128]{2,1,0:T(8,128)(2,1)S(1)} %collective-permute-done.13.refs_1_.refs_8_), channel_id=1, source_target_pairs={{0,4},{4,0},{8,12},{12,8},{16,20},{20,16},{24,28},{28,24},{1,5},{5... | collective-permute-start | bytes 1966088 | tf_op jit(solution)/shard_map/ppermute | solution.py:399

commit v5 on v4

--- a/solution.py
+++ b/solution.py
@@ -61,38 +61,50 @@
     return lax.broadcasted_iota(jnp.int32, (rows, LANES), 1)
 
 
-def begin_kernel(latent_hbm, sums_ref, last_ref, first_ref, latent_ref, sem):
-    copy = pltpu.make_async_copy(latent_hbm, latent_ref, sem.at[0])
-    copy.start()
-    copy.wait()
+def begin_kernel(
+    latent_hbm, wq_hbm, wk_hbm, wv_hbm, sums_ref, last_ref, first_ref, w_ref, latent_ref, sems
+):
+    copies = [pltpu.make_async_copy(latent_hbm, latent_ref, sems.at[0])]
+    for i, w_hbm in enumerate((wq_hbm, wk_hbm, wv_hbm)):
+        copies.append(pltpu.make_async_copy(w_hbm, w_ref.at[i], sems.at[1 + i]))
+    for copy in copies:
+        copy.start()
+    copies[0].wait()
     first, last = latent_ref[0].astype(F32), latent_ref[1].astype(F32)
     sums_ref[0:1] = jnp.sum(first + last, axis=0, keepdims=True)
     sums_ref[1:2] = jnp.sum(first * first + last * last, axis=0, keepdims=True)
     last_ref[0] = latent_ref[1]
     first_ref[0] = latent_ref[0]
-
-
-def begin(latent):
+    for copy in copies[1:]:
+        copy.wait()
+
+
+def begin(latent, w_query, w_key, w_value):
     edge = jax.ShapeDtypeStruct((1,) + latent.shape[1:], BF16)
+    far = [latent, w_query, w_key, w_value]
+    far = [pltpu.with_memory_space_constraint(a, pltpu.HBM) for a in far]
     return pl.pallas_call(
         begin_kernel,
-        in_specs=[pl.BlockSpec(memory_space=pltpu.HBM)],
-        out_specs=[pl.BlockSpec(memory_space=pltpu.VMEM)] * 3,
-        out_shape=[jax.ShapeDtypeStruct((2, latent.shape[2]), F32), edge, edge],
-        scratch_shapes=[pltpu.VMEM(latent.shape, BF16), pltpu.SemaphoreType.DMA((1,))],
+        in_specs=[pl.BlockSpec(memory_space=pltpu.HBM)] * 4,
+        out_specs=[pl.BlockSpec(memory_space=pltpu.VMEM)] * 4,
+        out_shape=[
+            pltpu.VMEM((2, latent.shape[2]), F32),
+            edge,
+            edge,
+            pltpu.VMEM((3,) + w_query.shape, BF16),
+        ],
+        scratch_shapes=[pltpu.VMEM(latent.shape, BF16), pltpu.SemaphoreType.DMA((4,))],
         name="begin",
-    )(pltpu.with_memory_space_constraint(latent, pltpu.HBM))
+    )(*far)
 
 
 def front_kernel(
-    sums_ref, vec_ref, before_ref, after_ref, latent_hbm, conv_hbm, wq_hbm, wk_hbm, wv_hbm,
-    hidden_ref, send_ref, shift_ref, latent_ref, conv_ref, w_ref, sems,
+    sums_ref, vec_ref, before_ref, after_ref, w_ref, latent_hbm, conv_hbm,
+    hidden_ref, send_ref, shift_ref, latent_ref, conv_ref, sems,
 ):
     copies = [pltpu.make_async_copy(latent_hbm, latent_ref, sems.at[0])]
     for i in range(3):
         copies.append(pltpu.make_async_copy(conv_hbm.at[i], conv_ref.at[i], sems.at[1 + i]))
-    for i, w_hbm in enumerate((wq_hbm, wk_hbm, wv_hbm)):
-        copies.append(pltpu.make_async_copy(w_hbm, w_ref.at[i], sems.at[4 + i]))
     for copy in copies:
         copy.start()
     chans = latent_ref.shape[2]
@@ -129,11 +141,8 @@
     spread = jnp.mean(values * values, axis=1, keepdims=True)
     normed = (values * lax.rsqrt(spread + 1e-05) * ln_gain + ln_bias).astype(BF16)
     scale = math.log2(math.e) / math.sqrt(HEAD_DIM)
-    copies[4].wait()
     query = (dot(normed, w_ref[0]) * scale).astype(BF16)
-    copies[5].wait()
     key = dot(normed, w_ref[1]).T.astype(BF16)
-    copies[6].wait()
     value = dot(normed, w_ref[2]).astype(BF16)
     for s in range(SETS):
         main, extra, part = 64 * s, 64 * (SETS + s // 4), 64 * (s % 4)
@@ -151,14 +160,14 @@
         )
 
 
-def front(sums, vec, before, after, latent, conv_weight, w_query, w_key, w_value):
+def front(sums, vec, before, after, weights, latent, conv_weight):
     chans = latent.shape[2]
-    far = [latent, conv_weight, w_query, w_key, w_value]
-    far = [pltpu.with_memory_space_constraint(a, pltpu.HBM) for a in far]
+    far = [pltpu.with_memory_space_constraint(a, pltpu.HBM) for a in (latent, conv_weight)]
+    near = pltpu.with_memory_space_constraint(weights, pltpu.VMEM)
     return pl.pallas_call(
         front_kernel,
-        in_specs=[pl.BlockSpec(memory_space=pltpu.VMEM)] * 4
-        + [pl.BlockSpec(memory_space=pltpu.HBM)] * 5,
+        in_specs=[pl.BlockSpec(memory_space=pltpu.VMEM)] * 5
+        + [pl.BlockSpec(memory_space=pltpu.HBM)] * 2,
         out_specs=[pl.BlockSpec(memory_space=pltpu.VMEM)] * 2,
         out_shape=[
             jax.ShapeDtypeStruct((256, chans), BF16),
@@ -168,12 +177,11 @@
             pltpu.VMEM((3, 512, chans), BF16),
             pltpu.VMEM(latent.shape, BF16),
             pltpu.VMEM(conv_weight.shape, BF16),
-            pltpu.VMEM((3, chans, chans), BF16),
-            pltpu.SemaphoreType.DMA((7,)),
+            pltpu.SemaphoreType.DMA((4,)),
         ],
         compiler_params=VMEM,
         name="front",
-    )(sums, vec, before, after, *far)
+    )(sums, vec, before, after, near, *far)
 
 
 def main_step(kv_ref, pair):
@@ -205,7 +213,7 @@
     if last:
         far_refs, refs = refs[:SETS], refs[SETS:]
     acc_ref = refs[0]
-    acc_ref[...] = jnp.zeros((2, tile, LANES), F32) if first else acc_in[...]
+    acc_ref[...] = jnp.zeros(acc_ref.shape, F32) if first else acc_in[...]
     query = q_ref[...].reshape(tile, LANES)
 
     steps = []
@@ -220,13 +228,15 @@
         if held is not None:
             held_kind, held_score, held_values = held
             weight = jnp.exp2(held_score).astype(BF16)
-            acc_ref[held_kind] += dot(weight, held_values)
+            update = dot(weight, held_values)
+            for i in range(tile // SPAN):
+                acc_ref[i, held_kind] += update[SPAN * i : SPAN * i + SPAN]
         held = None if step is None else (kind, score, values)
 
     if last:
         out_ref, store_ref, top_ref, sems = refs[1:]
         wide = lanes(tile)
-        total = jnp.where(wide < 64, acc_ref[1], acc_ref[0])
+        total = jnp.where(wide < 64, acc_ref[0, 1], acc_ref[0, 0])
         good = (jnp.min(total) > LOW) & (jnp.max(total) < HIGH)
         top_ref[...] = jnp.zeros((2, tile, LANES), F32)
 
@@ -237,7 +247,7 @@
                 here = store_ref.at[pl.ds(SETS * i, SETS)]
                 copies.append(pltpu.make_async_copy(far_ref, here, sems.at[i]))
                 copies[-1].start()
-            acc_ref[...] = jnp.zeros((2, tile, LANES), F32)
+            acc_ref[...] = jnp.zeros(acc_ref.shape, F32)
             top_ref[...] = jnp.full((2, tile, LANES), -1e30, F32)
             for copy in copies:
                 copy.wait()
@@ -248,7 +258,7 @@
                 top = jnp.maximum(top_ref[kind], jnp.max(score, axis=1, keepdims=True))
                 weight = jnp.exp2(score - top[:, 0:1]).astype(BF16)
                 factor = jnp.exp2(top_ref[kind] - top)
-                acc_ref[kind] = acc_ref[kind] * factor + dot(weight, values)
+                acc_ref[0, kind] = acc_ref[0, kind] * factor + dot(weight, values)
                 top_ref[kind] = top
 
             def pair_body(pair, carry):
@@ -262,7 +272,7 @@
             lax.fori_loop(0, SETS * SETS // 2, pair_body, 0)
             lax.fori_loop(0, SETS, block_body, 0)
 
-        main, extra = acc_ref[0], acc_ref[1]
+        main, extra = acc_ref[0, 0], acc_ref[0, 1]
         out = jnp.where(wide < 64, main, extra) / jnp.where(wide < 64, swap(main), swap(extra))
         out = out.astype(BF16)
         level = (jnp.log2(extra) + top_ref[1])[:, 0:1]
@@ -280,12 +290,12 @@
             out_ref[src, 256:272] = tail.astype(BF16)
 
 
-def fold(got, blocks, acc, every=None, tile=512):
+def fold(got, blocks, acc, every=None, tile=SPAN):
     first, last = acc is None, every is not None
-    acc_spec = pl.BlockSpec((2, tile, LANES), lambda t: (0, t, 0))
+    acc_spec = pl.BlockSpec((tile // SPAN, 2, SPAN, LANES), lambda t: (t, 0, 0, 0))
     kv_spec = pl.BlockSpec((SETS, KV_ROWS, LANES), lambda t: (0, 0, 0))
     out_specs = [acc_spec]
-    out_shape = [jax.ShapeDtypeStruct((2, TOKENS, LANES), F32)]
+    out_shape = [jax.ShapeDtypeStruct((TOKENS // SPAN, 2, SPAN, LANES), F32)]
     scratch = []
     if last:
         out_specs.append(pl.BlockSpec((tile // 256, BACK_ROWS, LANES), lambda t: (t, 0, 0)))
@@ -357,7 +367,7 @@
 ):
     rows_here, cols, chans = latent.shape
     width = chans // GROUPS
-    sums, last, first = begin(latent)
+    sums, last, first, weights = begin(latent, w_query, w_key, w_value)
     before, after = halo(last, first)
     sums = total_of(sums)
     sums = jnp.sum(sums.reshape(2, GROUPS, width), axis=2, keepdims=True)
@@ -368,9 +378,7 @@
     vec = jnp.where(row == 6, jnp.where(place < BANDS - 1, 1.0, 0.0), vec)
     for i, part in enumerate((gn_gain, gn_bias, conv_bias, ln_gain, ln_bias)):
         vec = jnp.where(row == i, part, vec)
-    hidden, send = front(
-        sums, vec, before, after, latent, conv_weight, w_query, w_key, w_value
-    )
+    hidden, send = front(sums, vec, before, after, weights, latent, conv_weight)
 
     got = lax.all_to_all(send, ("x", "z"), 0, 0)
     own = got[:, Q_ROWS:]

time: 255 us -> 255 us (level)
  transfers between devices with their start and end apart: 18 -> 18, of which waited for: 3 -> 3; matrix products, arithmetic and copies ran while one was open for 1% -> 0% of each run, Pallas kernels for 17% -> 17%
where the time goes in v5:
time: 255 us
  Pallas kernels  190 us (75%)
  blocking collectives  30.6 us (12%)
  starting transfers between devices  27.4 us (11%)
  waiting for transfers between devices  6.06 us (2%)
    pallas_call x7, Pallas kernels, fold(): pl.pallas_call(functools.partial(fold_kernel, len(blocks), tile, first, l...  180 us
    all_to_all x1, blocking collectives, on_device(): got = lax.all_to_all(send, ('x', 'z'), 0, 0)  17.9 us
    all_to_all x1, blocking collectives, on_device(): back = lax.all_to_all(out, ('x', 'z'), 0, 0)  12.6 us
    ppermute x9, starting transfers between devices, total_of(): parts.append(lax.ppermute(value, axis, perm))  12.5 us
    pallas_call x1, Pallas kernels, front(): pl.pallas_call(front_kernel, in_specs=[pl.BlockSpec(memory_space=pltpu.VM...  6.31 us
    ppermute x9, waiting for transfers between devices, total_of(): parts.append(lax.ppermute(value, axis, perm))  6.03 us
  transfers between devices with their start and end apart: 18, of which 3 were waited for; matrix products, arithmetic and copies ran while one was open for 0% of the time, Pallas kernels for 17%

profile of v5, /device:TPU:1, one launch (start us, length us, event | category | flops | bytes accessed | tf_op | source)
XLA Modules:
  0.0 255.1 jit_solution(8141644829923987148)
XLA Ops:
  0.0 0.0 copy-start.4
  0.0 0.0 copy-start.3
  0.0 0.0 copy-start.2
  0.0 0.0 copy-start.1
  0.0 0.0 copy-start
  0.0 2.5 begin.1
  2.6 3.6 %collective-permute-start.2 = (f32[2,640]{1,0:T(2,128)S(1)}, f32[2,640]{1,0:T(2,128)S(1)}, u32[]{:S(2)}, u32[]{:S(2)}) collective-permute-start(f32[2,640]{1,0:T(2,128)S(1)} %get-tuple-element.22), channel_id=1, source_target_pairs={{0,24},{8,0},{16,8},{24,16},{1,25},{9,1},{17,9},{25,17},{2,26},{10... | collective-permute-start | bytes 15368 | tf_op jit(solution)/shard_map/ppermute | solution.py:39
  6.2 0.3 collective-permute-start.1
  6.6 0.7 collective-permute-start
  7.3 4.9 %collective-permute-start.9 = (bf16[1,128,640]{2,1,0:T(8,128)(2,1)}, bf16[1,128,640]{2,1,0:T(8,128)(2,1)S(1)}, u32[]{:S(2)}, u32[]{:S(2)}) collective-permute-start(bf16[1,128,640]{2,1,0:T(8,128)(2,1)} %get-tuple-element.23), channel_id=1, source_target_pairs={{0,4},{4,8},{8,12},{12,16},{16,20},{20,24},{24,28},{28,32},{32,36}... | collective-permute-start | bytes 491528 | tf_op jit(solution)/shard_map/ppermute | solution.py:47
  12.2 1.9 collective-permute-start.10
  14.2 0.0 collective-permute-done.2
  14.2 0.0 collective-permute-done.1
  14.2 0.0 collective-permute-done
  14.2 0.1 collective-permute-start.5
  14.3 4.0 %collective-permute-start.4 = (f32[2,640]{1,0:T(2,128)S(1)}, f32[2,640]{1,0:T(2,128)S(1)}, u32[]{:S(2)}, u32[]{:S(2)}) collective-permute-start(f32[2,640]{1,0:T(2,128)S(1)} %add_add_fusion.2), channel_id=1, source_target_pairs={{0,32},{4,36},{32,0},{36,4},{1,33},{5,37},{33,1},{37,5},{2,34},{6,... | collective-permute-start | bytes 15368 | tf_op jit(solution)/shard_map/ppermute | solution.py:39
  18.3 0.1 collective-permute-start.3
  18.4 3.1 %collective-permute-done.5 = f32[2,640]{1,0:T(2,128)S(1)} collective-permute-done((f32[2,640]{1,0:T(2,128)S(1)}, f32[2,640]{1,0:T(2,128)S(1)}, u32[]{:S(2)}, u32[]{:S(2)}) %collective-permute-start.5) | collective-permute-done | bytes 5152 | tf_op jit(solution)/shard_map/ppermute | solution.py:39
  21.4 0.0 collective-permute-done.4
  21.4 0.0 collective-permute-done.3
  21.4 2.6 %collective-permute-start.8 = (f32[2,640]{1,0:T(2,128)S(1)}, f32[2,640]{1,0:T(2,128)S(1)}, u32[]{:S(2)}, u32[]{:S(2)}) collective-permute-start(f32[2,640]{1,0:T(2,128)S(1)} %add_add_fusion.1), channel_id=1, source_target_pairs={{0,192},{64,0},{128,64},{192,128},{1,193},{65,1},{129,65},{193,129... | collective-permute-start | bytes 15368 | tf_op jit(solution)/shard_map/ppermute | solution.py:39
  24.0 0.5 collective-permute-start.7
  24.5 0.6 collective-permute-start.6
  25.1 0.0 copy-done.4
  25.1 0.0 copy-done.3
  25.1 0.0 copy-done.2
  25.1 0.0 copy-done.1
  25.1 0.0 copy-done
  25.1 0.1 select_select_fusion.vec_ref
  25.2 0.0 collective-permute-done.8
  25.2 2.7 %collective-permute-done.7 = f32[2,640]{1,0:T(2,128)S(1)} collective-permute-done((f32[2,640]{1,0:T(2,128)S(1)}, f32[2,640]{1,0:T(2,128)S(1)}, u32[]{:S(2)}, u32[]{:S(2)}) %collective-permute-start.7) | collective-permute-done | bytes 5152 | tf_op jit(solution)/shard_map/ppermute | solution.py:39
  28.0 0.2 collective-permute-done.6
  28.2 0.1 reshape.10
  28.3 0.2 fusion
  28.5 0.1 reshape.11.sums_ref
  28.6 0.0 collective-permute-done.9.before_ref
  28.6 0.0 collective-permute-done.10.after_ref
  28.6 6.3 %front.1 = (bf16[256,640]{1,0:T(8,128)(2,1)S(1)}, bf16[8,576,128]{2,1,0:T(8,128)(2,1)S(1)}) custom-call(f32[2,640]{1,0:T(2,128)S(1)} %reshape.11.sums_ref, f32[8,640]{1,0:T(8,128)S(1)} %select_select_fusion.vec_ref, bf16[1,128,640]{2,1,0:T(8,128)(2,1)S(1)} %collective-permute-done.9.before_ref, bf16[1,128,640]{2,1,0:T(8,128)(2,1)S(1)} %collective-permute-done.10.after_ref, ...), custom_call_target="tpu_custom_call" | custom-call | tf_op jit(solution)/shard_map/front/pallas_call | solution.py:167
  34.9 17.9 %all_to_all.10.q_ref = bf16[8,576,128]{2,1,0:T(8,128)(2,1)S(1)} all-to-all(bf16[8,576,128]{2,1,0:T(8,128)(2,1)S(1)} %get-tuple-element.26), channel_id=1, replica_groups=mesh['x'=4,'z'=2,'y'=4,'core'=2,'img'=4] {'x','z'}, dimensions={0} | all-to-all | bytes 2359296 | tf_op jit(solution)/shard_map/all_to_all | solution.py:383
  52.9 3.4 %collective-permute-start.12 = (bf16[8,320,128]{2,1,0:T(8,128)(2,1)S(1)}, bf16[8,320,128]{2,1,0:T(8,128)(2,1)S(1)}, u32[]{:S(2)}, u32[]{:S(2)}) collective-permute-start(bf16[8,320,128]{2,1,0:T(8,128)(2,1)S(1)} %slice.4.refs_0_.refs_2_), channel_id=1, source_target_pairs={{0,4},{4,0},{8,12},{12,8},{16,20},{20,16},{24,28},{28,24},{1,5},{5... | collective-permute-start | bytes 1966088 | tf_op jit(solution)/shard_map/ppermute | solution.py:391
  56.3 0.0 collective-permute-start.11
  56.3 6.1 %fold.7.refs_1_ = f32[4,2,512,128]{3,2,1,0:T(8,128)S(1)} custom-call(bf16[8,576,128]{2,1,0:T(8,128)(2,1)S(1)} %all_to_all.10.q_ref, bf16[8,320,128]{2,1,0:T(8,128)(2,1)S(1)} %slice.4.refs_0_.refs_2_), custom_call_target="tpu_custom_call" | custom-call | tf_op jit(solution)/shard_map/fold/pallas_call | solution.py:308
  62.4 1.5 collective-permute-start.15
  63.9 0.0 collective-permute-done.12.refs_0_.refs_3_
  63.9 6.2 %fold.8.refs_1_ = f32[4,2,512,128]{3,2,1,0:T(8,128)S(1)} custom-call(bf16[8,576,128]{2,1,0:T(8,128)(2,1)S(1)} %all_to_all.10.q_ref, bf16[8,320,128]{2,1,0:T(8,128)(2,1)S(1)} %collective-permute-done.12.refs_0_.refs_3_, f32[4,2,512,128]{3,2,1,0:T(8,128)S(1)} %fold.7.refs_1_), custom_call_target="tpu_custom_call", output_to_operand_aliasing={{}: (2, {})} | custom-call | tf_op jit(solution)/shard_map/fold/pallas_call | solution.py:308
  70.1 0.0 collective-permute-done.11.refs_0_.refs_4_
  70.2 2.1 collective-permute-start.14
  72.3 6.3 %fold.9.refs_1_ = f32[4,2,512,128]{3,2,1,0:T(8,128)S(1)} custom-call(bf16[8,576,128]{2,1,0:T(8,128)(2,1)S(1)} %all_to_all.10.q_ref, bf16[8,320,128]{2,1,0:T(8,128)(2,1)S(1)} %collective-permute-done.11.refs_0_.refs_4_, f32[4,2,512,128]{3,2,1,0:T(8,128)S(1)} %fold.8.refs_1_), custom_call_target="tpu_custom_call", output_to_operand_aliasing={{}: (2, {})} | custom-call | tf_op jit(solution)/shard_map/fold/pallas_call | solution.py:308
  78.6 0.1 collective-permute-start.13
  78.7 0.0 collective-permute-done.15.refs_0_.refs_5_
  78.7 6.3 %fold.10.refs_1_ = f32[4,2,512,128]{3,2,1,0:T(8,128)S(1)} custom-call(bf16[8,576,128]{2,1,0:T(8,128)(2,1)S(1)} %all_to_all.10.q_ref, bf16[8,320,128]{2,1,0:T(8,128)(2,1)S(1)} %collective-permute-done.15.refs_0_.refs_5_, f32[4,2,512,128]{3,2,1,0:T(8,128)S(1)} %fold.9.refs_1_), custom_call_target="tpu_custom_call", output_to_operand_aliasing={{}: (2, {})} | custom-call | tf_op jit(solution)/shard_map/fold/pallas_call | solution.py:308
  85.0 0.3 collective-permute-start.17
  85.3 0.0 collective-permute-done.14.refs_0_.refs_6_
  85.3 6.2 %fold.11.refs_2_ = f32[4,2,512,128]{3,2,1,0:T(8,128)S(1)} custom-call(bf16[8,576,128]{2,1,0:T(8,128)(2,1)S(1)} %all_to_all.10.q_ref, bf16[8,320,128]{2,1,0:T(8,128)(2,1)S(1)} %collective-permute-done.14.refs_0_.refs_6_, f32[4,2,512,128]{3,2,1,0:T(8,128)S(1)} %fold.10.refs_1_), custom_call_target="tpu_custom_call", output_to_operand_aliasing={{}: (2, {})} | custom-call | tf_op jit(solution)/shard_map/fold/pallas_call | solution.py:308
  91.6 0.0 collective-permute-done.13.refs_1_.refs_8_
  91.6 0.6 collective-permute-start.16
  92.1 0.0 collective-permute-done.17.refs_0_.refs_7_
  92.1 12.2 %fold.12.refs_1_ = f32[4,2,512,128]{3,2,1,0:T(8,128)S(1)} custom-call(bf16[8,576,128]{2,1,0:T(8,128)(2,1)S(1)} %all_to_all.10.q_ref, bf16[8,320,128]{2,1,0:T(8,128)(2,1)S(1)} %collective-permute-done.17.refs_0_.refs_7_, bf16[8,320,128]{2,1,0:T(8,128)(2,1)S(1)} %collective-permute-done.13.refs_1_.refs_8_, ...), custom_call_target="tpu_custom_call", output_to_operand_aliasing={{}: (3, {})} | custom-call | tf_op jit(solution)/shard_map/fold/pallas_call | solution.py:308
  104.3 0.0 collective-permute-done.16.refs_0_.refs_9_
  104.4 136.7 %fold.13 = (f32[4,2,512,128]{3,2,1,0:T(8,128)S(1)}, bf16[8,272,128]{2,1,0:T(8,128)(2,1)S(1)}) custom-call(bf16[8,576,128]{2,1,0:T(8,128)(2,1)S(1)} %all_to_all.10.q_ref, bf16[8,320,128]{2,1,0:T(8,128)(2,1)S(1)} %collective-permute-done.16.refs_0_.refs_9_, f32[4,2,512,128]{3,2,1,0:T(8,128)S(1)} %fold.12.refs_1_, ...), custom_call_target="tpu_custom_call", output_to_operand_aliasing={{0}: (2, {})} | custom-call | tf_op jit(solution)/shard_map/fold/pallas_call | solution.py:308
  241.1 12.6 %all_to_all.11.back_ref = bf16[8,272,128]{2,1,0:T(8,128)(2,1)S(1)} all-to-all(bf16[8,272,128]{2,1,0:T(8,128)(2,1)S(1)} %get-tuple-element.37), channel_id=1, replica_groups=mesh['x'=4,'z'=2,'y'=4,'core'=2,'img'=4] {'x','z'}, dimensions={0} | all-to-all | bytes 1114112 | tf_op jit(solution)/shard_map/all_to_all | solution.py:412
  253.7 1.3 finish.1
  (8 shorter events, 0.1 us)
Async XLA Ops:
  0.0 25.1 %copy-start.4 = (f32[640]{0:T(1024)S(1)}, f32[640]{0:T(1024)}, u32[]{:S(2)}) copy-start(f32[640]{0:T(1024)} %param.16) | copy-start | bytes 7684
  0.0 25.1 %copy-start.3 = (f32[640]{0:T(1024)S(1)}, f32[640]{0:T(1024)}, u32[]{:S(2)}) copy-start(f32[640]{0:T(1024)} %param.15) | copy-start | bytes 7684
  0.0 25.1 %copy-start.2 = (f32[640]{0:T(1024)S(1)}, f32[640]{0:T(1024)}, u32[]{:S(2)}) copy-start(f32[640]{0:T(1024)} %param.14) | copy-start | bytes 7684
  0.0 25.1 %copy-start.1 = (f32[640]{0:T(1024)S(1)}, f32[640]{0:T(1024)}, u32[]{:S(2)}) copy-start(f32[640]{0:T(1024)} %param.12) | copy-start | bytes 7684
  0.0 25.1 %copy-start = (f32[640]{0:T(1024)S(1)}, f32[640]{0:T(1024)}, u32[]{:S(2)}) copy-start(f32[640]{0:T(1024)} %param.11) | copy-start | bytes 7684
  2.6 11.6 %collective-permute-start.2 = (f32[2,640]{1,0:T(2,128)S(1)}, f32[2,640]{1,0:T(2,128)S(1)}, u32[]{:S(2)}, u32[]{:S(2)}) collective-permute-start(f32[2,640]{1,0:T(2,128)S(1)} %get-tuple-element.22), channel_id=1, source_target_pairs={{0,24},{8,0},{16,8},{24,16},{1,25},{9,1},{17,9},{25,17},{2,26},{10... | collective-permute-start | bytes 15368 | tf_op jit(solution)/shard_map/ppermute | solution.py:39
  6.2 7.9 %collective-permute-start.1 = (f32[2,640]{1,0:T(2,128)S(1)}, f32[2,640]{1,0:T(2,128)S(1)}, u32[]{:S(2)}, u32[]{:S(2)}) collective-permute-start(f32[2,640]{1,0:T(2,128)S(1)} %get-tuple-element.22), channel_id=1, source_target_pairs={{0,16},{8,24},{16,0},{24,8},{1,17},{9,25},{17,1},{25,9},{2,18},{10... | collective-permute-start | bytes 15368 | tf_op jit(solution)/shard_map/ppermute | solution.py:39
  6.6 7.6 %collective-permute-start = (f32[2,640]{1,0:T(2,128)S(1)}, f32[2,640]{1,0:T(2,128)S(1)}, u32[]{:S(2)}, u32[]{:S(2)}) collective-permute-start(f32[2,640]{1,0:T(2,128)S(1)} %get-tuple-element.22), channel_id=1, source_target_pairs={{0,8},{8,16},{16,24},{24,0},{1,9},{9,17},{17,25},{25,1},{2,10},{10... | collective-permute-start | bytes 15368 | tf_op jit(solution)/shard_map/ppermute | solution.py:39
  7.3 21.3 %collective-permute-start.9 = (bf16[1,128,640]{2,1,0:T(8,128)(2,1)}, bf16[1,128,640]{2,1,0:T(8,128)(2,1)S(1)}, u32[]{:S(2)}, u32[]{:S(2)}) collective-permute-start(bf16[1,128,640]{2,1,0:T(8,128)(2,1)} %get-tuple-element.23), channel_id=1, source_target_pairs={{0,4},{4,8},{8,12},{12,16},{16,20},{20,24},{24,28},{28,32},{32,36}... | collective-permute-start | bytes 491528 | tf_op jit(solution)/shard_map/ppermute | solution.py:47
  12.2 16.4 %collective-permute-start.10 = (bf16[1,128,640]{2,1,0:T(8,128)(2,1)}, bf16[1,128,640]{2,1,0:T(8,128)(2,1)S(1)}, u32[]{:S(2)}, u32[]{:S(2)}) collective-permute-start(bf16[1,128,640]{2,1,0:T(8,128)(2,1)} %get-tuple-element.24), channel_id=1, source_target_pairs={{4,0},{8,4},{12,8},{16,12},{20,16},{24,20},{28,24},{32,28},{36,32}... | collective-permute-start | bytes 491528 | tf_op jit(solution)/shard_map/ppermute | solution.py:48
  14.2 7.2 %collective-permute-start.5 = (f32[2,640]{1,0:T(2,128)S(1)}, f32[2,640]{1,0:T(2,128)S(1)}, u32[]{:S(2)}, u32[]{:S(2)}) collective-permute-start(f32[2,640]{1,0:T(2,128)S(1)} %add_add_fusion.2), channel_id=1, source_target_pairs={{0,36},{4,0},{32,4},{36,32},{1,37},{5,1},{33,5},{37,33},{2,38},{6,... | collective-permute-start | bytes 15368 | tf_op jit(solution)/shard_map/ppermute | solution.py:39
  14.3 7.1 %collective-permute-start.4 = (f32[2,640]{1,0:T(2,128)S(1)}, f32[2,640]{1,0:T(2,128)S(1)}, u32[]{:S(2)}, u32[]{:S(2)}) collective-permute-start(f32[2,640]{1,0:T(2,128)S(1)} %add_add_fusion.2), channel_id=1, source_target_pairs={{0,32},{4,36},{32,0},{36,4},{1,33},{5,37},{33,1},{37,5},{2,34},{6,... | collective-permute-start | bytes 15368 | tf_op jit(solution)/shard_map/ppermute | solution.py:39
  18.3 3.1 %collective-permute-start.3 = (f32[2,640]{1,0:T(2,128)S(1)}, f32[2,640]{1,0:T(2,128)S(1)}, u32[]{:S(2)}, u32[]{:S(2)}) collective-permute-start(f32[2,640]{1,0:T(2,128)S(1)} %add_add_fusion.2), channel_id=1, source_target_pairs={{0,4},{4,32},{32,36},{36,0},{1,5},{5,33},{33,37},{37,1},{2,6},{6,3... | collective-permute-start | bytes 15368 | tf_op jit(solution)/shard_map/ppermute | solution.py:39
  21.4 3.8 %collective-permute-start.8 = (f32[2,640]{1,0:T(2,128)S(1)}, f32[2,640]{1,0:T(2,128)S(1)}, u32[]{:S(2)}, u32[]{:S(2)}) collective-permute-start(f32[2,640]{1,0:T(2,128)S(1)} %add_add_fusion.1), channel_id=1, source_target_pairs={{0,192},{64,0},{128,64},{192,128},{1,193},{65,1},{129,65},{193,129... | collective-permute-start | bytes 15368 | tf_op jit(solution)/shard_map/ppermute | solution.py:39
  24.0 4.0 %collective-permute-start.7 = (f32[2,640]{1,0:T(2,128)S(1)}, f32[2,640]{1,0:T(2,128)S(1)}, u32[]{:S(2)}, u32[]{:S(2)}) collective-permute-start(f32[2,640]{1,0:T(2,128)S(1)} %add_add_fusion.1), channel_id=1, source_target_pairs={{0,128},{64,192},{128,0},{192,64},{1,129},{65,193},{129,1},{193,65... | collective-permute-start | bytes 15368 | tf_op jit(solution)/shard_map/ppermute | solution.py:39
  24.5 3.7 %collective-permute-start.6 = (f32[2,640]{1,0:T(2,128)S(1)}, f32[2,640]{1,0:T(2,128)S(1)}, u32[]{:S(2)}, u32[]{:S(2)}) collective-permute-start(f32[2,640]{1,0:T(2,128)S(1)} %add_add_fusion.1), channel_id=1, source_target_pairs={{0,64},{64,128},{128,192},{192,0},{1,65},{65,129},{129,193},{193,1... | collective-permute-start | bytes 15368 | tf_op jit(solution)/shard_map/ppermute | solution.py:39
  52.9 11.0 %collective-permute-start.12 = (bf16[8,320,128]{2,1,0:T(8,128)(2,1)S(1)}, bf16[8,320,128]{2,1,0:T(8,128)(2,1)S(1)}, u32[]{:S(2)}, u32[]{:S(2)}) collective-permute-start(bf16[8,320,128]{2,1,0:T(8,128)(2,1)S(1)} %slice.4.refs_0_.refs_2_), channel_id=1, source_target_pairs={{0,4},{4,0},{8,12},{12,8},{16,20},{20,16},{24,28},{28,24},{1,5},{5... | collective-permute-start | bytes 1966088 | tf_op jit(solution)/shard_map/ppermute | solution.py:391
  56.3 13.9 %collective-permute-start.11 = (bf16[8,320,128]{2,1,0:T(8,128)(2,1)S(1)}, bf16[8,320,128]{2,1,0:T(8,128)(2,1)S(1)}, u32[]{:S(2)}, u32[]{:S(2)}) collective-permute-start(bf16[8,320,128]{2,1,0:T(8,128)(2,1)S(1)} %slice.4.refs_0_.refs_2_), channel_id=1, source_target_pairs={{0,8},{4,28},{8,16},{12,4},{16,24},{20,12},{24,0},{28,20},{1,9},{5... | collective-permute-start | bytes 1966088 | tf_op jit(solution)/shard_map/ppermute | solution.py:392
  62.4 16.3 %collective-permute-start.15 = (bf16[8,320,128]{2,1,0:T(8,128)(2,1)S(1)}, bf16[8,320,128]{2,1,0:T(8,128)(2,1)S(1)}, u32[]{:S(2)}, u32[]{:S(2)}) collective-permute-start(bf16[8,320,128]{2,1,0:T(8,128)(2,1)S(1)} %slice.4.refs_0_.refs_2_), channel_id=1, source_target_pairs={{8,0},{28,4},{16,8},{4,12},{24,16},{12,20},{0,24},{20,28},{9,1},{2... | collective-permute-start | bytes 1966088 | tf_op jit(solution)/shard_map/ppermute | solution.py:395
  70.2 15.2 %collective-permute-start.14 = (bf16[8,320,128]{2,1,0:T(8,128)(2,1)S(1)}, bf16[8,320,128]{2,1,0:T(8,128)(2,1)S(1)}, u32[]{:S(2)}, u32[]{:S(2)}) collective-permute-start(bf16[8,320,128]{2,1,0:T(8,128)(2,1)S(1)} %collective-permute-done.11.refs_0_.refs_4_), channel_id=1, source_target_pairs={{0,4},{4,0},{8,12},{12,8},{16,20},{20,16},{24,28},{28,24},{1,5},{5... | collective-permute-start | bytes 1966088 | tf_op jit(solution)/shard_map/ppermute | solution.py:398
  78.6 13.0 %collective-permute-start.13 = (bf16[8,320,128]{2,1,0:T(8,128)(2,1)S(1)}, bf16[8,320,128]{2,1,0:T(8,128)(2,1)S(1)}, u32[]{:S(2)}, u32[]{:S(2)}) collective-permute-start(bf16[8,320,128]{2,1,0:T(8,128)(2,1)S(1)} %collective-permute-done.11.refs_0_.refs_4_), channel_id=1, source_target_pairs={{0,8},{4,28},{8,16},{12,4},{16,24},{20,12},{24,0},{28,20},{1,9},{5... | collective-permute-start | bytes 1966088 | tf_op jit(solution)/shard_map/ppermute | solution.py:401
  85.0 7.1 %collective-permute-start.17 = (bf16[8,320,128]{2,1,0:T(8,128)(2,1)S(1)}, bf16[8,320,128]{2,1,0:T(8,128)(2,1)S(1)}, u32[]{:S(2)}, u32[]{:S(2)}) collective-permute-start(bf16[8,320,128]{2,1,0:T(8,128)(2,1)S(1)} %collective-permute-done.15.refs_0_.refs_5_), channel_id=1, source_target_pairs={{0,4},{4,0},{8,12},{12,8},{16,20},{20,16},{24,28},{28,24},{1,5},{5... | collective-permute-start | bytes 1966088 | tf_op jit(solution)/shard_map/ppermute | solution.py:404
  91.6 12.8 %collective-permute-start.16 = (bf16[8,320,128]{2,1,0:T(8,128)(2,1)S(1)}, bf16[8,320,128]{2,1,0:T(8,128)(2,1)S(1)}, u32[]{:S(2)}, u32[]{:S(2)}) collective-permute-start(bf16[8,320,128]{2,1,0:T(8,128)(2,1)S(1)} %collective-permute-done.13.refs_1_.refs_8_), channel_id=1, source_target_pairs={{0,4},{4,0},{8,12},{12,8},{16,20},{20,16},{24,28},{28,24},{1,5},{5... | collective-permute-start | bytes 1966088 | tf_op jit(solution)/shard_map/ppermute | solution.py:407

commit v6 on v4

--- a/solution.py
+++ b/solution.py
@@ -19,6 +19,7 @@
 BANDS = NX * NZ * NY * NC
 SPAN = 512
 TOKENS = 2048
+ACC = 1024
 LANES = 128
 Q_ROWS = 256
 KV_ROWS = 320
@@ -78,7 +79,7 @@
         begin_kernel,
         in_specs=[pl.BlockSpec(memory_space=pltpu.HBM)],
         out_specs=[pl.BlockSpec(memory_space=pltpu.VMEM)] * 3,
-        out_shape=[jax.ShapeDtypeStruct((2, latent.shape[2]), F32), edge, edge],
+        out_shape=[pltpu.VMEM((2, latent.shape[2]), F32), edge, edge],
         scratch_shapes=[pltpu.VMEM(latent.shape, BF16), pltpu.SemaphoreType.DMA((1,))],
         name="begin",
     )(pltpu.with_memory_space_constraint(latent, pltpu.HBM))
@@ -199,19 +200,31 @@
 
 
 def fold_kernel(count, tile, first, last, q_ref, *refs):
+    block = pl.program_id(1)
     kv_refs, refs = refs[:count], refs[count:]
     if not first:
         acc_in, refs = refs[0], refs[1:]
     if last:
         far_refs, refs = refs[:SETS], refs[SETS:]
     acc_ref = refs[0]
-    acc_ref[...] = jnp.zeros((2, tile, LANES), F32) if first else acc_in[...]
+    if count == 1:
+        kv_ref = kv_refs[0]
+    else:
+        kv_ref = refs[-1]
+        for i in range(count):
+
+            @pl.when(block == i)
+            def _():
+                kv_ref[...] = kv_refs[i][...]
+
+    @pl.when(block == 0)
+    def _():
+        acc_ref[...] = jnp.zeros(acc_ref.shape, F32) if first else acc_in[...]
+
     query = q_ref[...].reshape(tile, LANES)
 
-    steps = []
-    for kv_ref in kv_refs:
-        steps += [functools.partial(main_step, kv_ref, pair) for pair in range(SETS // 2)]
-        steps.append(functools.partial(extra_step, kv_ref, 0))
+    steps = [functools.partial(main_step, kv_ref, pair) for pair in range(SETS // 2)]
+    steps.append(functools.partial(extra_step, kv_ref, 0))
     held = None
     for step in steps + [None]:
         if step is not None:
@@ -220,13 +233,13 @@
         if held is not None:
             held_kind, held_score, held_values = held
             weight = jnp.exp2(held_score).astype(BF16)
-            acc_ref[held_kind] += dot(weight, held_values)
+            acc_ref[0, held_kind] += dot(weight, held_values)
         held = None if step is None else (kind, score, values)
 
     if last:
         out_ref, store_ref, top_ref, sems = refs[1:]
         wide = lanes(tile)
-        total = jnp.where(wide < 64, acc_ref[1], acc_ref[0])
+        total = jnp.where(wide < 64, acc_ref[0, 1], acc_ref[0, 0])
         good = (jnp.min(total) > LOW) & (jnp.max(total) < HIGH)
         top_ref[...] = jnp.zeros((2, tile, LANES), F32)
 
@@ -237,7 +250,7 @@
                 here = store_ref.at[pl.ds(SETS * i, SETS)]
                 copies.append(pltpu.make_async_copy(far_ref, here, sems.at[i]))
                 copies[-1].start()
-            acc_ref[...] = jnp.zeros((2, tile, LANES), F32)
+            acc_ref[...] = jnp.zeros(acc_ref.shape, F32)
             top_ref[...] = jnp.full((2, tile, LANES), -1e30, F32)
             for copy in copies:
                 copy.wait()
@@ -248,7 +261,7 @@
                 top = jnp.maximum(top_ref[kind], jnp.max(score, axis=1, keepdims=True))
                 weight = jnp.exp2(score - top[:, 0:1]).astype(BF16)
                 factor = jnp.exp2(top_ref[kind] - top)
-                acc_ref[kind] = acc_ref[kind] * factor + dot(weight, values)
+                acc_ref[0, kind] = acc_ref[0, kind] * factor + dot(weight, values)
                 top_ref[kind] = top
 
             def pair_body(pair, carry):
@@ -262,7 +275,7 @@
             lax.fori_loop(0, SETS * SETS // 2, pair_body, 0)
             lax.fori_loop(0, SETS, block_body, 0)
 
-        main, extra = acc_ref[0], acc_ref[1]
+        main, extra = acc_ref[0, 0], acc_ref[0, 1]
         out = jnp.where(wide < 64, main, extra) / jnp.where(wide < 64, swap(main), swap(extra))
         out = out.astype(BF16)
         level = (jnp.log2(extra) + top_ref[1])[:, 0:1]
@@ -281,14 +294,15 @@
 
 
 def fold(got, blocks, acc, every=None, tile=512):
+    per = ACC // tile
     first, last = acc is None, every is not None
-    acc_spec = pl.BlockSpec((2, tile, LANES), lambda t: (0, t, 0))
-    kv_spec = pl.BlockSpec((SETS, KV_ROWS, LANES), lambda t: (0, 0, 0))
+    acc_spec = pl.BlockSpec((1, 2, tile, LANES), lambda t, b: (t // per, 0, t % per, 0))
+    kv_spec = pl.BlockSpec((SETS, KV_ROWS, LANES), lambda t, b: (0, 0, 0))
     out_specs = [acc_spec]
-    out_shape = [jax.ShapeDtypeStruct((2, TOKENS, LANES), F32)]
-    scratch = []
+    out_shape = [jax.ShapeDtypeStruct((TOKENS // ACC, 2, ACC, LANES), F32)]
+    scratch = [pltpu.VMEM(blocks[0].shape, BF16)] if len(blocks) > 1 else []
     if last:
-        out_specs.append(pl.BlockSpec((tile // 256, BACK_ROWS, LANES), lambda t: (t, 0, 0)))
+        out_specs.append(pl.BlockSpec((tile // 256, BACK_ROWS, LANES), lambda t, b: (t, 0, 0)))
         out_shape.append(jax.ShapeDtypeStruct((SETS, BACK_ROWS, LANES), BF16))
         scratch = [
             pltpu.VMEM((SETS * SETS, KV_ROWS, LANES), BF16),
@@ -297,8 +311,8 @@
         ]
     return pl.pallas_call(
         functools.partial(fold_kernel, len(blocks), tile, first, last),
-        grid=(TOKENS // tile,),
-        in_specs=[pl.BlockSpec((tile // 256, Q_ROWS, LANES), lambda t: (t, 0, 0))]
+        grid=(TOKENS // tile, len(blocks)),
+        in_specs=[pl.BlockSpec((tile // 256, Q_ROWS, LANES), lambda t, b: (t, 0, 0))]
         + [kv_spec] * len(blocks)
         + ([] if first else [acc_spec])
         + ([pl.BlockSpec(memory_space=pl.ANY)] * SETS if last else []),
@@ -388,16 +402,16 @@
     (acc,) = fold(got, [twin], acc)
     ahead, acc = tied((ahead, acc))
     ahead_twin = lax.ppermute(ahead, RING, cross)
-    (acc,) = fold(got, [ahead], acc, tile=1024)
+    (acc,) = fold(got, [ahead], acc)
     ahead, acc = tied((ahead, acc))
     far = lax.ppermute(ahead, RING, along)
     (acc,) = fold(got, [behind], acc, tile=1024)
     behind, acc = tied((behind, acc))
     behind_twin = lax.ppermute(behind, RING, cross)
-    (acc,) = fold(got, [ahead_twin], acc)
+    (acc,) = fold(got, [ahead_twin], acc, tile=1024)
     far, acc = tied((far, acc))
     far_twin = lax.ppermute(far, RING, cross)
-    (acc,) = fold(got, [behind_twin, far], acc)
+    (acc,) = fold(got, [behind_twin, far], acc, tile=1024)
     every = [own, twin, ahead, behind, ahead_twin, behind_twin, far, far_twin]
     unused, out = fold(got, [far_twin], acc, every)
 

time: 255 us -> 256 us (level)
  transfers between devices with their start and end apart: 18 -> 18, of which waited for: 3 -> 3; matrix products, arithmetic and copies ran while one was open for 1% -> 0% of each run, Pallas kernels for 17% -> 17%
where the time goes in v6:
time: 256 us
  Pallas kernels  191 us (75%)
  blocking collectives  30.6 us (12%)
  starting transfers between devices  27.4 us (11%)
  waiting for transfers between devices  5.34 us (2%)
    pallas_call x7, Pallas kernels, fold(): pl.pallas_call(functools.partial(fold_kernel, len(blocks), tile, first, l...  181 us
    all_to_all x1, blocking collectives, on_device(): got = lax.all_to_all(send, ('x', 'z'), 0, 0)  17.9 us
    all_to_all x1, blocking collectives, on_device(): back = lax.all_to_all(out, ('x', 'z'), 0, 0)  12.7 us
    ppermute x9, starting transfers between devices, total_of(): parts.append(lax.ppermute(value, axis, perm))  12.5 us
    pallas_call x1, Pallas kernels, front(): pl.pallas_call(front_kernel, in_specs=[pl.BlockSpec(memory_space=pltpu.VM...  6.88 us
    ppermute x9, waiting for transfers between devices, total_of(): parts.append(lax.ppermute(value, axis, perm))  5.31 us
  transfers between devices with their start and end apart: 18, of which 3 were waited for; matrix products, arithmetic and copies ran while one was open for 0% of the time, Pallas kernels for 17%

profile of v6, /device:TPU:1, one launch (start us, length us, event | category | flops | bytes accessed | tf_op | source)
XLA Modules:
  0.0 255.7 jit_solution(17238075590947383052)
XLA Ops:
  0.0 1.7 begin.1
  1.7 3.6 %collective-permute-start.2 = (f32[2,640]{1,0:T(2,128)S(1)}, f32[2,640]{1,0:T(2,128)S(1)}, u32[]{:S(2)}, u32[]{:S(2)}) collective-permute-start(f32[2,640]{1,0:T(2,128)S(1)} %get-tuple-element.21), channel_id=1, source_target_pairs={{0,24},{8,0},{16,8},{24,16},{1,25},{9,1},{17,9},{25,17},{2,26},{10... | collective-permute-start | bytes 15368 | tf_op jit(solution)/shard_map/ppermute | solution.py:40
  5.4 0.3 collective-permute-start.1
  5.7 0.7 collective-permute-start
  6.4 4.9 %collective-permute-start.9 = (bf16[1,128,640]{2,1,0:T(8,128)(2,1)}, bf16[1,128,640]{2,1,0:T(8,128)(2,1)S(1)}, u32[]{:S(2)}, u32[]{:S(2)}) collective-permute-start(bf16[1,128,640]{2,1,0:T(8,128)(2,1)} %get-tuple-element.22), channel_id=1, source_target_pairs={{0,4},{4,8},{8,12},{12,16},{16,20},{20,24},{24,28},{28,32},{32,36}... | collective-permute-start | bytes 491528 | tf_op jit(solution)/shard_map/ppermute | solution.py:48
  11.3 1.9 collective-permute-start.10
  13.3 0.0 collective-permute-done.2
  13.3 0.0 collective-permute-done.1
  13.3 0.0 collective-permute-done
  13.3 0.1 collective-permute-start.5
  13.4 4.0 %collective-permute-start.4 = (f32[2,640]{1,0:T(2,128)S(1)}, f32[2,640]{1,0:T(2,128)S(1)}, u32[]{:S(2)}, u32[]{:S(2)}) collective-permute-start(f32[2,640]{1,0:T(2,128)S(1)} %add_add_fusion.2), channel_id=1, source_target_pairs={{0,32},{4,36},{32,0},{36,4},{1,33},{5,37},{33,1},{37,5},{2,34},{6,... | collective-permute-start | bytes 15368 | tf_op jit(solution)/shard_map/ppermute | solution.py:40
  17.4 0.1 collective-permute-start.3
  17.5 3.1 %collective-permute-done.5 = f32[2,640]{1,0:T(2,128)S(1)} collective-permute-done((f32[2,640]{1,0:T(2,128)S(1)}, f32[2,640]{1,0:T(2,128)S(1)}, u32[]{:S(2)}, u32[]{:S(2)}) %collective-permute-start.5) | collective-permute-done | bytes 5152 | tf_op jit(solution)/shard_map/ppermute | solution.py:40
  20.6 0.0 collective-permute-done.4
  20.6 0.0 collective-permute-done.3
  20.6 2.6 collective-permute-start.8
  23.1 0.5 collective-permute-start.7
  23.7 0.6 collective-permute-start.6
  24.3 0.8 select_select_fusion.vec_ref
  25.1 0.0 collective-permute-done.8
  25.1 2.0 collective-permute-done.7
  27.1 0.2 collective-permute-done.6
  27.3 0.1 reshape.10
  27.4 0.2 fusion
  27.6 0.1 reshape.11.sums_ref
  27.7 0.0 collective-permute-done.9.before_ref
  27.7 0.0 collective-permute-done.10.after_ref
  27.7 6.9 %front.1 = (bf16[256,640]{1,0:T(8,128)(2,1)S(1)}, bf16[8,576,128]{2,1,0:T(8,128)(2,1)S(1)}) custom-call(f32[2,640]{1,0:T(2,128)S(1)} %reshape.11.sums_ref, f32[8,640]{1,0:T(8,128)S(1)} %select_select_fusion.vec_ref, bf16[1,128,640]{2,1,0:T(8,128)(2,1)S(1)} %collective-permute-done.9.before_ref, bf16[1,128,640]{2,1,0:T(8,128)(2,1)S(1)} %collective-permute-done.10.after_ref, ...), custom_call_target="tpu_custom_call" | custom-call | tf_op jit(solution)/shard_map/front/pallas_call | solution.py:159
  34.6 17.9 %all_to_all.10.q_ref = bf16[8,576,128]{2,1,0:T(8,128)(2,1)S(1)} all-to-all(bf16[8,576,128]{2,1,0:T(8,128)(2,1)S(1)} %get-tuple-element.24), channel_id=1, replica_groups=mesh['x'=4,'z'=2,'y'=4,'core'=2,'img'=4] {'x','z'}, dimensions={0} | all-to-all | bytes 2359296 | tf_op jit(solution)/shard_map/all_to_all | solution.py:389
  52.6 3.6 %collective-permute-start.12 = (bf16[8,320,128]{2,1,0:T(8,128)(2,1)S(1)}, bf16[8,320,128]{2,1,0:T(8,128)(2,1)S(1)}, u32[]{:S(2)}, u32[]{:S(2)}) collective-permute-start(bf16[8,320,128]{2,1,0:T(8,128)(2,1)S(1)} %slice.4.refs_0_.refs_2_), channel_id=1, source_target_pairs={{0,4},{4,0},{8,12},{12,8},{16,20},{20,16},{24,28},{28,24},{1,5},{5... | collective-permute-start | bytes 1966088 | tf_op jit(solution)/shard_map/ppermute | solution.py:397
  56.2 0.0 collective-permute-start.11
  56.2 6.3 %fold.7.refs_1_ = f32[2,2,1024,128]{3,2,1,0:T(8,128)S(1)} custom-call(bf16[8,576,128]{2,1,0:T(8,128)(2,1)S(1)} %all_to_all.10.q_ref, bf16[8,320,128]{2,1,0:T(8,128)(2,1)S(1)} %slice.4.refs_0_.refs_2_), custom_call_target="tpu_custom_call" | custom-call | tf_op jit(solution)/shard_map/fold/pallas_call | solution.py:312
  62.5 1.5 collective-permute-start.15
  64.0 0.0 collective-permute-done.12.refs_0_.refs_3_
  64.1 6.5 %fold.8.refs_1_ = f32[2,2,1024,128]{3,2,1,0:T(8,128)S(1)} custom-call(bf16[8,576,128]{2,1,0:T(8,128)(2,1)S(1)} %all_to_all.10.q_ref, bf16[8,320,128]{2,1,0:T(8,128)(2,1)S(1)} %collective-permute-done.12.refs_0_.refs_3_, f32[2,2,1024,128]{3,2,1,0:T(8,128)S(1)} %fold.7.refs_1_), custom_call_target="tpu_custom_call", output_to_operand_aliasing={{}: (2, {})} | custom-call | tf_op jit(solution)/shard_map/fold/pallas_call | solution.py:312
  70.6 0.0 collective-permute-done.11.refs_0_.refs_4_
  70.6 1.9 collective-permute-start.14
  72.5 6.5 %fold.9.refs_1_ = f32[2,2,1024,128]{3,2,1,0:T(8,128)S(1)} custom-call(bf16[8,576,128]{2,1,0:T(8,128)(2,1)S(1)} %all_to_all.10.q_ref, bf16[8,320,128]{2,1,0:T(8,128)(2,1)S(1)} %collective-permute-done.11.refs_0_.refs_4_, f32[2,2,1024,128]{3,2,1,0:T(8,128)S(1)} %fold.8.refs_1_), custom_call_target="tpu_custom_call", output_to_operand_aliasing={{}: (2, {})} | custom-call | tf_op jit(solution)/shard_map/fold/pallas_call | solution.py:312
  79.0 0.1 collective-permute-start.13
  79.1 0.0 collective-permute-done.15.refs_0_.refs_5_
  79.1 6.0 %fold.10.refs_1_ = f32[2,2,1024,128]{3,2,1,0:T(8,128)S(1)} custom-call(bf16[8,576,128]{2,1,0:T(8,128)(2,1)S(1)} %all_to_all.10.q_ref, bf16[8,320,128]{2,1,0:T(8,128)(2,1)S(1)} %collective-permute-done.15.refs_0_.refs_5_, f32[2,2,1024,128]{3,2,1,0:T(8,128)S(1)} %fold.9.refs_1_), custom_call_target="tpu_custom_call", output_to_operand_aliasing={{}: (2, {})} | custom-call | tf_op jit(solution)/shard_map/fold/pallas_call | solution.py:312
  85.2 0.3 collective-permute-start.17
  85.5 0.0 collective-permute-done.14.refs_0_.refs_6_
  85.5 6.0 %fold.11.refs_2_ = f32[2,2,1024,128]{3,2,1,0:T(8,128)S(1)} custom-call(bf16[8,576,128]{2,1,0:T(8,128)(2,1)S(1)} %all_to_all.10.q_ref, bf16[8,320,128]{2,1,0:T(8,128)(2,1)S(1)} %collective-permute-done.14.refs_0_.refs_6_, f32[2,2,1024,128]{3,2,1,0:T(8,128)S(1)} %fold.10.refs_1_), custom_call_target="tpu_custom_call", output_to_operand_aliasing={{}: (2, {})} | custom-call | tf_op jit(solution)/shard_map/fold/pallas_call | solution.py:312
  91.5 0.0 collective-permute-done.13.refs_1_.refs_8_
  91.5 0.6 collective-permute-start.16
  92.1 0.0 collective-permute-done.17.refs_0_.refs_7_
  92.1 12.0 %fold.12.refs_1_ = f32[2,2,1024,128]{3,2,1,0:T(8,128)S(1)} custom-call(bf16[8,576,128]{2,1,0:T(8,128)(2,1)S(1)} %all_to_all.10.q_ref, bf16[8,320,128]{2,1,0:T(8,128)(2,1)S(1)} %collective-permute-done.17.refs_0_.refs_7_, bf16[8,320,128]{2,1,0:T(8,128)(2,1)S(1)} %collective-permute-done.13.refs_1_.refs_8_, ...), custom_call_target="tpu_custom_call", output_to_operand_aliasing={{}: (3, {})} | custom-call | tf_op jit(solution)/shard_map/fold/pallas_call | solution.py:312
  104.1 0.0 collective-permute-done.16.refs_0_.refs_9_
  104.1 137.5 %fold.13 = (f32[2,2,1024,128]{3,2,1,0:T(8,128)S(1)}, bf16[8,272,128]{2,1,0:T(8,128)(2,1)S(1)}) custom-call(bf16[8,576,128]{2,1,0:T(8,128)(2,1)S(1)} %all_to_all.10.q_ref, bf16[8,320,128]{2,1,0:T(8,128)(2,1)S(1)} %collective-permute-done.16.refs_0_.refs_9_, f32[2,2,1024,128]{3,2,1,0:T(8,128)S(1)} %fold.12.refs_1_, ...), custom_call_target="tpu_custom_call", output_to_operand_aliasing={{0}: (2, {})} | custom-call | tf_op jit(solution)/shard_map/fold/pallas_call | solution.py:312
  241.7 12.7 %all_to_all.11.back_ref = bf16[8,272,128]{2,1,0:T(8,128)(2,1)S(1)} all-to-all(bf16[8,272,128]{2,1,0:T(8,128)(2,1)S(1)} %get-tuple-element.35), channel_id=1, replica_groups=mesh['x'=4,'z'=2,'y'=4,'core'=2,'img'=4] {'x','z'}, dimensions={0} | all-to-all | bytes 1114112 | tf_op jit(solution)/shard_map/all_to_all | solution.py:418
  254.4 1.3 finish.1
  (8 shorter events, 0.1 us)
Async XLA Ops:
  1.7 11.6 %collective-permute-start.2 = (f32[2,640]{1,0:T(2,128)S(1)}, f32[2,640]{1,0:T(2,128)S(1)}, u32[]{:S(2)}, u32[]{:S(2)}) collective-permute-start(f32[2,640]{1,0:T(2,128)S(1)} %get-tuple-element.21), channel_id=1, source_target_pairs={{0,24},{8,0},{16,8},{24,16},{1,25},{9,1},{17,9},{25,17},{2,26},{10... | collective-permute-start | bytes 15368 | tf_op jit(solution)/shard_map/ppermute | solution.py:40
  5.4 7.9 %collective-permute-start.1 = (f32[2,640]{1,0:T(2,128)S(1)}, f32[2,640]{1,0:T(2,128)S(1)}, u32[]{:S(2)}, u32[]{:S(2)}) collective-permute-start(f32[2,640]{1,0:T(2,128)S(1)} %get-tuple-element.21), channel_id=1, source_target_pairs={{0,16},{8,24},{16,0},{24,8},{1,17},{9,25},{17,1},{25,9},{2,18},{10... | collective-permute-start | bytes 15368 | tf_op jit(solution)/shard_map/ppermute | solution.py:40
  5.7 7.6 %collective-permute-start = (f32[2,640]{1,0:T(2,128)S(1)}, f32[2,640]{1,0:T(2,128)S(1)}, u32[]{:S(2)}, u32[]{:S(2)}) collective-permute-start(f32[2,640]{1,0:T(2,128)S(1)} %get-tuple-element.21), channel_id=1, source_target_pairs={{0,8},{8,16},{16,24},{24,0},{1,9},{9,17},{17,25},{25,1},{2,10},{10... | collective-permute-start | bytes 15368 | tf_op jit(solution)/shard_map/ppermute | solution.py:40
  6.4 21.3 %collective-permute-start.9 = (bf16[1,128,640]{2,1,0:T(8,128)(2,1)}, bf16[1,128,640]{2,1,0:T(8,128)(2,1)S(1)}, u32[]{:S(2)}, u32[]{:S(2)}) collective-permute-start(bf16[1,128,640]{2,1,0:T(8,128)(2,1)} %get-tuple-element.22), channel_id=1, source_target_pairs={{0,4},{4,8},{8,12},{12,16},{16,20},{20,24},{24,28},{28,32},{32,36}... | collective-permute-start | bytes 491528 | tf_op jit(solution)/shard_map/ppermute | solution.py:48
  11.3 16.4 %collective-permute-start.10 = (bf16[1,128,640]{2,1,0:T(8,128)(2,1)}, bf16[1,128,640]{2,1,0:T(8,128)(2,1)S(1)}, u32[]{:S(2)}, u32[]{:S(2)}) collective-permute-start(bf16[1,128,640]{2,1,0:T(8,128)(2,1)} %get-tuple-element.23), channel_id=1, source_target_pairs={{4,0},{8,4},{12,8},{16,12},{20,16},{24,20},{28,24},{32,28},{36,32}... | collective-permute-start | bytes 491528 | tf_op jit(solution)/shard_map/ppermute | solution.py:49
  13.3 7.2 %collective-permute-start.5 = (f32[2,640]{1,0:T(2,128)S(1)}, f32[2,640]{1,0:T(2,128)S(1)}, u32[]{:S(2)}, u32[]{:S(2)}) collective-permute-start(f32[2,640]{1,0:T(2,128)S(1)} %add_add_fusion.2), channel_id=1, source_target_pairs={{0,36},{4,0},{32,4},{36,32},{1,37},{5,1},{33,5},{37,33},{2,38},{6,... | collective-permute-start | bytes 15368 | tf_op jit(solution)/shard_map/ppermute | solution.py:40
  13.4 7.1 %collective-permute-start.4 = (f32[2,640]{1,0:T(2,128)S(1)}, f32[2,640]{1,0:T(2,128)S(1)}, u32[]{:S(2)}, u32[]{:S(2)}) collective-permute-start(f32[2,640]{1,0:T(2,128)S(1)} %add_add_fusion.2), channel_id=1, source_target_pairs={{0,32},{4,36},{32,0},{36,4},{1,33},{5,37},{33,1},{37,5},{2,34},{6,... | collective-permute-start | bytes 15368 | tf_op jit(solution)/shard_map/ppermute | solution.py:40
  17.4 3.1 %collective-permute-start.3 = (f32[2,640]{1,0:T(2,128)S(1)}, f32[2,640]{1,0:T(2,128)S(1)}, u32[]{:S(2)}, u32[]{:S(2)}) collective-permute-start(f32[2,640]{1,0:T(2,128)S(1)} %add_add_fusion.2), channel_id=1, source_target_pairs={{0,4},{4,32},{32,36},{36,0},{1,5},{5,33},{33,37},{37,1},{2,6},{6,3... | collective-permute-start | bytes 15368 | tf_op jit(solution)/shard_map/ppermute | solution.py:40
  20.6 4.5 %collective-permute-start.8 = (f32[2,640]{1,0:T(2,128)S(1)}, f32[2,640]{1,0:T(2,128)S(1)}, u32[]{:S(2)}, u32[]{:S(2)}) collective-permute-start(f32[2,640]{1,0:T(2,128)S(1)} %add_add_fusion.1), channel_id=1, source_target_pairs={{0,192},{64,0},{128,64},{192,128},{1,193},{65,1},{129,65},{193,129... | collective-permute-start | bytes 15368 | tf_op jit(solution)/shard_map/ppermute | solution.py:40
  23.1 4.0 %collective-permute-start.7 = (f32[2,640]{1,0:T(2,128)S(1)}, f32[2,640]{1,0:T(2,128)S(1)}, u32[]{:S(2)}, u32[]{:S(2)}) collective-permute-start(f32[2,640]{1,0:T(2,128)S(1)} %add_add_fusion.1), channel_id=1, source_target_pairs={{0,128},{64,192},{128,0},{192,64},{1,129},{65,193},{129,1},{193,65... | collective-permute-start | bytes 15368 | tf_op jit(solution)/shard_map/ppermute | solution.py:40
  23.7 3.7 %collective-permute-start.6 = (f32[2,640]{1,0:T(2,128)S(1)}, f32[2,640]{1,0:T(2,128)S(1)}, u32[]{:S(2)}, u32[]{:S(2)}) collective-permute-start(f32[2,640]{1,0:T(2,128)S(1)} %add_add_fusion.1), channel_id=1, source_target_pairs={{0,64},{64,128},{128,192},{192,0},{1,65},{65,129},{129,193},{193,1... | collective-permute-start | bytes 15368 | tf_op jit(solution)/shard_map/ppermute | solution.py:40
  52.6 11.4 %collective-permute-start.12 = (bf16[8,320,128]{2,1,0:T(8,128)(2,1)S(1)}, bf16[8,320,128]{2,1,0:T(8,128)(2,1)S(1)}, u32[]{:S(2)}, u32[]{:S(2)}) collective-permute-start(bf16[8,320,128]{2,1,0:T(8,128)(2,1)S(1)} %slice.4.refs_0_.refs_2_), channel_id=1, source_target_pairs={{0,4},{4,0},{8,12},{12,8},{16,20},{20,16},{24,28},{28,24},{1,5},{5... | collective-permute-start | bytes 1966088 | tf_op jit(solution)/shard_map/ppermute | solution.py:397
  56.2 14.4 %collective-permute-start.11 = (bf16[8,320,128]{2,1,0:T(8,128)(2,1)S(1)}, bf16[8,320,128]{2,1,0:T(8,128)(2,1)S(1)}, u32[]{:S(2)}, u32[]{:S(2)}) collective-permute-start(bf16[8,320,128]{2,1,0:T(8,128)(2,1)S(1)} %slice.4.refs_0_.refs_2_), channel_id=1, source_target_pairs={{0,8},{4,28},{8,16},{12,4},{16,24},{20,12},{24,0},{28,20},{1,9},{5... | collective-permute-start | bytes 1966088 | tf_op jit(solution)/shard_map/ppermute | solution.py:398
  62.5 16.6 %collective-permute-start.15 = (bf16[8,320,128]{2,1,0:T(8,128)(2,1)S(1)}, bf16[8,320,128]{2,1,0:T(8,128)(2,1)S(1)}, u32[]{:S(2)}, u32[]{:S(2)}) collective-permute-start(bf16[8,320,128]{2,1,0:T(8,128)(2,1)S(1)} %slice.4.refs_0_.refs_2_), channel_id=1, source_target_pairs={{8,0},{28,4},{16,8},{4,12},{24,16},{12,20},{0,24},{20,28},{9,1},{2... | collective-permute-start | bytes 1966088 | tf_op jit(solution)/shard_map/ppermute | solution.py:401
  70.6 14.9 %collective-permute-start.14 = (bf16[8,320,128]{2,1,0:T(8,128)(2,1)S(1)}, bf16[8,320,128]{2,1,0:T(8,128)(2,1)S(1)}, u32[]{:S(2)}, u32[]{:S(2)}) collective-permute-start(bf16[8,320,128]{2,1,0:T(8,128)(2,1)S(1)} %collective-permute-done.11.refs_0_.refs_4_), channel_id=1, source_target_pairs={{0,4},{4,0},{8,12},{12,8},{16,20},{20,16},{24,28},{28,24},{1,5},{5... | collective-permute-start | bytes 1966088 | tf_op jit(solution)/shard_map/ppermute | solution.py:404
  79.0 12.5 %collective-permute-start.13 = (bf16[8,320,128]{2,1,0:T(8,128)(2,1)S(1)}, bf16[8,320,128]{2,1,0:T(8,128)(2,1)S(1)}, u32[]{:S(2)}, u32[]{:S(2)}) collective-permute-start(bf16[8,320,128]{2,1,0:T(8,128)(2,1)S(1)} %collective-permute-done.11.refs_0_.refs_4_), channel_id=1, source_target_pairs={{0,8},{4,28},{8,16},{12,4},{16,24},{20,12},{24,0},{28,20},{1,9},{5... | collective-permute-start | bytes 1966088 | tf_op jit(solution)/shard_map/ppermute | solution.py:407
  85.2 6.9 %collective-permute-start.17 = (bf16[8,320,128]{2,1,0:T(8,128)(2,1)S(1)}, bf16[8,320,128]{2,1,0:T(8,128)(2,1)S(1)}, u32[]{:S(2)}, u32[]{:S(2)}) collective-permute-start(bf16[8,320,128]{2,1,0:T(8,128)(2,1)S(1)} %collective-permute-done.15.refs_0_.refs_5_), channel_id=1, source_target_pairs={{0,4},{4,0},{8,12},{12,8},{16,20},{20,16},{24,28},{28,24},{1,5},{5... | collective-permute-start | bytes 1966088 | tf_op jit(solution)/shard_map/ppermute | solution.py:410
  91.5 12.6 %collective-permute-start.16 = (bf16[8,320,128]{2,1,0:T(8,128)(2,1)S(1)}, bf16[8,320,128]{2,1,0:T(8,128)(2,1)S(1)}, u32[]{:S(2)}, u32[]{:S(2)}) collective-permute-start(bf16[8,320,128]{2,1,0:T(8,128)(2,1)S(1)} %collective-permute-done.13.refs_1_.refs_8_), channel_id=1, source_target_pairs={{0,4},{4,0},{8,12},{12,8},{16,20},{20,16},{24,28},{28,24},{1,5},{5... | collective-permute-start | bytes 1966088 | tf_op jit(solution)/shard_map/ppermute | solution.py:413

commit v7 on v6

--- a/solution.py
+++ b/solution.py
@@ -293,7 +293,7 @@
             out_ref[src, 256:272] = tail.astype(BF16)
 
 
-def fold(got, blocks, acc, every=None, tile=512):
+def fold(got, blocks, acc, every=None, tile=1024):
     per = ACC // tile
     first, last = acc is None, every is not None
     acc_spec = pl.BlockSpec((1, 2, tile, LANES), lambda t, b: (t // per, 0, t % per, 0))
@@ -396,22 +396,18 @@
     tied = lax.optimization_barrier
     twin = lax.ppermute(own, RING, cross)
     ahead = lax.ppermute(own, RING, along)
-    (acc,) = fold(got, [own], None)
-    own, acc = tied((own, acc))
     behind = lax.ppermute(own, RING, against)
-    (acc,) = fold(got, [twin], acc)
+    (acc,) = fold(got, [own, twin], None)
     ahead, acc = tied((ahead, acc))
     ahead_twin = lax.ppermute(ahead, RING, cross)
+    far = lax.ppermute(ahead, RING, along)
     (acc,) = fold(got, [ahead], acc)
-    ahead, acc = tied((ahead, acc))
-    far = lax.ppermute(ahead, RING, along)
-    (acc,) = fold(got, [behind], acc, tile=1024)
     behind, acc = tied((behind, acc))
     behind_twin = lax.ppermute(behind, RING, cross)
-    (acc,) = fold(got, [ahead_twin], acc, tile=1024)
+    (acc,) = fold(got, [behind, ahead_twin], acc)
     far, acc = tied((far, acc))
     far_twin = lax.ppermute(far, RING, cross)
-    (acc,) = fold(got, [behind_twin, far], acc, tile=1024)
+    (acc,) = fold(got, [behind_twin, far], acc)
     every = [own, twin, ahead, behind, ahead_twin, behind_twin, far, far_twin]
     unused, out = fold(got, [far_twin], acc, every)
 

time: 256 us -> 209 us (0.82)
  Pallas kernels: 191 us -> 141 us
  waiting for transfers between devices: 5.34 us -> 8.11 us
    pallas_call x7 -> x5, Pallas kernels: 181 us -> 131 us  [fold(): pl.pallas_call(functools.partial(fold_kernel, len(blocks), tile, first, l...]
  transfers between devices with their start and end apart: 18 -> 18, of which waited for: 3 -> 5; matrix products, arithmetic and copies ran while one was open for 0% -> 1% of each run, Pallas kernels for 17% -> 20%
where the time goes in v7:
time: 209 us; the launch traced here: 208 us
  Pallas kernels  141 us (67%)
  blocking collectives  30.6 us (15%)
  starting transfers between devices  27.4 us (13%)
  waiting for transfers between devices  8.11 us (4%)
    pallas_call x5, Pallas kernels, fold(): pl.pallas_call(functools.partial(fold_kernel, len(blocks), tile, first, l...  131 us
    all_to_all x1, blocking collectives, on_device(): got = lax.all_to_all(send, ('x', 'z'), 0, 0)  17.9 us
    all_to_all x1, blocking collectives, on_device(): back = lax.all_to_all(out, ('x', 'z'), 0, 0)  12.6 us
    ppermute x9, starting transfers between devices, total_of(): parts.append(lax.ppermute(value, axis, perm))  12.5 us
    pallas_call x1, Pallas kernels, front(): pl.pallas_call(front_kernel, in_specs=[pl.BlockSpec(memory_space=pltpu.VM...  6.88 us
    ppermute x9, waiting for transfers between devices, total_of(): parts.append(lax.ppermute(value, axis, perm))  5.31 us
    ppermute x1, starting transfers between devices, halo(): before = lax.ppermute(last, BAND, up)  4.9 us
  transfers between devices with their start and end apart: 18, of which 5 were waited for; matrix products, arithmetic and copies ran while one was open for 1% of the time, Pallas kernels for 20%

profile of v7, /device:TPU:1, one launch (start us, length us, event | category | flops | bytes accessed | tf_op | source)
XLA Modules:
  0.0 208.4 jit_solution(8595482463711368890)
XLA Ops:
  0.0 1.7 begin.1
  1.7 3.6 %collective-permute-start.2 = (f32[2,640]{1,0:T(2,128)S(1)}, f32[2,640]{1,0:T(2,128)S(1)}, u32[]{:S(2)}, u32[]{:S(2)}) collective-permute-start(f32[2,640]{1,0:T(2,128)S(1)} %get-tuple-element.17), channel_id=1, source_target_pairs={{0,24},{8,0},{16,8},{24,16},{1,25},{9,1},{17,9},{25,17},{2,26},{10... | collective-permute-start | bytes 15368 | tf_op jit(solution)/shard_map/ppermute | solution.py:40
  5.4 0.3 collective-permute-start.1
  5.7 0.7 collective-permute-start
  6.4 4.9 %collective-permute-start.9 = (bf16[1,128,640]{2,1,0:T(8,128)(2,1)}, bf16[1,128,640]{2,1,0:T(8,128)(2,1)S(1)}, u32[]{:S(2)}, u32[]{:S(2)}) collective-permute-start(bf16[1,128,640]{2,1,0:T(8,128)(2,1)} %get-tuple-element.18), channel_id=1, source_target_pairs={{0,4},{4,8},{8,12},{12,16},{16,20},{20,24},{24,28},{28,32},{32,36}... | collective-permute-start | bytes 491528 | tf_op jit(solution)/shard_map/ppermute | solution.py:48
  11.3 1.9 collective-permute-start.10
  13.3 0.0 collective-permute-done.2
  13.3 0.0 collective-permute-done.1
  13.3 0.0 collective-permute-done
  13.3 0.1 collective-permute-start.5
  13.4 4.0 %collective-permute-start.4 = (f32[2,640]{1,0:T(2,128)S(1)}, f32[2,640]{1,0:T(2,128)S(1)}, u32[]{:S(2)}, u32[]{:S(2)}) collective-permute-start(f32[2,640]{1,0:T(2,128)S(1)} %add_add_fusion.2), channel_id=1, source_target_pairs={{0,32},{4,36},{32,0},{36,4},{1,33},{5,37},{33,1},{37,5},{2,34},{6,... | collective-permute-start | bytes 15368 | tf_op jit(solution)/shard_map/ppermute | solution.py:40
  17.4 0.1 collective-permute-start.3
  17.5 3.1 %collective-permute-done.5 = f32[2,640]{1,0:T(2,128)S(1)} collective-permute-done((f32[2,640]{1,0:T(2,128)S(1)}, f32[2,640]{1,0:T(2,128)S(1)}, u32[]{:S(2)}, u32[]{:S(2)}) %collective-permute-start.5) | collective-permute-done | bytes 5152 | tf_op jit(solution)/shard_map/ppermute | solution.py:40
  20.6 0.0 collective-permute-done.4
  20.6 0.0 collective-permute-done.3
  20.6 2.6 %collective-permute-start.8 = (f32[2,640]{1,0:T(2,128)S(1)}, f32[2,640]{1,0:T(2,128)S(1)}, u32[]{:S(2)}, u32[]{:S(2)}) collective-permute-start(f32[2,640]{1,0:T(2,128)S(1)} %add_add_fusion.1), channel_id=1, source_target_pairs={{0,192},{64,0},{128,64},{192,128},{1,193},{65,1},{129,65},{193,129... | collective-permute-start | bytes 15368 | tf_op jit(solution)/shard_map/ppermute | solution.py:40
  23.1 0.5 collective-permute-start.7
  23.7 0.6 collective-permute-start.6
  24.3 0.8 select_select_fusion.vec_ref
  25.1 0.0 collective-permute-done.8
  25.1 2.0 collective-permute-done.7
  27.1 0.2 collective-permute-done.6
  27.3 0.1 reshape.10
  27.4 0.2 fusion
  27.6 0.1 reshape.11.sums_ref
  27.7 0.0 collective-permute-done.9.before_ref
  27.7 0.0 collective-permute-done.10.after_ref
  27.7 6.9 %front.1 = (bf16[256,640]{1,0:T(8,128)(2,1)S(1)}, bf16[8,576,128]{2,1,0:T(8,128)(2,1)S(1)}) custom-call(f32[2,640]{1,0:T(2,128)S(1)} %reshape.11.sums_ref, f32[8,640]{1,0:T(8,128)S(1)} %select_select_fusion.vec_ref, bf16[1,128,640]{2,1,0:T(8,128)(2,1)S(1)} %collective-permute-done.9.before_ref, bf16[1,128,640]{2,1,0:T(8,128)(2,1)S(1)} %collective-permute-done.10.after_ref, ...), custom_call_target="tpu_custom_call" | custom-call | tf_op jit(solution)/shard_map/front/pallas_call | solution.py:159
  34.6 17.9 %all_to_all.10.q_ref = bf16[8,576,128]{2,1,0:T(8,128)(2,1)S(1)} all-to-all(bf16[8,576,128]{2,1,0:T(8,128)(2,1)S(1)} %get-tuple-element.20), channel_id=1, replica_groups=mesh['x'=4,'z'=2,'y'=4,'core'=2,'img'=4] {'x','z'}, dimensions={0} | all-to-all | bytes 2359296 | tf_op jit(solution)/shard_map/all_to_all | solution.py:389
  52.6 3.6 %collective-permute-start.12 = (bf16[8,320,128]{2,1,0:T(8,128)(2,1)S(1)}, bf16[8,320,128]{2,1,0:T(8,128)(2,1)S(1)}, u32[]{:S(2)}, u32[]{:S(2)}) collective-permute-start(bf16[8,320,128]{2,1,0:T(8,128)(2,1)S(1)} %slice.4.refs_0_.refs_2_), channel_id=1, source_target_pairs={{0,4},{4,0},{8,12},{12,8},{16,20},{20,16},{24,28},{28,24},{1,5},{5... | collective-permute-start | bytes 1966088 | tf_op jit(solution)/shard_map/ppermute | solution.py:397
  56.2 0.0 collective-permute-start.11
  56.2 1.5 collective-permute-start.14
  57.6 0.3 collective-permute-done.12.refs_1_.refs_3_
  57.9 11.9 %fold.5.refs_1_ = f32[2,2,1024,128]{3,2,1,0:T(8,128)S(1)} custom-call(bf16[8,576,128]{2,1,0:T(8,128)(2,1)S(1)} %all_to_all.10.q_ref, bf16[8,320,128]{2,1,0:T(8,128)(2,1)S(1)} %slice.4.refs_0_.refs_2_, bf16[8,320,128]{2,1,0:T(8,128)(2,1)S(1)} %collective-permute-done.12.refs_1_.refs_3_), custom_call_target="tpu_custom_call" | custom-call | tf_op jit(solution)/shard_map/fold/pallas_call | solution.py:312
  69.8 2.5 %collective-permute-done.11.refs_0_.refs_4_ = bf16[8,320,128]{2,1,0:T(8,128)(2,1)S(1)} collective-permute-done((bf16[8,320,128]{2,1,0:T(8,128)(2,1)S(1)}, bf16[8,320,128]{2,1,0:T(8,128)(2,1)S(1)}, u32[]{:S(2)}, u32[]{:S(2)}) %collective-permute-start.11) | collective-permute-done | bytes 655392 | tf_op jit(solution)/shard_map/ppermute | solution.py:398
  72.3 2.2 %collective-permute-start.15 = (bf16[8,320,128]{2,1,0:T(8,128)(2,1)S(1)}, bf16[8,320,128]{2,1,0:T(8,128)(2,1)S(1)}, u32[]{:S(2)}, u32[]{:S(2)}) collective-permute-start(bf16[8,320,128]{2,1,0:T(8,128)(2,1)S(1)} %collective-permute-done.11.refs_0_.refs_4_), channel_id=1, source_target_pairs={{0,4},{4,0},{8,12},{12,8},{16,20},{20,16},{24,28},{28,24},{1,5},{5... | collective-permute-start | bytes 1966088 | tf_op jit(solution)/shard_map/ppermute | solution.py:402
  74.5 0.0 collective-permute-start.13
  74.5 6.0 %fold.6.refs_2_ = f32[2,2,1024,128]{3,2,1,0:T(8,128)S(1)} custom-call(bf16[8,576,128]{2,1,0:T(8,128)(2,1)S(1)} %all_to_all.10.q_ref, bf16[8,320,128]{2,1,0:T(8,128)(2,1)S(1)} %collective-permute-done.11.refs_0_.refs_4_, f32[2,2,1024,128]{3,2,1,0:T(8,128)S(1)} %fold.5.refs_1_), custom_call_target="tpu_custom_call", output_to_operand_aliasing={{}: (2, {})} | custom-call | tf_op jit(solution)/shard_map/fold/pallas_call | solution.py:312
  80.6 0.0 collective-permute-done.14.refs_0_.refs_5_
  80.6 0.3 collective-permute-start.17
  80.9 0.0 collective-permute-done.15.refs_1_.refs_6_
  80.9 12.1 %fold.7.refs_2_ = f32[2,2,1024,128]{3,2,1,0:T(8,128)S(1)} custom-call(bf16[8,576,128]{2,1,0:T(8,128)(2,1)S(1)} %all_to_all.10.q_ref, bf16[8,320,128]{2,1,0:T(8,128)(2,1)S(1)} %collective-permute-done.14.refs_0_.refs_5_, bf16[8,320,128]{2,1,0:T(8,128)(2,1)S(1)} %collective-permute-done.15.refs_1_.refs_6_, ...), custom_call_target="tpu_custom_call", output_to_operand_aliasing={{}: (3, {})} | custom-call | tf_op jit(solution)/shard_map/fold/pallas_call | solution.py:312
  93.0 0.0 collective-permute-done.13.refs_1_.refs_8_
  93.0 0.6 collective-permute-start.16
  93.5 0.0 collective-permute-done.17.refs_0_.refs_7_
  93.5 12.0 %fold.8.refs_1_ = f32[2,2,1024,128]{3,2,1,0:T(8,128)S(1)} custom-call(bf16[8,576,128]{2,1,0:T(8,128)(2,1)S(1)} %all_to_all.10.q_ref, bf16[8,320,128]{2,1,0:T(8,128)(2,1)S(1)} %collective-permute-done.17.refs_0_.refs_7_, bf16[8,320,128]{2,1,0:T(8,128)(2,1)S(1)} %collective-permute-done.13.refs_1_.refs_8_, ...), custom_call_target="tpu_custom_call", output_to_operand_aliasing={{}: (3, {})} | custom-call | tf_op jit(solution)/shard_map/fold/pallas_call | solution.py:312
  105.6 0.0 collective-permute-done.16.refs_0_.refs_9_
  105.6 88.9 %fold.9 = (f32[2,2,1024,128]{3,2,1,0:T(8,128)S(1)}, bf16[8,272,128]{2,1,0:T(8,128)(2,1)S(1)}) custom-call(bf16[8,576,128]{2,1,0:T(8,128)(2,1)S(1)} %all_to_all.10.q_ref, bf16[8,320,128]{2,1,0:T(8,128)(2,1)S(1)} %collective-permute-done.16.refs_0_.refs_9_, f32[2,2,1024,128]{3,2,1,0:T(8,128)S(1)} %fold.8.refs_1_, ...), custom_call_target="tpu_custom_call", output_to_operand_aliasing={{0}: (2, {})} | custom-call | tf_op jit(solution)/shard_map/fold/pallas_call | solution.py:312
  194.5 12.6 %all_to_all.11.back_ref = bf16[8,272,128]{2,1,0:T(8,128)(2,1)S(1)} all-to-all(bf16[8,272,128]{2,1,0:T(8,128)(2,1)S(1)} %get-tuple-element.27), channel_id=1, replica_groups=mesh['x'=4,'z'=2,'y'=4,'core'=2,'img'=4] {'x','z'}, dimensions={0} | all-to-all | bytes 1114112 | tf_op jit(solution)/shard_map/all_to_all | solution.py:414
  207.1 1.3 finish.1
  (8 shorter events, 0.1 us)
Async XLA Ops:
  1.7 11.6 %collective-permute-start.2 = (f32[2,640]{1,0:T(2,128)S(1)}, f32[2,640]{1,0:T(2,128)S(1)}, u32[]{:S(2)}, u32[]{:S(2)}) collective-permute-start(f32[2,640]{1,0:T(2,128)S(1)} %get-tuple-element.17), channel_id=1, source_target_pairs={{0,24},{8,0},{16,8},{24,16},{1,25},{9,1},{17,9},{25,17},{2,26},{10... | collective-permute-start | bytes 15368 | tf_op jit(solution)/shard_map/ppermute | solution.py:40
  5.4 7.9 %collective-permute-start.1 = (f32[2,640]{1,0:T(2,128)S(1)}, f32[2,640]{1,0:T(2,128)S(1)}, u32[]{:S(2)}, u32[]{:S(2)}) collective-permute-start(f32[2,640]{1,0:T(2,128)S(1)} %get-tuple-element.17), channel_id=1, source_target_pairs={{0,16},{8,24},{16,0},{24,8},{1,17},{9,25},{17,1},{25,9},{2,18},{10... | collective-permute-start | bytes 15368 | tf_op jit(solution)/shard_map/ppermute | solution.py:40
  5.7 7.6 %collective-permute-start = (f32[2,640]{1,0:T(2,128)S(1)}, f32[2,640]{1,0:T(2,128)S(1)}, u32[]{:S(2)}, u32[]{:S(2)}) collective-permute-start(f32[2,640]{1,0:T(2,128)S(1)} %get-tuple-element.17), channel_id=1, source_target_pairs={{0,8},{8,16},{16,24},{24,0},{1,9},{9,17},{17,25},{25,1},{2,10},{10... | collective-permute-start | bytes 15368 | tf_op jit(solution)/shard_map/ppermute | solution.py:40
  6.4 21.3 %collective-permute-start.9 = (bf16[1,128,640]{2,1,0:T(8,128)(2,1)}, bf16[1,128,640]{2,1,0:T(8,128)(2,1)S(1)}, u32[]{:S(2)}, u32[]{:S(2)}) collective-permute-start(bf16[1,128,640]{2,1,0:T(8,128)(2,1)} %get-tuple-element.18), channel_id=1, source_target_pairs={{0,4},{4,8},{8,12},{12,16},{16,20},{20,24},{24,28},{28,32},{32,36}... | collective-permute-start | bytes 491528 | tf_op jit(solution)/shard_map/ppermute | solution.py:48
  11.3 16.4 %collective-permute-start.10 = (bf16[1,128,640]{2,1,0:T(8,128)(2,1)}, bf16[1,128,640]{2,1,0:T(8,128)(2,1)S(1)}, u32[]{:S(2)}, u32[]{:S(2)}) collective-permute-start(bf16[1,128,640]{2,1,0:T(8,128)(2,1)} %get-tuple-element.19), channel_id=1, source_target_pairs={{4,0},{8,4},{12,8},{16,12},{20,16},{24,20},{28,24},{32,28},{36,32}... | collective-permute-start | bytes 491528 | tf_op jit(solution)/shard_map/ppermute | solution.py:49
  13.3 7.2 %collective-permute-start.5 = (f32[2,640]{1,0:T(2,128)S(1)}, f32[2,640]{1,0:T(2,128)S(1)}, u32[]{:S(2)}, u32[]{:S(2)}) collective-permute-start(f32[2,640]{1,0:T(2,128)S(1)} %add_add_fusion.2), channel_id=1, source_target_pairs={{0,36},{4,0},{32,4},{36,32},{1,37},{5,1},{33,5},{37,33},{2,38},{6,... | collective-permute-start | bytes 15368 | tf_op jit(solution)/shard_map/ppermute | solution.py:40
  13.4 7.1 %collective-permute-start.4 = (f32[2,640]{1,0:T(2,128)S(1)}, f32[2,640]{1,0:T(2,128)S(1)}, u32[]{:S(2)}, u32[]{:S(2)}) collective-permute-start(f32[2,640]{1,0:T(2,128)S(1)} %add_add_fusion.2), channel_id=1, source_target_pairs={{0,32},{4,36},{32,0},{36,4},{1,33},{5,37},{33,1},{37,5},{2,34},{6,... | collective-permute-start | bytes 15368 | tf_op jit(solution)/shard_map/ppermute | solution.py:40
  17.4 3.1 %collective-permute-start.3 = (f32[2,640]{1,0:T(2,128)S(1)}, f32[2,640]{1,0:T(2,128)S(1)}, u32[]{:S(2)}, u32[]{:S(2)}) collective-permute-start(f32[2,640]{1,0:T(2,128)S(1)} %add_add_fusion.2), channel_id=1, source_target_pairs={{0,4},{4,32},{32,36},{36,0},{1,5},{5,33},{33,37},{37,1},{2,6},{6,3... | collective-permute-start | bytes 15368 | tf_op jit(solution)/shard_map/ppermute | solution.py:40
  20.6 4.5 %collective-permute-start.8 = (f32[2,640]{1,0:T(2,128)S(1)}, f32[2,640]{1,0:T(2,128)S(1)}, u32[]{:S(2)}, u32[]{:S(2)}) collective-permute-start(f32[2,640]{1,0:T(2,128)S(1)} %add_add_fusion.1), channel_id=1, source_target_pairs={{0,192},{64,0},{128,64},{192,128},{1,193},{65,1},{129,65},{193,129... | collective-permute-start | bytes 15368 | tf_op jit(solution)/shard_map/ppermute | solution.py:40
  23.1 4.0 %collective-permute-start.7 = (f32[2,640]{1,0:T(2,128)S(1)}, f32[2,640]{1,0:T(2,128)S(1)}, u32[]{:S(2)}, u32[]{:S(2)}) collective-permute-start(f32[2,640]{1,0:T(2,128)S(1)} %add_add_fusion.1), channel_id=1, source_target_pairs={{0,128},{64,192},{128,0},{192,64},{1,129},{65,193},{129,1},{193,65... | collective-permute-start | bytes 15368 | tf_op jit(solution)/shard_map/ppermute | solution.py:40
  23.7 3.7 %collective-permute-start.6 = (f32[2,640]{1,0:T(2,128)S(1)}, f32[2,640]{1,0:T(2,128)S(1)}, u32[]{:S(2)}, u32[]{:S(2)}) collective-permute-start(f32[2,640]{1,0:T(2,128)S(1)} %add_add_fusion.1), channel_id=1, source_target_pairs={{0,64},{64,128},{128,192},{192,0},{1,65},{65,129},{129,193},{193,1... | collective-permute-start | bytes 15368 | tf_op jit(solution)/shard_map/ppermute | solution.py:40
  52.6 5.3 %collective-permute-start.12 = (bf16[8,320,128]{2,1,0:T(8,128)(2,1)S(1)}, bf16[8,320,128]{2,1,0:T(8,128)(2,1)S(1)}, u32[]{:S(2)}, u32[]{:S(2)}) collective-permute-start(bf16[8,320,128]{2,1,0:T(8,128)(2,1)S(1)} %slice.4.refs_0_.refs_2_), channel_id=1, source_target_pairs={{0,4},{4,0},{8,12},{12,8},{16,20},{20,16},{24,28},{28,24},{1,5},{5... | collective-permute-start | bytes 1966088 | tf_op jit(solution)/shard_map/ppermute | solution.py:397
  56.2 16.2 %collective-permute-start.11 = (bf16[8,320,128]{2,1,0:T(8,128)(2,1)S(1)}, bf16[8,320,128]{2,1,0:T(8,128)(2,1)S(1)}, u32[]{:S(2)}, u32[]{:S(2)}) collective-permute-start(bf16[8,320,128]{2,1,0:T(8,128)(2,1)S(1)} %slice.4.refs_0_.refs_2_), channel_id=1, source_target_pairs={{0,8},{4,28},{8,16},{12,4},{16,24},{20,12},{24,0},{28,20},{1,9},{5... | collective-permute-start | bytes 1966088 | tf_op jit(solution)/shard_map/ppermute | solution.py:398
  56.2 24.4 %collective-permute-start.14 = (bf16[8,320,128]{2,1,0:T(8,128)(2,1)S(1)}, bf16[8,320,128]{2,1,0:T(8,128)(2,1)S(1)}, u32[]{:S(2)}, u32[]{:S(2)}) collective-permute-start(bf16[8,320,128]{2,1,0:T(8,128)(2,1)S(1)} %slice.4.refs_0_.refs_2_), channel_id=1, source_target_pairs={{8,0},{28,4},{16,8},{4,12},{24,16},{12,20},{0,24},{20,28},{9,1},{2... | collective-permute-start | bytes 1966088 | tf_op jit(solution)/shard_map/ppermute | solution.py:399
  72.3 8.6 %collective-permute-start.15 = (bf16[8,320,128]{2,1,0:T(8,128)(2,1)S(1)}, bf16[8,320,128]{2,1,0:T(8,128)(2,1)S(1)}, u32[]{:S(2)}, u32[]{:S(2)}) collective-permute-start(bf16[8,320,128]{2,1,0:T(8,128)(2,1)S(1)} %collective-permute-done.11.refs_0_.refs_4_), channel_id=1, source_target_pairs={{0,4},{4,0},{8,12},{12,8},{16,20},{20,16},{24,28},{28,24},{1,5},{5... | collective-permute-start | bytes 1966088 | tf_op jit(solution)/shard_map/ppermute | solution.py:402
  74.5 18.4 %collective-permute-start.13 = (bf16[8,320,128]{2,1,0:T(8,128)(2,1)S(1)}, bf16[8,320,128]{2,1,0:T(8,128)(2,1)S(1)}, u32[]{:S(2)}, u32[]{:S(2)}) collective-permute-start(bf16[8,320,128]{2,1,0:T(8,128)(2,1)S(1)} %collective-permute-done.11.refs_0_.refs_4_), channel_id=1, source_target_pairs={{0,8},{4,28},{8,16},{12,4},{16,24},{20,12},{24,0},{28,20},{1,9},{5... | collective-permute-start | bytes 1966088 | tf_op jit(solution)/shard_map/ppermute | solution.py:403
  80.6 13.0 %collective-permute-start.17 = (bf16[8,320,128]{2,1,0:T(8,128)(2,1)S(1)}, bf16[8,320,128]{2,1,0:T(8,128)(2,1)S(1)}, u32[]{:S(2)}, u32[]{:S(2)}) collective-permute-start(bf16[8,320,128]{2,1,0:T(8,128)(2,1)S(1)} %collective-permute-done.14.refs_0_.refs_5_), channel_id=1, source_target_pairs={{0,4},{4,0},{8,12},{12,8},{16,20},{20,16},{24,28},{28,24},{1,5},{5... | collective-permute-start | bytes 1966088 | tf_op jit(solution)/shard_map/ppermute | solution.py:406
  93.0 12.6 %collective-permute-start.16 = (bf16[8,320,128]{2,1,0:T(8,128)(2,1)S(1)}, bf16[8,320,128]{2,1,0:T(8,128)(2,1)S(1)}, u32[]{:S(2)}, u32[]{:S(2)}) collective-permute-start(bf16[8,320,128]{2,1,0:T(8,128)(2,1)S(1)} %collective-permute-done.13.refs_1_.refs_8_), channel_id=1, source_target_pairs={{0,4},{4,0},{8,12},{12,8},{16,20},{20,16},{24,28},{28,24},{1,5},{5... | collective-permute-start | bytes 1966088 | tf_op jit(solution)/shard_map/ppermute | solution.py:409

commit v8 on v7

--- a/solution.py
+++ b/solution.py
@@ -237,60 +237,63 @@
         held = None if step is None else (kind, score, values)
 
     if last:
-        out_ref, store_ref, top_ref, sems = refs[1:]
-        wide = lanes(tile)
-        total = jnp.where(wide < 64, acc_ref[0, 1], acc_ref[0, 0])
-        good = (jnp.min(total) > LOW) & (jnp.max(total) < HIGH)
-        top_ref[...] = jnp.zeros((2, tile, LANES), F32)
-
-        @pl.when(jnp.logical_not(good))
+        out_ref, store_ref, top_ref, sems = refs[1:5]
+
+        @pl.when(block == count - 1)
         def _():
-            copies = []
-            for i, far_ref in enumerate(far_refs):
-                here = store_ref.at[pl.ds(SETS * i, SETS)]
-                copies.append(pltpu.make_async_copy(far_ref, here, sems.at[i]))
-                copies[-1].start()
-            acc_ref[...] = jnp.zeros(acc_ref.shape, F32)
-            top_ref[...] = jnp.full((2, tile, LANES), -1e30, F32)
-            for copy in copies:
-                copy.wait()
-
-            def online(step):
-                kind, keys, values = step
-                score = dot(query, keys)
-                top = jnp.maximum(top_ref[kind], jnp.max(score, axis=1, keepdims=True))
-                weight = jnp.exp2(score - top[:, 0:1]).astype(BF16)
-                factor = jnp.exp2(top_ref[kind] - top)
-                acc_ref[0, kind] = acc_ref[0, kind] * factor + dot(weight, values)
-                top_ref[kind] = top
-
-            def pair_body(pair, carry):
-                online(main_step(store_ref, pair))
-                return carry
-
-            def block_body(block, carry):
-                online(extra_step(store_ref, block))
-                return carry
-
-            lax.fori_loop(0, SETS * SETS // 2, pair_body, 0)
-            lax.fori_loop(0, SETS, block_body, 0)
-
-        main, extra = acc_ref[0, 0], acc_ref[0, 1]
-        out = jnp.where(wide < 64, main, extra) / jnp.where(wide < 64, swap(main), swap(extra))
-        out = out.astype(BF16)
-        level = (jnp.log2(extra) + top_ref[1])[:, 0:1]
-        row = lax.broadcasted_iota(jnp.int32, (16, LANES), 0)
-        for src in range(tile // 256):
-            out_ref[src, 0:256] = out[256 * src : 256 * src + 256]
-            tail = jnp.zeros((16, LANES), F32)
-            for half in range(2):
-                base = 256 * src + 128 * half
-                line = jnp.broadcast_to(level[base : base + 128], (128, LANES)).T[0:16]
-                for part in range(3):
-                    piece = line.astype(BF16).astype(F32)
-                    tail = jnp.where(row == 2 * part + half, piece, tail)
-                    line = line - piece
-            out_ref[src, 256:272] = tail.astype(BF16)
+            wide = lanes(tile)
+            total = jnp.where(wide < 64, acc_ref[0, 1], acc_ref[0, 0])
+            good = (jnp.min(total) > LOW) & (jnp.max(total) < HIGH)
+            top_ref[...] = jnp.zeros((2, tile, LANES), F32)
+
+            @pl.when(jnp.logical_not(good))
+            def _():
+                copies = []
+                for i, far_ref in enumerate(far_refs):
+                    here = store_ref.at[pl.ds(SETS * i, SETS)]
+                    copies.append(pltpu.make_async_copy(far_ref, here, sems.at[i]))
+                    copies[-1].start()
+                acc_ref[...] = jnp.zeros(acc_ref.shape, F32)
+                top_ref[...] = jnp.full((2, tile, LANES), -1e30, F32)
+                for copy in copies:
+                    copy.wait()
+
+                def online(step):
+                    kind, keys, values = step
+                    score = dot(query, keys)
+                    top = jnp.maximum(top_ref[kind], jnp.max(score, axis=1, keepdims=True))
+                    weight = jnp.exp2(score - top[:, 0:1]).astype(BF16)
+                    factor = jnp.exp2(top_ref[kind] - top)
+                    acc_ref[0, kind] = acc_ref[0, kind] * factor + dot(weight, values)
+                    top_ref[kind] = top
+
+                def pair_body(pair, carry):
+                    online(main_step(store_ref, pair))
+                    return carry
+
+                def block_body(block, carry):
+                    online(extra_step(store_ref, block))
+                    return carry
+
+                lax.fori_loop(0, SETS * SETS // 2, pair_body, 0)
+                lax.fori_loop(0, SETS, block_body, 0)
+
+            main, extra = acc_ref[0, 0], acc_ref[0, 1]
+            out = jnp.where(wide < 64, main, extra) / jnp.where(wide < 64, swap(main), swap(extra))
+            out = out.astype(BF16)
+            level = (jnp.log2(extra) + top_ref[1])[:, 0:1]
+            row = lax.broadcasted_iota(jnp.int32, (16, LANES), 0)
+            for src in range(tile // 256):
+                out_ref[src, 0:256] = out[256 * src : 256 * src + 256]
+                tail = jnp.zeros((16, LANES), F32)
+                for half in range(2):
+                    base = 256 * src + 128 * half
+                    line = jnp.broadcast_to(level[base : base + 128], (128, LANES)).T[0:16]
+                    for part in range(3):
+                        piece = line.astype(BF16).astype(F32)
+                        tail = jnp.where(row == 2 * part + half, piece, tail)
+                        line = line - piece
+                out_ref[src, 256:272] = tail.astype(BF16)
 
 
 def fold(got, blocks, acc, every=None, tile=1024):
@@ -308,7 +311,7 @@
             pltpu.VMEM((SETS * SETS, KV_ROWS, LANES), BF16),
             pltpu.VMEM((2, tile, LANES), F32),
             pltpu.SemaphoreType.DMA((SETS,)),
-        ]
+        ] + scratch
     return pl.pallas_call(
         functools.partial(fold_kernel, len(blocks), tile, first, last),
         grid=(TOKENS // tile, len(blocks)),
@@ -396,20 +399,18 @@
     tied = lax.optimization_barrier
     twin = lax.ppermute(own, RING, cross)
     ahead = lax.ppermute(own, RING, along)
+    (acc,) = fold(got, [own, twin], None)
+    own, ahead, acc = tied((own, ahead, acc))
+    ahead_twin = lax.ppermute(ahead, RING, cross)
     behind = lax.ppermute(own, RING, against)
-    (acc,) = fold(got, [own, twin], None)
-    ahead, acc = tied((ahead, acc))
-    ahead_twin = lax.ppermute(ahead, RING, cross)
     far = lax.ppermute(ahead, RING, along)
-    (acc,) = fold(got, [ahead], acc)
-    behind, acc = tied((behind, acc))
+    (acc,) = fold(got, [ahead, ahead_twin], acc)
+    behind, far, acc = tied((behind, far, acc))
     behind_twin = lax.ppermute(behind, RING, cross)
-    (acc,) = fold(got, [behind, ahead_twin], acc)
-    far, acc = tied((far, acc))
     far_twin = lax.ppermute(far, RING, cross)
-    (acc,) = fold(got, [behind_twin, far], acc)
+    (acc,) = fold(got, [behind, far], acc)
     every = [own, twin, ahead, behind, ahead_twin, behind_twin, far, far_twin]
-    unused, out = fold(got, [far_twin], acc, every)
+    unused, out = fold(got, [behind_twin, far_twin], acc, every)
 
     back = lax.all_to_all(out, ("x", "z"), 0, 0)
     return finish(back, hidden).reshape(rows_here, cols, chans)

time: 209 us -> 210 us (level)
    ppermute x1, starting transfers between devices: 0.01 us -> 2.67 us  [on_device(): far = lax.ppermute(ahead, RING, along)]
    ppermute x1, waiting for transfers between devices: 2.52 us -> 0.01 us  [on_device(): ahead = lax.ppermute(own, RING, along)]
    pallas_call x5 -> x4, Pallas kernels: 131 us -> 131 us  [fold(): pl.pallas_call(functools.partial(fold_kernel, len(blocks), tile, first, l...]
  transfers between devices with their start and end apart: 18 -> 18, of which waited for: 5 -> 6; matrix products, arithmetic and copies ran while one was open for 1% -> 1% of each run, Pallas kernels for 20% -> 17%
where the time goes in v8:
time: 210 us; the launch traced here: 209 us
  Pallas kernels  141 us (67%)
  blocking collectives  30.3 us (14%)
  starting transfers between devices  28.2 us (13%)
  waiting for transfers between devices  8.52 us (4%)
    pallas_call x4, Pallas kernels, fold(): pl.pallas_call(functools.partial(fold_kernel, len(blocks), tile, first, l...  131 us
    all_to_all x1, blocking collectives, on_device(): got = lax.all_to_all(send, ('x', 'z'), 0, 0)  17.9 us
    ppermute x9, starting transfers between devices, total_of(): parts.append(lax.ppermute(value, axis, perm))  12.5 us
    all_to_all x1, blocking collectives, on_device(): back = lax.all_to_all(out, ('x', 'z'), 0, 0)  12.4 us
    pallas_call x1, Pallas kernels, front(): pl.pallas_call(front_kernel, in_specs=[pl.BlockSpec(memory_space=pltpu.VM...  6.88 us
    ppermute x9, waiting for transfers between devices, total_of(): parts.append(lax.ppermute(value, axis, perm))  5.31 us
    ppermute x1, starting transfers between devices, halo(): before = lax.ppermute(last, BAND, up)  4.9 us
  transfers between devices with their start and end apart: 18, of which 6 were waited for; matrix products, arithmetic and copies ran while one was open for 1% of the time, Pallas kernels for 17%

profile of v8, /device:TPU:1, one launch (start us, length us, event | category | flops | bytes accessed | tf_op | source)
XLA Modules:
  0.0 209.4 jit_solution(7916510763045912217)
XLA Ops:
  0.0 1.7 begin.1
  1.7 3.6 %collective-permute-start.2 = (f32[2,640]{1,0:T(2,128)S(1)}, f32[2,640]{1,0:T(2,128)S(1)}, u32[]{:S(2)}, u32[]{:S(2)}) collective-permute-start(f32[2,640]{1,0:T(2,128)S(1)} %get-tuple-element.17), channel_id=1, source_target_pairs={{0,24},{8,0},{16,8},{24,16},{1,25},{9,1},{17,9},{25,17},{2,26},{10... | collective-permute-start | bytes 15368 | tf_op jit(solution)/shard_map/ppermute | solution.py:40
  5.4 0.3 collective-permute-start.1
  5.7 0.7 collective-permute-start
  6.4 4.9 %collective-permute-start.9 = (bf16[1,128,640]{2,1,0:T(8,128)(2,1)}, bf16[1,128,640]{2,1,0:T(8,128)(2,1)S(1)}, u32[]{:S(2)}, u32[]{:S(2)}) collective-permute-start(bf16[1,128,640]{2,1,0:T(8,128)(2,1)} %get-tuple-element.18), channel_id=1, source_target_pairs={{0,4},{4,8},{8,12},{12,16},{16,20},{20,24},{24,28},{28,32},{32,36}... | collective-permute-start | bytes 491528 | tf_op jit(solution)/shard_map/ppermute | solution.py:48
  11.3 1.9 collective-permute-start.10
  13.3 0.0 collective-permute-done.2
  13.3 0.0 collective-permute-done.1
  13.3 0.0 collective-permute-done
  13.3 0.1 collective-permute-start.5
  13.4 4.0 %collective-permute-start.4 = (f32[2,640]{1,0:T(2,128)S(1)}, f32[2,640]{1,0:T(2,128)S(1)}, u32[]{:S(2)}, u32[]{:S(2)}) collective-permute-start(f32[2,640]{1,0:T(2,128)S(1)} %add_add_fusion.2), channel_id=1, source_target_pairs={{0,32},{4,36},{32,0},{36,4},{1,33},{5,37},{33,1},{37,5},{2,34},{6,... | collective-permute-start | bytes 15368 | tf_op jit(solution)/shard_map/ppermute | solution.py:40
  17.4 0.1 collective-permute-start.3
  17.5 3.1 %collective-permute-done.5 = f32[2,640]{1,0:T(2,128)S(1)} collective-permute-done((f32[2,640]{1,0:T(2,128)S(1)}, f32[2,640]{1,0:T(2,128)S(1)}, u32[]{:S(2)}, u32[]{:S(2)}) %collective-permute-start.5) | collective-permute-done | bytes 5152 | tf_op jit(solution)/shard_map/ppermute | solution.py:40
  20.6 0.0 collective-permute-done.4
  20.6 0.0 collective-permute-done.3
  20.6 2.6 %collective-permute-start.8 = (f32[2,640]{1,0:T(2,128)S(1)}, f32[2,640]{1,0:T(2,128)S(1)}, u32[]{:S(2)}, u32[]{:S(2)}) collective-permute-start(f32[2,640]{1,0:T(2,128)S(1)} %add_add_fusion.1), channel_id=1, source_target_pairs={{0,192},{64,0},{128,64},{192,128},{1,193},{65,1},{129,65},{193,129... | collective-permute-start | bytes 15368 | tf_op jit(solution)/shard_map/ppermute | solution.py:40
  23.1 0.5 collective-permute-start.7
  23.7 0.6 collective-permute-start.6
  24.3 0.8 select_select_fusion.vec_ref
  25.1 0.0 collective-permute-done.8
  25.1 2.0 collective-permute-done.7
  27.1 0.2 collective-permute-done.6
  27.3 0.1 reshape.10
  27.4 0.2 fusion
  27.6 0.1 reshape.11.sums_ref
  27.7 0.0 collective-permute-done.9.before_ref
  27.7 0.0 collective-permute-done.10.after_ref
  27.7 6.9 %front.1 = (bf16[256,640]{1,0:T(8,128)(2,1)S(1)}, bf16[8,576,128]{2,1,0:T(8,128)(2,1)S(1)}) custom-call(f32[2,640]{1,0:T(2,128)S(1)} %reshape.11.sums_ref, f32[8,640]{1,0:T(8,128)S(1)} %select_select_fusion.vec_ref, bf16[1,128,640]{2,1,0:T(8,128)(2,1)S(1)} %collective-permute-done.9.before_ref, bf16[1,128,640]{2,1,0:T(8,128)(2,1)S(1)} %collective-permute-done.10.after_ref, ...), custom_call_target="tpu_custom_call" | custom-call | tf_op jit(solution)/shard_map/front/pallas_call | solution.py:159
  34.6 17.9 %all_to_all.10.q_ref = bf16[8,576,128]{2,1,0:T(8,128)(2,1)S(1)} all-to-all(bf16[8,576,128]{2,1,0:T(8,128)(2,1)S(1)} %get-tuple-element.20), channel_id=1, replica_groups=mesh['x'=4,'z'=2,'y'=4,'core'=2,'img'=4] {'x','z'}, dimensions={0} | all-to-all | bytes 2359296 | tf_op jit(solution)/shard_map/all_to_all | solution.py:392
  52.6 3.6 %collective-permute-start.12 = (bf16[8,320,128]{2,1,0:T(8,128)(2,1)S(1)}, bf16[8,320,128]{2,1,0:T(8,128)(2,1)S(1)}, u32[]{:S(2)}, u32[]{:S(2)}) collective-permute-start(bf16[8,320,128]{2,1,0:T(8,128)(2,1)S(1)} %slice.4.refs_0_.refs_3_), channel_id=1, source_target_pairs={{0,4},{4,0},{8,12},{12,8},{16,20},{20,16},{24,28},{28,24},{1,5},{5... | collective-permute-start | bytes 1966088 | tf_op jit(solution)/shard_map/ppermute | solution.py:400
  56.2 0.0 collective-permute-start.11
  56.2 1.7 collective-permute-done.12.refs_1_.refs_4_
  57.9 11.9 %fold.4.refs_2_ = f32[2,2,1024,128]{3,2,1,0:T(8,128)S(1)} custom-call(bf16[8,576,128]{2,1,0:T(8,128)(2,1)S(1)} %all_to_all.10.q_ref, bf16[8,320,128]{2,1,0:T(8,128)(2,1)S(1)} %slice.4.refs_0_.refs_3_, bf16[8,320,128]{2,1,0:T(8,128)(2,1)S(1)} %collective-permute-done.12.refs_1_.refs_4_), custom_call_target="tpu_custom_call" | custom-call | tf_op jit(solution)/shard_map/fold/pallas_call | solution.py:315
  69.8 0.0 collective-permute-done.11.refs_0_.refs_5_
  69.8 0.5 collective-permute-start.15
  70.3 0.0 collective-permute-start.13
  70.3 2.7 %collective-permute-start.14 = (bf16[8,320,128]{2,1,0:T(8,128)(2,1)S(1)}, bf16[8,320,128]{2,1,0:T(8,128)(2,1)S(1)}, u32[]{:S(2)}, u32[]{:S(2)}) collective-permute-start(bf16[8,320,128]{2,1,0:T(8,128)(2,1)S(1)} %collective-permute-done.11.refs_0_.refs_5_), channel_id=1, source_target_pairs={{0,8},{4,28},{8,16},{12,4},{16,24},{20,12},{24,0},{28,20},{1,9},{5... | collective-permute-start | bytes 1966088 | tf_op jit(solution)/shard_map/ppermute | solution.py:406
  73.0 0.0 collective-permute-done.15.refs_1_.refs_7_
  73.0 12.0 %fold.5.refs_2_ = f32[2,2,1024,128]{3,2,1,0:T(8,128)S(1)} custom-call(bf16[8,576,128]{2,1,0:T(8,128)(2,1)S(1)} %all_to_all.10.q_ref, bf16[8,320,128]{2,1,0:T(8,128)(2,1)S(1)} %collective-permute-done.11.refs_0_.refs_5_, bf16[8,320,128]{2,1,0:T(8,128)(2,1)S(1)} %collective-permute-done.15.refs_1_.refs_7_, ...), custom_call_target="tpu_custom_call", output_to_operand_aliasing={{}: (3, {})} | custom-call | tf_op jit(solution)/shard_map/fold/pallas_call | solution.py:315
  85.0 1.4 collective-permute-done.13.refs_0_.refs_6_
  86.4 0.1 collective-permute-done.14.refs_1_.refs_9_
  86.5 2.2 %collective-permute-start.16 = (bf16[8,320,128]{2,1,0:T(8,128)(2,1)S(1)}, bf16[8,320,128]{2,1,0:T(8,128)(2,1)S(1)}, u32[]{:S(2)}, u32[]{:S(2)}) collective-permute-start(bf16[8,320,128]{2,1,0:T(8,128)(2,1)S(1)} %collective-permute-done.13.refs_0_.refs_6_), channel_id=1, source_target_pairs={{0,4},{4,0},{8,12},{12,8},{16,20},{20,16},{24,28},{28,24},{1,5},{5... | collective-permute-start | bytes 1966088 | tf_op jit(solution)/shard_map/ppermute | solution.py:409
  88.6 0.0 collective-permute-start.17
  88.6 12.0 %fold.6.refs_2_ = f32[2,2,1024,128]{3,2,1,0:T(8,128)S(1)} custom-call(bf16[8,576,128]{2,1,0:T(8,128)(2,1)S(1)} %all_to_all.10.q_ref, bf16[8,320,128]{2,1,0:T(8,128)(2,1)S(1)} %collective-permute-done.13.refs_0_.refs_6_, bf16[8,320,128]{2,1,0:T(8,128)(2,1)S(1)} %collective-permute-done.14.refs_1_.refs_9_, ...), custom_call_target="tpu_custom_call", output_to_operand_aliasing={{}: (3, {})} | custom-call | tf_op jit(solution)/shard_map/fold/pallas_call | solution.py:315
  100.7 0.0 collective-permute-done.16.refs_0_.refs_8_
  100.7 0.0 collective-permute-done.17.refs_1_.refs_10_
  100.7 95.0 %fold.7 = (f32[2,2,1024,128]{3,2,1,0:T(8,128)S(1)}, bf16[8,272,128]{2,1,0:T(8,128)(2,1)S(1)}) custom-call(bf16[8,576,128]{2,1,0:T(8,128)(2,1)S(1)} %all_to_all.10.q_ref, bf16[8,320,128]{2,1,0:T(8,128)(2,1)S(1)} %collective-permute-done.16.refs_0_.refs_8_, ...), custom_call_target="tpu_custom_call", output_to_operand_aliasing={{0}: (3, {})} | custom-call | tf_op jit(solution)/shard_map/fold/pallas_call | solution.py:315
  195.7 12.4 %all_to_all.11.back_ref = bf16[8,272,128]{2,1,0:T(8,128)(2,1)S(1)} all-to-all(bf16[8,272,128]{2,1,0:T(8,128)(2,1)S(1)} %get-tuple-element.27), channel_id=1, replica_groups=mesh['x'=4,'z'=2,'y'=4,'core'=2,'img'=4] {'x','z'}, dimensions={0} | all-to-all | bytes 1114112 | tf_op jit(solution)/shard_map/all_to_all | solution.py:415
  208.1 1.3 finish.1
  (8 shorter events, 0.1 us)
Async XLA Ops:
  1.7 11.6 %collective-permute-start.2 = (f32[2,640]{1,0:T(2,128)S(1)}, f32[2,640]{1,0:T(2,128)S(1)}, u32[]{:S(2)}, u32[]{:S(2)}) collective-permute-start(f32[2,640]{1,0:T(2,128)S(1)} %get-tuple-element.17), channel_id=1, source_target_pairs={{0,24},{8,0},{16,8},{24,16},{1,25},{9,1},{17,9},{25,17},{2,26},{10... | collective-permute-start | bytes 15368 | tf_op jit(solution)/shard_map/ppermute | solution.py:40
  5.4 7.9 %collective-permute-start.1 = (f32[2,640]{1,0:T(2,128)S(1)}, f32[2,640]{1,0:T(2,128)S(1)}, u32[]{:S(2)}, u32[]{:S(2)}) collective-permute-start(f32[2,640]{1,0:T(2,128)S(1)} %get-tuple-element.17), channel_id=1, source_target_pairs={{0,16},{8,24},{16,0},{24,8},{1,17},{9,25},{17,1},{25,9},{2,18},{10... | collective-permute-start | bytes 15368 | tf_op jit(solution)/shard_map/ppermute | solution.py:40
  5.7 7.6 %collective-permute-start = (f32[2,640]{1,0:T(2,128)S(1)}, f32[2,640]{1,0:T(2,128)S(1)}, u32[]{:S(2)}, u32[]{:S(2)}) collective-permute-start(f32[2,640]{1,0:T(2,128)S(1)} %get-tuple-element.17), channel_id=1, source_target_pairs={{0,8},{8,16},{16,24},{24,0},{1,9},{9,17},{17,25},{25,1},{2,10},{10... | collective-permute-start | bytes 15368 | tf_op jit(solution)/shard_map/ppermute | solution.py:40
  6.4 21.3 %collective-permute-start.9 = (bf16[1,128,640]{2,1,0:T(8,128)(2,1)}, bf16[1,128,640]{2,1,0:T(8,128)(2,1)S(1)}, u32[]{:S(2)}, u32[]{:S(2)}) collective-permute-start(bf16[1,128,640]{2,1,0:T(8,128)(2,1)} %get-tuple-element.18), channel_id=1, source_target_pairs={{0,4},{4,8},{8,12},{12,16},{16,20},{20,24},{24,28},{28,32},{32,36}... | collective-permute-start | bytes 491528 | tf_op jit(solution)/shard_map/ppermute | solution.py:48
  11.3 16.4 %collective-permute-start.10 = (bf16[1,128,640]{2,1,0:T(8,128)(2,1)}, bf16[1,128,640]{2,1,0:T(8,128)(2,1)S(1)}, u32[]{:S(2)}, u32[]{:S(2)}) collective-permute-start(bf16[1,128,640]{2,1,0:T(8,128)(2,1)} %get-tuple-element.19), channel_id=1, source_target_pairs={{4,0},{8,4},{12,8},{16,12},{20,16},{24,20},{28,24},{32,28},{36,32}... | collective-permute-start | bytes 491528 | tf_op jit(solution)/shard_map/ppermute | solution.py:49
  13.3 7.2 %collective-permute-start.5 = (f32[2,640]{1,0:T(2,128)S(1)}, f32[2,640]{1,0:T(2,128)S(1)}, u32[]{:S(2)}, u32[]{:S(2)}) collective-permute-start(f32[2,640]{1,0:T(2,128)S(1)} %add_add_fusion.2), channel_id=1, source_target_pairs={{0,36},{4,0},{32,4},{36,32},{1,37},{5,1},{33,5},{37,33},{2,38},{6,... | collective-permute-start | bytes 15368 | tf_op jit(solution)/shard_map/ppermute | solution.py:40
  13.4 7.1 %collective-permute-start.4 = (f32[2,640]{1,0:T(2,128)S(1)}, f32[2,640]{1,0:T(2,128)S(1)}, u32[]{:S(2)}, u32[]{:S(2)}) collective-permute-start(f32[2,640]{1,0:T(2,128)S(1)} %add_add_fusion.2), channel_id=1, source_target_pairs={{0,32},{4,36},{32,0},{36,4},{1,33},{5,37},{33,1},{37,5},{2,34},{6,... | collective-permute-start | bytes 15368 | tf_op jit(solution)/shard_map/ppermute | solution.py:40
  17.4 3.1 %collective-permute-start.3 = (f32[2,640]{1,0:T(2,128)S(1)}, f32[2,640]{1,0:T(2,128)S(1)}, u32[]{:S(2)}, u32[]{:S(2)}) collective-permute-start(f32[2,640]{1,0:T(2,128)S(1)} %add_add_fusion.2), channel_id=1, source_target_pairs={{0,4},{4,32},{32,36},{36,0},{1,5},{5,33},{33,37},{37,1},{2,6},{6,3... | collective-permute-start | bytes 15368 | tf_op jit(solution)/shard_map/ppermute | solution.py:40
  20.6 4.5 %collective-permute-start.8 = (f32[2,640]{1,0:T(2,128)S(1)}, f32[2,640]{1,0:T(2,128)S(1)}, u32[]{:S(2)}, u32[]{:S(2)}) collective-permute-start(f32[2,640]{1,0:T(2,128)S(1)} %add_add_fusion.1), channel_id=1, source_target_pairs={{0,192},{64,0},{128,64},{192,128},{1,193},{65,1},{129,65},{193,129... | collective-permute-start | bytes 15368 | tf_op jit(solution)/shard_map/ppermute | solution.py:40
  23.1 4.0 %collective-permute-start.7 = (f32[2,640]{1,0:T(2,128)S(1)}, f32[2,640]{1,0:T(2,128)S(1)}, u32[]{:S(2)}, u32[]{:S(2)}) collective-permute-start(f32[2,640]{1,0:T(2,128)S(1)} %add_add_fusion.1), channel_id=1, source_target_pairs={{0,128},{64,192},{128,0},{192,64},{1,129},{65,193},{129,1},{193,65... | collective-permute-start | bytes 15368 | tf_op jit(solution)/shard_map/ppermute | solution.py:40
  23.7 3.7 %collective-permute-start.6 = (f32[2,640]{1,0:T(2,128)S(1)}, f32[2,640]{1,0:T(2,128)S(1)}, u32[]{:S(2)}, u32[]{:S(2)}) collective-permute-start(f32[2,640]{1,0:T(2,128)S(1)} %add_add_fusion.1), channel_id=1, source_target_pairs={{0,64},{64,128},{128,192},{192,0},{1,65},{65,129},{129,193},{193,1... | collective-permute-start | bytes 15368 | tf_op jit(solution)/shard_map/ppermute | solution.py:40
  52.6 5.3 %collective-permute-start.12 = (bf16[8,320,128]{2,1,0:T(8,128)(2,1)S(1)}, bf16[8,320,128]{2,1,0:T(8,128)(2,1)S(1)}, u32[]{:S(2)}, u32[]{:S(2)}) collective-permute-start(bf16[8,320,128]{2,1,0:T(8,128)(2,1)S(1)} %slice.4.refs_0_.refs_3_), channel_id=1, source_target_pairs={{0,4},{4,0},{8,12},{12,8},{16,20},{20,16},{24,28},{28,24},{1,5},{5... | collective-permute-start | bytes 1966088 | tf_op jit(solution)/shard_map/ppermute | solution.py:400
  56.2 13.7 %collective-permute-start.11 = (bf16[8,320,128]{2,1,0:T(8,128)(2,1)S(1)}, bf16[8,320,128]{2,1,0:T(8,128)(2,1)S(1)}, u32[]{:S(2)}, u32[]{:S(2)}) collective-permute-start(bf16[8,320,128]{2,1,0:T(8,128)(2,1)S(1)} %slice.4.refs_0_.refs_3_), channel_id=1, source_target_pairs={{0,8},{4,28},{8,16},{12,4},{16,24},{20,12},{24,0},{28,20},{1,9},{5... | collective-permute-start | bytes 1966088 | tf_op jit(solution)/shard_map/ppermute | solution.py:401
  69.8 3.1 %collective-permute-start.15 = (bf16[8,320,128]{2,1,0:T(8,128)(2,1)S(1)}, bf16[8,320,128]{2,1,0:T(8,128)(2,1)S(1)}, u32[]{:S(2)}, u32[]{:S(2)}) collective-permute-start(bf16[8,320,128]{2,1,0:T(8,128)(2,1)S(1)} %collective-permute-done.11.refs_0_.refs_5_), channel_id=1, source_target_pairs={{0,4},{4,0},{8,12},{12,8},{16,20},{20,16},{24,28},{28,24},{1,5},{5... | collective-permute-start | bytes 1966088 | tf_op jit(solution)/shard_map/ppermute | solution.py:404
  70.3 16.1 %collective-permute-start.13 = (bf16[8,320,128]{2,1,0:T(8,128)(2,1)S(1)}, bf16[8,320,128]{2,1,0:T(8,128)(2,1)S(1)}, u32[]{:S(2)}, u32[]{:S(2)}) collective-permute-start(bf16[8,320,128]{2,1,0:T(8,128)(2,1)S(1)} %slice.4.refs_0_.refs_3_), channel_id=1, source_target_pairs={{8,0},{28,4},{16,8},{4,12},{24,16},{12,20},{0,24},{20,28},{9,1},{2... | collective-permute-start | bytes 1966088 | tf_op jit(solution)/shard_map/ppermute | solution.py:405
  70.3 16.2 %collective-permute-start.14 = (bf16[8,320,128]{2,1,0:T(8,128)(2,1)S(1)}, bf16[8,320,128]{2,1,0:T(8,128)(2,1)S(1)}, u32[]{:S(2)}, u32[]{:S(2)}) collective-permute-start(bf16[8,320,128]{2,1,0:T(8,128)(2,1)S(1)} %collective-permute-done.11.refs_0_.refs_5_), channel_id=1, source_target_pairs={{0,8},{4,28},{8,16},{12,4},{16,24},{20,12},{24,0},{28,20},{1,9},{5... | collective-permute-start | bytes 1966088 | tf_op jit(solution)/shard_map/ppermute | solution.py:406
  86.5 14.2 %collective-permute-start.16 = (bf16[8,320,128]{2,1,0:T(8,128)(2,1)S(1)}, bf16[8,320,128]{2,1,0:T(8,128)(2,1)S(1)}, u32[]{:S(2)}, u32[]{:S(2)}) collective-permute-start(bf16[8,320,128]{2,1,0:T(8,128)(2,1)S(1)} %collective-permute-done.13.refs_0_.refs_6_), channel_id=1, source_target_pairs={{0,4},{4,0},{8,12},{12,8},{16,20},{20,16},{24,28},{28,24},{1,5},{5... | collective-permute-start | bytes 1966088 | tf_op jit(solution)/shard_map/ppermute | solution.py:409
  88.6 12.1 %collective-permute-start.17 = (bf16[8,320,128]{2,1,0:T(8,128)(2,1)S(1)}, bf16[8,320,128]{2,1,0:T(8,128)(2,1)S(1)}, u32[]{:S(2)}, u32[]{:S(2)}) collective-permute-start(bf16[8,320,128]{2,1,0:T(8,128)(2,1)S(1)} %collective-permute-done.14.refs_1_.refs_9_), channel_id=1, source_target_pairs={{0,4},{4,0},{8,12},{12,8},{16,20},{20,16},{24,28},{28,24},{1,5},{5... | collective-permute-start | bytes 1966088 | tf_op jit(solution)/shard_map/ppermute | solution.py:410

commit v9 on v4

--- a/solution.py
+++ b/solution.py
@@ -78,7 +78,7 @@
         begin_kernel,
         in_specs=[pl.BlockSpec(memory_space=pltpu.HBM)],
         out_specs=[pl.BlockSpec(memory_space=pltpu.VMEM)] * 3,
-        out_shape=[jax.ShapeDtypeStruct((2, latent.shape[2]), F32), edge, edge],
+        out_shape=[pltpu.VMEM((2, latent.shape[2]), F32), edge, edge],
         scratch_shapes=[pltpu.VMEM(latent.shape, BF16), pltpu.SemaphoreType.DMA((1,))],
         name="begin",
     )(pltpu.with_memory_space_constraint(latent, pltpu.HBM))
@@ -205,7 +205,7 @@
     if last:
         far_refs, refs = refs[:SETS], refs[SETS:]
     acc_ref = refs[0]
-    acc_ref[...] = jnp.zeros((2, tile, LANES), F32) if first else acc_in[...]
+    acc_ref[...] = jnp.zeros(acc_ref.shape, F32) if first else acc_in[...]
     query = q_ref[...].reshape(tile, LANES)
 
     steps = []
@@ -220,13 +220,15 @@
         if held is not None:
             held_kind, held_score, held_values = held
             weight = jnp.exp2(held_score).astype(BF16)
-            acc_ref[held_kind] += dot(weight, held_values)
+            update = dot(weight, held_values)
+            for i in range(tile // SPAN):
+                acc_ref[i, held_kind] += update[SPAN * i : SPAN * i + SPAN]
         held = None if step is None else (kind, score, values)
 
     if last:
         out_ref, store_ref, top_ref, sems = refs[1:]
         wide = lanes(tile)
-        total = jnp.where(wide < 64, acc_ref[1], acc_ref[0])
+        total = jnp.where(wide < 64, acc_ref[0, 1], acc_ref[0, 0])
         good = (jnp.min(total) > LOW) & (jnp.max(total) < HIGH)
         top_ref[...] = jnp.zeros((2, tile, LANES), F32)
 
@@ -237,7 +239,7 @@
                 here = store_ref.at[pl.ds(SETS * i, SETS)]
                 copies.append(pltpu.make_async_copy(far_ref, here, sems.at[i]))
                 copies[-1].start()
-            acc_ref[...] = jnp.zeros((2, tile, LANES), F32)
+            acc_ref[...] = jnp.zeros(acc_ref.shape, F32)
             top_ref[...] = jnp.full((2, tile, LANES), -1e30, F32)
             for copy in copies:
                 copy.wait()
@@ -248,7 +250,7 @@
                 top = jnp.maximum(top_ref[kind], jnp.max(score, axis=1, keepdims=True))
                 weight = jnp.exp2(score - top[:, 0:1]).astype(BF16)
                 factor = jnp.exp2(top_ref[kind] - top)
-                acc_ref[kind] = acc_ref[kind] * factor + dot(weight, values)
+                acc_ref[0, kind] = acc_ref[0, kind] * factor + dot(weight, values)
                 top_ref[kind] = top
 
             def pair_body(pair, carry):
@@ -262,7 +264,7 @@
             lax.fori_loop(0, SETS * SETS // 2, pair_body, 0)
             lax.fori_loop(0, SETS, block_body, 0)
 
-        main, extra = acc_ref[0], acc_ref[1]
+        main, extra = acc_ref[0, 0], acc_ref[0, 1]
         out = jnp.where(wide < 64, main, extra) / jnp.where(wide < 64, swap(main), swap(extra))
         out = out.astype(BF16)
         level = (jnp.log2(extra) + top_ref[1])[:, 0:1]
@@ -280,12 +282,12 @@
             out_ref[src, 256:272] = tail.astype(BF16)
 
 
-def fold(got, blocks, acc, every=None, tile=512):
+def fold(got, blocks, acc, every=None, tile=SPAN):
     first, last = acc is None, every is not None
-    acc_spec = pl.BlockSpec((2, tile, LANES), lambda t: (0, t, 0))
+    acc_spec = pl.BlockSpec((tile // SPAN, 2, SPAN, LANES), lambda t: (t, 0, 0, 0))
     kv_spec = pl.BlockSpec((SETS, KV_ROWS, LANES), lambda t: (0, 0, 0))
     out_specs = [acc_spec]
-    out_shape = [jax.ShapeDtypeStruct((2, TOKENS, LANES), F32)]
+    out_shape = [jax.ShapeDtypeStruct((TOKENS // SPAN, 2, SPAN, LANES), F32)]
     scratch = []
     if last:
         out_specs.append(pl.BlockSpec((tile // 256, BACK_ROWS, LANES), lambda t: (t, 0, 0)))
@@ -388,10 +390,10 @@
     (acc,) = fold(got, [twin], acc)
     ahead, acc = tied((ahead, acc))
     ahead_twin = lax.ppermute(ahead, RING, cross)
-    (acc,) = fold(got, [ahead], acc, tile=1024)
+    (acc,) = fold(got, [ahead], acc)
     ahead, acc = tied((ahead, acc))
     far = lax.ppermute(ahead, RING, along)
-    (acc,) = fold(got, [behind], acc, tile=1024)
+    (acc,) = fold(got, [behind], acc)
     behind, acc = tied((behind, acc))
     behind_twin = lax.ppermute(behind, RING, cross)
     (acc,) = fold(got, [ahead_twin], acc)

time: 255 us -> 255 us (level)
  transfers between devices with their start and end apart: 18 -> 18, of which waited for: 3 -> 3; matrix products, arithmetic and copies ran while one was open for 1% -> 0% of each run, Pallas kernels for 17% -> 17%
where the time goes in v9:
time: 255 us
  Pallas kernels  190 us (75%)
  blocking collectives  30.6 us (12%)
  starting transfers between devices  27.4 us (11%)
  waiting for transfers between devices  5.34 us (2%)
    pallas_call x7, Pallas kernels, fold(): pl.pallas_call(functools.partial(fold_kernel, len(blocks), tile, first, l...  180 us
    all_to_all x1, blocking collectives, on_device(): got = lax.all_to_all(send, ('x', 'z'), 0, 0)  17.9 us
    all_to_all x1, blocking collectives, on_device(): back = lax.all_to_all(out, ('x', 'z'), 0, 0)  12.7 us
    ppermute x9, starting transfers between devices, total_of(): parts.append(lax.ppermute(value, axis, perm))  12.5 us
    pallas_call x1, Pallas kernels, front(): pl.pallas_call(front_kernel, in_specs=[pl.BlockSpec(memory_space=pltpu.VM...  6.88 us
    ppermute x9, waiting for transfers between devices, total_of(): parts.append(lax.ppermute(value, axis, perm))  5.31 us
  transfers between devices with their start and end apart: 18, of which 3 were waited for; matrix products, arithmetic and copies ran while one was open for 0% of the time, Pallas kernels for 17%

profile of v9, /device:TPU:1, one launch (start us, length us, event | category | flops | bytes accessed | tf_op | source)
XLA Modules:
  0.0 254.7 jit_solution(1912989144776074116)
XLA Ops:
  0.0 1.7 begin.1
  1.7 3.6 %collective-permute-start.2 = (f32[2,640]{1,0:T(2,128)S(1)}, f32[2,640]{1,0:T(2,128)S(1)}, u32[]{:S(2)}, u32[]{:S(2)}) collective-permute-start(f32[2,640]{1,0:T(2,128)S(1)} %get-tuple-element.21), channel_id=1, source_target_pairs={{0,24},{8,0},{16,8},{24,16},{1,25},{9,1},{17,9},{25,17},{2,26},{10... | collective-permute-start | bytes 15368 | tf_op jit(solution)/shard_map/ppermute | solution.py:39
  5.4 0.3 collective-permute-start.1
  5.7 0.7 collective-permute-start
  6.4 4.9 %collective-permute-start.9 = (bf16[1,128,640]{2,1,0:T(8,128)(2,1)}, bf16[1,128,640]{2,1,0:T(8,128)(2,1)S(1)}, u32[]{:S(2)}, u32[]{:S(2)}) collective-permute-start(bf16[1,128,640]{2,1,0:T(8,128)(2,1)} %get-tuple-element.22), channel_id=1, source_target_pairs={{0,4},{4,8},{8,12},{12,16},{16,20},{20,24},{24,28},{28,32},{32,36}... | collective-permute-start | bytes 491528 | tf_op jit(solution)/shard_map/ppermute | solution.py:47
  11.3 1.9 collective-permute-start.10
  13.3 0.0 collective-permute-done.2
  13.3 0.0 collective-permute-done.1
  13.3 0.0 collective-permute-done
  13.3 0.1 collective-permute-start.5
  13.4 4.0 %collective-permute-start.4 = (f32[2,640]{1,0:T(2,128)S(1)}, f32[2,640]{1,0:T(2,128)S(1)}, u32[]{:S(2)}, u32[]{:S(2)}) collective-permute-start(f32[2,640]{1,0:T(2,128)S(1)} %add_add_fusion.2), channel_id=1, source_target_pairs={{0,32},{4,36},{32,0},{36,4},{1,33},{5,37},{33,1},{37,5},{2,34},{6,... | collective-permute-start | bytes 15368 | tf_op jit(solution)/shard_map/ppermute | solution.py:39
  17.4 0.1 collective-permute-start.3
  17.5 3.1 %collective-permute-done.5 = f32[2,640]{1,0:T(2,128)S(1)} collective-permute-done((f32[2,640]{1,0:T(2,128)S(1)}, f32[2,640]{1,0:T(2,128)S(1)}, u32[]{:S(2)}, u32[]{:S(2)}) %collective-permute-start.5) | collective-permute-done | bytes 5152 | tf_op jit(solution)/shard_map/ppermute | solution.py:39
  20.6 0.0 collective-permute-done.4
  20.6 0.0 collective-permute-done.3
  20.6 2.6 %collective-permute-start.8 = (f32[2,640]{1,0:T(2,128)S(1)}, f32[2,640]{1,0:T(2,128)S(1)}, u32[]{:S(2)}, u32[]{:S(2)}) collective-permute-start(f32[2,640]{1,0:T(2,128)S(1)} %add_add_fusion.1), channel_id=1, source_target_pairs={{0,192},{64,0},{128,64},{192,128},{1,193},{65,1},{129,65},{193,129... | collective-permute-start | bytes 15368 | tf_op jit(solution)/shard_map/ppermute | solution.py:39
  23.1 0.5 collective-permute-start.7
  23.7 0.6 collective-permute-start.6
  24.3 0.8 select_select_fusion.vec_ref
  25.1 0.0 collective-permute-done.8
  25.1 2.0 collective-permute-done.7
  27.1 0.2 collective-permute-done.6
  27.3 0.1 reshape.10
  27.4 0.2 fusion
  27.6 0.1 reshape.11.sums_ref
  27.7 0.0 collective-permute-done.9.before_ref
  27.7 0.0 collective-permute-done.10.after_ref
  27.7 6.9 %front.1 = (bf16[256,640]{1,0:T(8,128)(2,1)S(1)}, bf16[8,576,128]{2,1,0:T(8,128)(2,1)S(1)}) custom-call(f32[2,640]{1,0:T(2,128)S(1)} %reshape.11.sums_ref, f32[8,640]{1,0:T(8,128)S(1)} %select_select_fusion.vec_ref, bf16[1,128,640]{2,1,0:T(8,128)(2,1)S(1)} %collective-permute-done.9.before_ref, bf16[1,128,640]{2,1,0:T(8,128)(2,1)S(1)} %collective-permute-done.10.after_ref, ...), custom_call_target="tpu_custom_call" | custom-call | tf_op jit(solution)/shard_map/front/pallas_call | solution.py:158
  34.6 17.9 %all_to_all.10.q_ref = bf16[8,576,128]{2,1,0:T(8,128)(2,1)S(1)} all-to-all(bf16[8,576,128]{2,1,0:T(8,128)(2,1)S(1)} %get-tuple-element.24), channel_id=1, replica_groups=mesh['x'=4,'z'=2,'y'=4,'core'=2,'img'=4] {'x','z'}, dimensions={0} | all-to-all | bytes 2359296 | tf_op jit(solution)/shard_map/all_to_all | solution.py:377
  52.6 3.6 %collective-permute-start.12 = (bf16[8,320,128]{2,1,0:T(8,128)(2,1)S(1)}, bf16[8,320,128]{2,1,0:T(8,128)(2,1)S(1)}, u32[]{:S(2)}, u32[]{:S(2)}) collective-permute-start(bf16[8,320,128]{2,1,0:T(8,128)(2,1)S(1)} %slice.4.refs_0_.refs_2_), channel_id=1, source_target_pairs={{0,4},{4,0},{8,12},{12,8},{16,20},{20,16},{24,28},{28,24},{1,5},{5... | collective-permute-start | bytes 1966088 | tf_op jit(solution)/shard_map/ppermute | solution.py:385
  56.2 0.0 collective-permute-start.11
  56.2 6.1 %fold.7.refs_1_ = f32[4,2,512,128]{3,2,1,0:T(8,128)S(1)} custom-call(bf16[8,576,128]{2,1,0:T(8,128)(2,1)S(1)} %all_to_all.10.q_ref, bf16[8,320,128]{2,1,0:T(8,128)(2,1)S(1)} %slice.4.refs_0_.refs_2_), custom_call_target="tpu_custom_call" | custom-call | tf_op jit(solution)/shard_map/fold/pallas_call | solution.py:300
  62.3 1.5 collective-permute-start.15
  63.8 0.0 collective-permute-done.12.refs_0_.refs_3_
  63.8 6.2 %fold.8.refs_1_ = f32[4,2,512,128]{3,2,1,0:T(8,128)S(1)} custom-call(bf16[8,576,128]{2,1,0:T(8,128)(2,1)S(1)} %all_to_all.10.q_ref, bf16[8,320,128]{2,1,0:T(8,128)(2,1)S(1)} %collective-permute-done.12.refs_0_.refs_3_, f32[4,2,512,128]{3,2,1,0:T(8,128)S(1)} %fold.7.refs_1_), custom_call_target="tpu_custom_call", output_to_operand_aliasing={{}: (2, {})} | custom-call | tf_op jit(solution)/shard_map/fold/pallas_call | solution.py:300
  70.0 0.0 collective-permute-done.11.refs_0_.refs_4_
  70.1 1.9 collective-permute-start.14
  72.0 6.2 %fold.9.refs_1_ = f32[4,2,512,128]{3,2,1,0:T(8,128)S(1)} custom-call(bf16[8,576,128]{2,1,0:T(8,128)(2,1)S(1)} %all_to_all.10.q_ref, bf16[8,320,128]{2,1,0:T(8,128)(2,1)S(1)} %collective-permute-done.11.refs_0_.refs_4_, f32[4,2,512,128]{3,2,1,0:T(8,128)S(1)} %fold.8.refs_1_), custom_call_target="tpu_custom_call", output_to_operand_aliasing={{}: (2, {})} | custom-call | tf_op jit(solution)/shard_map/fold/pallas_call | solution.py:300
  78.2 0.1 collective-permute-start.13
  78.3 0.0 collective-permute-done.15.refs_0_.refs_5_
  78.3 6.2 %fold.10.refs_1_ = f32[4,2,512,128]{3,2,1,0:T(8,128)S(1)} custom-call(bf16[8,576,128]{2,1,0:T(8,128)(2,1)S(1)} %all_to_all.10.q_ref, bf16[8,320,128]{2,1,0:T(8,128)(2,1)S(1)} %collective-permute-done.15.refs_0_.refs_5_, f32[4,2,512,128]{3,2,1,0:T(8,128)S(1)} %fold.9.refs_1_), custom_call_target="tpu_custom_call", output_to_operand_aliasing={{}: (2, {})} | custom-call | tf_op jit(solution)/shard_map/fold/pallas_call | solution.py:300
  84.6 0.1 collective-permute-start.17
  84.7 0.0 collective-permute-done.14.refs_0_.refs_6_
  84.7 6.2 %fold.11.refs_2_ = f32[4,2,512,128]{3,2,1,0:T(8,128)S(1)} custom-call(bf16[8,576,128]{2,1,0:T(8,128)(2,1)S(1)} %all_to_all.10.q_ref, bf16[8,320,128]{2,1,0:T(8,128)(2,1)S(1)} %collective-permute-done.14.refs_0_.refs_6_, f32[4,2,512,128]{3,2,1,0:T(8,128)S(1)} %fold.10.refs_1_), custom_call_target="tpu_custom_call", output_to_operand_aliasing={{}: (2, {})} | custom-call | tf_op jit(solution)/shard_map/fold/pallas_call | solution.py:300
  90.9 0.0 collective-permute-done.13.refs_1_.refs_8_
  90.9 0.8 collective-permute-start.16
  91.7 0.0 collective-permute-done.17.refs_0_.refs_7_
  91.7 12.2 %fold.12.refs_1_ = f32[4,2,512,128]{3,2,1,0:T(8,128)S(1)} custom-call(bf16[8,576,128]{2,1,0:T(8,128)(2,1)S(1)} %all_to_all.10.q_ref, bf16[8,320,128]{2,1,0:T(8,128)(2,1)S(1)} %collective-permute-done.17.refs_0_.refs_7_, bf16[8,320,128]{2,1,0:T(8,128)(2,1)S(1)} %collective-permute-done.13.refs_1_.refs_8_, ...), custom_call_target="tpu_custom_call", output_to_operand_aliasing={{}: (3, {})} | custom-call | tf_op jit(solution)/shard_map/fold/pallas_call | solution.py:300
  103.9 0.0 collective-permute-done.16.refs_0_.refs_9_
  103.9 136.7 %fold.13 = (f32[4,2,512,128]{3,2,1,0:T(8,128)S(1)}, bf16[8,272,128]{2,1,0:T(8,128)(2,1)S(1)}) custom-call(bf16[8,576,128]{2,1,0:T(8,128)(2,1)S(1)} %all_to_all.10.q_ref, bf16[8,320,128]{2,1,0:T(8,128)(2,1)S(1)} %collective-permute-done.16.refs_0_.refs_9_, f32[4,2,512,128]{3,2,1,0:T(8,128)S(1)} %fold.12.refs_1_, ...), custom_call_target="tpu_custom_call", output_to_operand_aliasing={{0}: (2, {})} | custom-call | tf_op jit(solution)/shard_map/fold/pallas_call | solution.py:300
  240.7 12.7 %all_to_all.11.back_ref = bf16[8,272,128]{2,1,0:T(8,128)(2,1)S(1)} all-to-all(bf16[8,272,128]{2,1,0:T(8,128)(2,1)S(1)} %get-tuple-element.35), channel_id=1, replica_groups=mesh['x'=4,'z'=2,'y'=4,'core'=2,'img'=4] {'x','z'}, dimensions={0} | all-to-all | bytes 1114112 | tf_op jit(solution)/shard_map/all_to_all | solution.py:406
  253.3 1.3 finish.1
  (8 shorter events, 0.1 us)
Async XLA Ops:
  1.7 11.6 %collective-permute-start.2 = (f32[2,640]{1,0:T(2,128)S(1)}, f32[2,640]{1,0:T(2,128)S(1)}, u32[]{:S(2)}, u32[]{:S(2)}) collective-permute-start(f32[2,640]{1,0:T(2,128)S(1)} %get-tuple-element.21), channel_id=1, source_target_pairs={{0,24},{8,0},{16,8},{24,16},{1,25},{9,1},{17,9},{25,17},{2,26},{10... | collective-permute-start | bytes 15368 | tf_op jit(solution)/shard_map/ppermute | solution.py:39
  5.4 7.9 %collective-permute-start.1 = (f32[2,640]{1,0:T(2,128)S(1)}, f32[2,640]{1,0:T(2,128)S(1)}, u32[]{:S(2)}, u32[]{:S(2)}) collective-permute-start(f32[2,640]{1,0:T(2,128)S(1)} %get-tuple-element.21), channel_id=1, source_target_pairs={{0,16},{8,24},{16,0},{24,8},{1,17},{9,25},{17,1},{25,9},{2,18},{10... | collective-permute-start | bytes 15368 | tf_op jit(solution)/shard_map/ppermute | solution.py:39
  5.7 7.6 %collective-permute-start = (f32[2,640]{1,0:T(2,128)S(1)}, f32[2,640]{1,0:T(2,128)S(1)}, u32[]{:S(2)}, u32[]{:S(2)}) collective-permute-start(f32[2,640]{1,0:T(2,128)S(1)} %get-tuple-element.21), channel_id=1, source_target_pairs={{0,8},{8,16},{16,24},{24,0},{1,9},{9,17},{17,25},{25,1},{2,10},{10... | collective-permute-start | bytes 15368 | tf_op jit(solution)/shard_map/ppermute | solution.py:39
  6.4 21.3 %collective-permute-start.9 = (bf16[1,128,640]{2,1,0:T(8,128)(2,1)}, bf16[1,128,640]{2,1,0:T(8,128)(2,1)S(1)}, u32[]{:S(2)}, u32[]{:S(2)}) collective-permute-start(bf16[1,128,640]{2,1,0:T(8,128)(2,1)} %get-tuple-element.22), channel_id=1, source_target_pairs={{0,4},{4,8},{8,12},{12,16},{16,20},{20,24},{24,28},{28,32},{32,36}... | collective-permute-start | bytes 491528 | tf_op jit(solution)/shard_map/ppermute | solution.py:47
  11.3 16.4 %collective-permute-start.10 = (bf16[1,128,640]{2,1,0:T(8,128)(2,1)}, bf16[1,128,640]{2,1,0:T(8,128)(2,1)S(1)}, u32[]{:S(2)}, u32[]{:S(2)}) collective-permute-start(bf16[1,128,640]{2,1,0:T(8,128)(2,1)} %get-tuple-element.23), channel_id=1, source_target_pairs={{4,0},{8,4},{12,8},{16,12},{20,16},{24,20},{28,24},{32,28},{36,32}... | collective-permute-start | bytes 491528 | tf_op jit(solution)/shard_map/ppermute | solution.py:48
  13.3 7.2 %collective-permute-start.5 = (f32[2,640]{1,0:T(2,128)S(1)}, f32[2,640]{1,0:T(2,128)S(1)}, u32[]{:S(2)}, u32[]{:S(2)}) collective-permute-start(f32[2,640]{1,0:T(2,128)S(1)} %add_add_fusion.2), channel_id=1, source_target_pairs={{0,36},{4,0},{32,4},{36,32},{1,37},{5,1},{33,5},{37,33},{2,38},{6,... | collective-permute-start | bytes 15368 | tf_op jit(solution)/shard_map/ppermute | solution.py:39
  13.4 7.1 %collective-permute-start.4 = (f32[2,640]{1,0:T(2,128)S(1)}, f32[2,640]{1,0:T(2,128)S(1)}, u32[]{:S(2)}, u32[]{:S(2)}) collective-permute-start(f32[2,640]{1,0:T(2,128)S(1)} %add_add_fusion.2), channel_id=1, source_target_pairs={{0,32},{4,36},{32,0},{36,4},{1,33},{5,37},{33,1},{37,5},{2,34},{6,... | collective-permute-start | bytes 15368 | tf_op jit(solution)/shard_map/ppermute | solution.py:39
  17.4 3.1 %collective-permute-start.3 = (f32[2,640]{1,0:T(2,128)S(1)}, f32[2,640]{1,0:T(2,128)S(1)}, u32[]{:S(2)}, u32[]{:S(2)}) collective-permute-start(f32[2,640]{1,0:T(2,128)S(1)} %add_add_fusion.2), channel_id=1, source_target_pairs={{0,4},{4,32},{32,36},{36,0},{1,5},{5,33},{33,37},{37,1},{2,6},{6,3... | collective-permute-start | bytes 15368 | tf_op jit(solution)/shard_map/ppermute | solution.py:39
  20.6 4.5 %collective-permute-start.8 = (f32[2,640]{1,0:T(2,128)S(1)}, f32[2,640]{1,0:T(2,128)S(1)}, u32[]{:S(2)}, u32[]{:S(2)}) collective-permute-start(f32[2,640]{1,0:T(2,128)S(1)} %add_add_fusion.1), channel_id=1, source_target_pairs={{0,192},{64,0},{128,64},{192,128},{1,193},{65,1},{129,65},{193,129... | collective-permute-start | bytes 15368 | tf_op jit(solution)/shard_map/ppermute | solution.py:39
  23.1 4.0 %collective-permute-start.7 = (f32[2,640]{1,0:T(2,128)S(1)}, f32[2,640]{1,0:T(2,128)S(1)}, u32[]{:S(2)}, u32[]{:S(2)}) collective-permute-start(f32[2,640]{1,0:T(2,128)S(1)} %add_add_fusion.1), channel_id=1, source_target_pairs={{0,128},{64,192},{128,0},{192,64},{1,129},{65,193},{129,1},{193,65... | collective-permute-start | bytes 15368 | tf_op jit(solution)/shard_map/ppermute | solution.py:39
  23.7 3.7 %collective-permute-start.6 = (f32[2,640]{1,0:T(2,128)S(1)}, f32[2,640]{1,0:T(2,128)S(1)}, u32[]{:S(2)}, u32[]{:S(2)}) collective-permute-start(f32[2,640]{1,0:T(2,128)S(1)} %add_add_fusion.1), channel_id=1, source_target_pairs={{0,64},{64,128},{128,192},{192,0},{1,65},{65,129},{129,193},{193,1... | collective-permute-start | bytes 15368 | tf_op jit(solution)/shard_map/ppermute | solution.py:39
  52.6 11.2 %collective-permute-start.12 = (bf16[8,320,128]{2,1,0:T(8,128)(2,1)S(1)}, bf16[8,320,128]{2,1,0:T(8,128)(2,1)S(1)}, u32[]{:S(2)}, u32[]{:S(2)}) collective-permute-start(bf16[8,320,128]{2,1,0:T(8,128)(2,1)S(1)} %slice.4.refs_0_.refs_2_), channel_id=1, source_target_pairs={{0,4},{4,0},{8,12},{12,8},{16,20},{20,16},{24,28},{28,24},{1,5},{5... | collective-permute-start | bytes 1966088 | tf_op jit(solution)/shard_map/ppermute | solution.py:385
  56.2 13.9 %collective-permute-start.11 = (bf16[8,320,128]{2,1,0:T(8,128)(2,1)S(1)}, bf16[8,320,128]{2,1,0:T(8,128)(2,1)S(1)}, u32[]{:S(2)}, u32[]{:S(2)}) collective-permute-start(bf16[8,320,128]{2,1,0:T(8,128)(2,1)S(1)} %slice.4.refs_0_.refs_2_), channel_id=1, source_target_pairs={{0,8},{4,28},{8,16},{12,4},{16,24},{20,12},{24,0},{28,20},{1,9},{5... | collective-permute-start | bytes 1966088 | tf_op jit(solution)/shard_map/ppermute | solution.py:386
  62.3 16.1 %collective-permute-start.15 = (bf16[8,320,128]{2,1,0:T(8,128)(2,1)S(1)}, bf16[8,320,128]{2,1,0:T(8,128)(2,1)S(1)}, u32[]{:S(2)}, u32[]{:S(2)}) collective-permute-start(bf16[8,320,128]{2,1,0:T(8,128)(2,1)S(1)} %slice.4.refs_0_.refs_2_), channel_id=1, source_target_pairs={{8,0},{28,4},{16,8},{4,12},{24,16},{12,20},{0,24},{20,28},{9,1},{2... | collective-permute-start | bytes 1966088 | tf_op jit(solution)/shard_map/ppermute | solution.py:389
  70.1 14.6 %collective-permute-start.14 = (bf16[8,320,128]{2,1,0:T(8,128)(2,1)S(1)}, bf16[8,320,128]{2,1,0:T(8,128)(2,1)S(1)}, u32[]{:S(2)}, u32[]{:S(2)}) collective-permute-start(bf16[8,320,128]{2,1,0:T(8,128)(2,1)S(1)} %collective-permute-done.11.refs_0_.refs_4_), channel_id=1, source_target_pairs={{0,4},{4,0},{8,12},{12,8},{16,20},{20,16},{24,28},{28,24},{1,5},{5... | collective-permute-start | bytes 1966088 | tf_op jit(solution)/shard_map/ppermute | solution.py:392
  78.2 12.7 %collective-permute-start.13 = (bf16[8,320,128]{2,1,0:T(8,128)(2,1)S(1)}, bf16[8,320,128]{2,1,0:T(8,128)(2,1)S(1)}, u32[]{:S(2)}, u32[]{:S(2)}) collective-permute-start(bf16[8,320,128]{2,1,0:T(8,128)(2,1)S(1)} %collective-permute-done.11.refs_0_.refs_4_), channel_id=1, source_target_pairs={{0,8},{4,28},{8,16},{12,4},{16,24},{20,12},{24,0},{28,20},{1,9},{5... | collective-permute-start | bytes 1966088 | tf_op jit(solution)/shard_map/ppermute | solution.py:395
  84.6 7.2 %collective-permute-start.17 = (bf16[8,320,128]{2,1,0:T(8,128)(2,1)S(1)}, bf16[8,320,128]{2,1,0:T(8,128)(2,1)S(1)}, u32[]{:S(2)}, u32[]{:S(2)}) collective-permute-start(bf16[8,320,128]{2,1,0:T(8,128)(2,1)S(1)} %collective-permute-done.15.refs_0_.refs_5_), channel_id=1, source_target_pairs={{0,4},{4,0},{8,12},{12,8},{16,20},{20,16},{24,28},{28,24},{1,5},{5... | collective-permute-start | bytes 1966088 | tf_op jit(solution)/shard_map/ppermute | solution.py:398
  90.9 13.0 %collective-permute-start.16 = (bf16[8,320,128]{2,1,0:T(8,128)(2,1)S(1)}, bf16[8,320,128]{2,1,0:T(8,128)(2,1)S(1)}, u32[]{:S(2)}, u32[]{:S(2)}) collective-permute-start(bf16[8,320,128]{2,1,0:T(8,128)(2,1)S(1)} %collective-permute-done.13.refs_1_.refs_8_), channel_id=1, source_target_pairs={{0,4},{4,0},{8,12},{12,8},{16,20},{20,16},{24,28},{28,24},{1,5},{5... | collective-permute-start | bytes 1966088 | tf_op jit(solution)/shard_map/ppermute | solution.py:401
